TPU v7x, 128 devices: a whole 4x4x4 slice. The times are simulated.
128 devices in a mesh: seq: 32 (over y_lo, x, z), head: 4 (over y_hi, core).
Axes of the slice: x: 4, y: 4 (y_hi: 2, y_lo: 2; y = y_hi * 2 + y_lo), z: 4, core: 2. Of those that a mesh axis runs over, the one named last changes fastest.
Arguments:
- tokens: bfloat16 [16384, 4096], P('seq'), may hold values from -15 to 15
- mask_flags: int32 [16384], P('seq'), may hold values 0 or 1
- mask_embed: bfloat16 [4096], replicated, may hold values from -5 to 5
- w_query: bfloat16 [4096, 2048], P(None, 'head'), as said below
- w_key: bfloat16 [4096, 2048], P(None, 'head'), as said below
- w_value: bfloat16 [4096, 2048], P(None, 'head'), may hold values from -0.375 to 0.375
- w_out: bfloat16 [2048, 4096], P('head'), may hold values from -0.125 to 0.125
Outputs:
- mixed_rows: bfloat16 [16384, 4096], P(('seq', 'head'))
Inputs may be any that keep to these rules, and one draw needn't show every extreme that they name: `w_query`: entries of order one over the square root of 4096. `w_key`: entries of order one over the square root of 4096.
All inputs are finite; a program needn't handle non-finite values. No bound on the sum of `mask_flags` on one device may be relied on, other than what follows from the above.
Results may differ from a plain program's by a relative error of at most 0.015.
Values may be sent and summed in bfloat16 or wider, within the bound.
A program may use at most 384 MiB of HBM per device.

v0:
```python
import math

import jax
import jax.numpy as jnp
from jax import lax
from jax.sharding import PartitionSpec as P

DH = 128


def rotate(values, positions, head_size):
    halfway = head_size // 2
    indices = jnp.arange(halfway).astype(jnp.float32)
    frequency = jnp.exp(indices * (-2.0 * math.log(500000.0) / head_size))
    angles = positions[:, None] * frequency[None, :]
    cosine = jnp.cos(angles)[:, None, :]
    sine_table = jnp.sin(angles)[:, None, :]
    shaped = values.reshape(values.shape[0], -1, head_size)
    leading = shaped[..., :halfway]
    trailing = shaped[..., halfway:]
    turned = jnp.concatenate(
        [leading * cosine - trailing * sine_table, trailing * cosine + leading * sine_table],
        axis=-1,
    )
    return turned.reshape(values.shape)


def shards(tokens, mask_flags, mask_embed, w_query, w_key, w_value, w_out):
    tok_rows = tokens.shape[0]
    head_size = DH
    heads_here = w_query.shape[1] // head_size
    mask_rows = mask_flags.astype(jnp.float32)[:, None]
    hidden = (
        tokens.astype(jnp.float32) + mask_rows * mask_embed.astype(jnp.float32)[None, :]
    ).astype(jnp.bfloat16)
    positions = (lax.axis_index("seq") * tok_rows + jnp.arange(tok_rows)).astype(jnp.float32)
    query_rows = rotate(
        jnp.dot(hidden, w_query, preferred_element_type=jnp.float32), positions, head_size
    ).astype(jnp.bfloat16)
    key_rows = rotate(
        jnp.dot(hidden, w_key, preferred_element_type=jnp.float32), positions, head_size
    ).astype(jnp.bfloat16)
    value_rows = jnp.dot(hidden, w_value, preferred_element_type=jnp.float32).astype(jnp.bfloat16)
    queries = query_rows.reshape(tok_rows, heads_here, head_size)
    score_scale = head_size ** (-0.5)
    row_peak = jnp.full((heads_here, tok_rows), -1e30, jnp.float32)
    weighted = jnp.zeros((tok_rows, heads_here, head_size), jnp.float32)
    key_part = lax.all_gather(key_rows, "seq", axis=0, tiled=True).reshape(
        -1, heads_here, head_size
    )
    value_part = lax.all_gather(value_rows, "seq", axis=0, tiled=True).reshape(
        -1, heads_here, head_size
    )
    scores = (
        jnp.einsum("qhd,khd->hqk", queries, key_part, preferred_element_type=jnp.float32)
        * score_scale
    )
    new_peak = jnp.maximum(row_peak, jnp.max(scores, axis=-1))
    factor = jnp.exp(row_peak - new_peak)
    weights = jnp.exp(scores - new_peak[..., None])
    new_total = jnp.sum(weights, axis=-1)
    update = jnp.einsum(
        "hqk,khd->qhd", weights.astype(jnp.bfloat16), value_part, preferred_element_type=jnp.float32
    )
    new_weighted = weighted * factor.T[:, :, None] + update
    attention = (
        (new_weighted / new_total.T[:, :, None])
        .reshape(tok_rows, heads_here * head_size)
        .astype(jnp.bfloat16)
    )
    partials = jnp.dot(attention, w_out, preferred_element_type=jnp.float32)
    mixed_rows = lax.psum_scatter(
        partials.astype(jnp.bfloat16), "head", scatter_dimension=0, tiled=True
    )
    return mixed_rows


def solution(mesh):
    placed = (
        P("seq", None),
        P("seq"),
        P(),
        P(None, "head"),
        P(None, "head"),
        P(None, "head"),
        P("head", None),
    )
    return jax.shard_map(
        shards, mesh=mesh, in_specs=placed, out_specs=P(("seq", "head"), None), check_vma=False
    )
```

profile of v0, /device:TPU:1, one launch (start us, length us, event | category | flops | bytes accessed | tf_op | source)
XLA Modules:
  0.0 553.0 jit_solution(10607201224086478193)
XLA Ops:
  6.5 0.0 all-gather.3.cloned.1.call-start
  6.5 0.7 convert_element_type.50
  7.2 0.7 convert_element_type.49
  7.9 5.9 %fusion.16 = f32[512,512]{0,1:T(8,128)S(1)} fusion(bf16[4096,512]{1,0:T(8,128)(2,1)} %param.10, bf16[512,4096]{1,0:T(8,128)(2,1)} %param.7, f32[4096]{0:T(1024)S(1)} %convert_element_type.50, f32[512]{0:T(512)S(1)} %convert_element_type.49), kind=kOutput, calls=%fused_computation.28 | convolution fusion | flops 2155872256 | bytes 9455616 | tf_op jit(solution)/shard_map/dot_general | solution.py:38
  13.9 0.1 fusion.17
  14.0 0.3 copy.22
  14.3 0.3 copy.23
  14.7 5.9 %fusion.15 = f32[512,512]{0,1:T(8,128)S(1)} fusion(bf16[4096,512]{1,0:T(8,128)(2,1)} %param.11, bf16[512,4096]{1,0:T(8,128)(2,1)} %param.7, f32[4096]{0:T(1024)S(1)} %convert_element_type.50, f32[512]{0:T(512)S(1)} %convert_element_type.49), kind=kOutput, calls=%fused_computation.27 | convolution fusion | flops 2155872256 | bytes 9455616 | tf_op jit(solution)/shard_map/dot_general | solution.py:41
  20.6 1.1 fusion.18
  21.6 1.4 copy.24
  23.0 2.4 copy.25
  25.4 1.0 multiply_cosine_fusion
  26.4 2.7 subtract_convert_fusion.1
  29.1 0.3 pad_maximum_fusion
  29.4 1.0 copy.17
  30.4 0.0 all-gather.3.cloned.1.call-update
  30.5 0.0 copy-start
  30.5 0.0 copy-start.1
  30.5 0.0 all-gather.5.cloned.1.call-start
  30.5 6.7 %convolution_convert_fusion.1 = bf16[512,512]{1,0:T(8,128)(2,1)} fusion(bf16[4096,512]{1,0:T(8,128)(2,1)} %param.12, bf16[512,4096]{1,0:T(8,128)(2,1)} %param.7, f32[4096]{0:T(1024)S(1)} %convert_element_type.50, f32[512]{0:T(512)S(1)} %convert_element_type.49), kind=kOutput, calls=%fused_computation.8 | convolution fusion | flops 2156134400 | bytes 8931328 | tf_op jit(solution)/shard_map/dot_general | solution.py:43
  37.2 0.0 all-gather.5.cloned.1.call-update
  37.2 0.2 reduce-scatter.2.cloned.1.call-start
  37.5 184.3 %all-gather.3.cloned.1.call-done = bf16[16384,512]{0,1:T(8,128)(2,1)} async-done(((bf16[512,512]{0,1:T(8,128)(2,1)}), bf16[16384,512]{0,1:T(8,128)(2,1)}) %all-gather.3.cloned.1.call-update) | async-done | bytes 16777232 | tf_op jit(solution)/shard_map/all_gather | solution.py:48
  221.8 0.0 copy-done
  221.8 52.5 %multiply_reduce_fusion = (f32[4,512]{1,0:T(4,128)S(1)}, f32[4,512,16384]{2,1,0:T(8,128)}) fusion(bf16[16384,4,128]{0,2,1:T(8,128)(2,1)} %bitcast.21, bf16[512,4,64]{2,0,1:T(8,128)(2,1)S(1)} %copy-done.1, bf16[512,4,64]{2,0,1:T(8,128)(2,1)S(1)} %copy-done), kind=kOutput, calls=%fused_computation.1 | convolution fusion | flops 8658089984 | bytes 151527424 | tf_op jit(solution)/shard_map/qhd,khd->hqk/dot_general | solution.py:55
  274.3 41.6 %fusion = f32[4,512]{1,0:T(4,128)S(1)} fusion(f32[4,512,16384]{2,1,0:T(8,128)} %get-tuple-element.20, f32[4,512]{1,0:T(4,128)S(1)} %get-tuple-element.16), kind=kLoop, calls=%fused_computation.2 | loop fusion | flops 100661248 | bytes 134234112 | tf_op jit(solution)/shard_map/reduce_sum | solution.py:61
  316.0 98.7 %all-gather.5.cloned.1.call-done = bf16[16384,512]{1,0:T(8,128)(2,1)} async-done(((bf16[512,512]{1,0:T(8,128)(2,1)}), bf16[16384,512]{1,0:T(8,128)(2,1)}) %all-gather.5.cloned.1.call-update) | async-done | bytes 16777232 | tf_op jit(solution)/shard_map/all_gather | solution.py:51
  414.6 21.3 %copy.21 = bf16[16384,512]{0,1:T(8,128)(2,1)} copy(bf16[16384,512]{1,0:T(8,128)(2,1)} %all-gather.5.cloned.1.call-done) | data formatting | bytes 33554432 | tf_op jit(solution)/shard_map/reshape | solution.py:51
  435.9 48.5 %divide_convert_fusion = bf16[512,4,128]{0,2,1:T(8,128)(2,1)S(1)} fusion(bf16[16384,4,128]{0,2,1:T(8,128)(2,1)} %bitcast.22, f32[4,512,16384]{2,1,0:T(8,128)} %get-tuple-element.20, f32[4,512]{1,0:T(4,128)S(1)} %get-tuple-element.16, f32[512,4]{0,1:T(4,128)S(1)} %bitcast.27, f32[512,4]{0,1:T(4,128)S(1)} %get-tuple-element.15), kind=kOutput, calls=%fused_computation.9 | convolution fusion | flops 8691384320 | bytes 151543808 | tf_op jit(solution)/shard_map/hqk,khd->qhd/dot_general | solution.py:62
  484.4 6.5 %convolution_convert_fusion = bf16[512,4096]{1,0:T(8,128)(2,1)} fusion(bf16[512,512]{0,1:T(8,128)(2,1)S(1)} %bitcast.26, bf16[512,4096]{1,0:T(8,128)(2,1)} %param.13), kind=kOutput, calls=%fused_computation.6 | convolution fusion | flops 2149580800 | bytes 8912896 | tf_op jit(solution)/shard_map/dot_general | solution.py:71
  490.9 0.0 reduce-scatter.2.cloned.1.call-update
  490.9 55.6 %reduce-scatter.2.cloned.1.call-done = bf16[128,4096]{1,0:T(8,128)(2,1)} async-done(((bf16[512,4096]{1,0:T(8,128)(2,1)}), bf16[128,4096]{1,0:T(8,128)(2,1)}) %reduce-scatter.2.cloned.1.call-update) | async-done | bytes 1048592 | tf_op jit(solution)/shard_map/reduce_scatter | solution.py:72
  (4 shorter events, 0.0 us)
Async XLA Ops:
  6.5 215.3 %all-gather.3.cloned.1.call-start = ((), (), s32[]{:S(2)}) async-start(), calls=%async_computation.1 | async-start | bytes 17301504 | tf_op jit(solution)/shard_map/all_gather | solution.py:48
  30.5 191.4 %copy-start = (bf16[512,4,64]{2,0,1:T(8,128)(2,1)S(1)}, bf16[512,4,64]{2,0,1:T(8,128)(2,1)}, u32[]{:S(2)}) copy-start(bf16[512,4,64]{2,0,1:T(8,128)(2,1)} %get-tuple-element.5) | copy-start | bytes 786436
  30.5 191.3 %copy-start.1 = (bf16[512,4,64]{2,0,1:T(8,128)(2,1)S(1)}, bf16[512,4,64]{2,0,1:T(8,128)(2,1)}, u32[]{:S(2)}) copy-start(bf16[512,4,64]{2,0,1:T(8,128)(2,1)} %get-tuple-element.6) | copy-start | bytes 786436
  30.5 384.1 %all-gather.5.cloned.1.call-start = ((), (), s32[]{:S(2)}) async-start(), calls=%async_computation.2 | async-start | bytes 17301504 | tf_op jit(solution)/shard_map/all_gather | solution.py:51
  37.2 509.3 %reduce-scatter.2.cloned.1.call-start = ((), (), s32[]{:S(2)}) async-start(), calls=%async_computation.3 | async-start | bytes 5242880 | tf_op jit(solution)/shard_map/reduce_scatter | solution.py:72
Sparse Core Ops, SparseCore 0:
  30.6 191.1 all-gather.2
  223.4 191.1 all-gather.4
  491.0 55.4 reduce-scatter.1
where the time goes:
time: 554 us; the launch traced here: 553 us
  waiting for transfers between devices  339 us (61%)
  matrix products  126 us (23%)
  other arithmetic  47 us (8%)
  local copies, waits for them, and re-layouts  27.8 us (5%)
  between operations  13.2 us (2%)
    all_gather x1, waiting for transfers between devices, shards(): lax.all_gather(key_rows, 'seq', axis=0, tiled=True)  184 us
    all_gather x1, waiting for transfers between devices, shards(): lax.all_gather(value_rows, 'seq', axis=0, tiled=True)  98.7 us
    reduce_scatter x1, waiting for transfers between devices, shards(): lax.psum_scatter(partials.astype(jnp.bfloat16), 'head', scatter_dimension...  55.6 us
    dot_general x1, matrix products, shards(): jnp.einsum('qhd,khd->hqk', queries, key_part, preferred_element_type=jnp....  52.5 us
    dot_general x1, matrix products, shards(): jnp.einsum('hqk,khd->qhd', weights.astype(jnp.bfloat16), value_part, pref...  48.5 us
    reduce_sum x1, other arithmetic, shards(): new_total = jnp.sum(weights, axis=-1)  41.6 us
    reshape x1, local copies, waits for them, and re-layouts, shards(): lax.all_gather(value_rows, 'seq', axis=0, tiled=True)  21.3 us
  transfers between devices with their start and end apart: 3, of which 3 were waited for; matrix products, arithmetic and copies ran while one was open for 18% of the time, Pallas kernels for 0%

commit v1 on v0

v1 whole, which is shorter than its diff:
```python
import functools
import math

import jax
import jax.numpy as jnp
from jax import lax
from jax.experimental import pallas as pl
from jax.experimental.pallas import tpu as pltpu
from jax.sharding import PartitionSpec as P

DH = 128
MESH = pl.DeviceIdType.MESH
F32 = jnp.float32
BF16 = jnp.bfloat16
VMEM_BYTES = 58 * 2**20
TOTAL_LOW = 2.0**-60
TOTAL_HIGH = 2.0**100

OWN = {(0, d): d + (d + 3) // 4 for d in range(4)}
SIB = {(0, 0): 1, (0, 1): 5, (0, 2): 6, (0, 3): 7}
for _d in range(4):
    OWN[1, _d], OWN[3, _d], SIB[1, _d], SIB[3, _d] = (8 + 4 * _d + n for n in range(4))
    OWN[2, _d] = 24 + 4 * (_d // 2) + _d % 2
    SIB[2, _d] = OWN[2, _d] + 2
OWN_OF = {slot: key for key, slot in OWN.items()}


def place():
    seq, head = lax.axis_index("seq"), lax.axis_index("head")
    y_lo, x, z = seq // 16, (seq // 4) % 4, seq % 4
    y_hi, core = head // 2, head % 2
    return y_lo, x, z, y_hi, core


def seq_of(y_lo, x, z):
    return y_lo * 16 + x * 4 + z


def remote(src, dst, send_sem, recv_sem, seq, head):
    return pltpu.make_async_remote_copy(
        src_ref=src, dst_ref=dst, send_sem=send_sem, recv_sem=recv_sem,
        device_id=(seq, head), device_id_type=MESH,
    )


def lanes(blocks):
    return jnp.concatenate([blocks[n] for n in range(blocks.shape[0])], axis=1)


def turned_blocks(rows):
    return jnp.concatenate(
        [rows[n * DH:(n + 1) * DH].T for n in range(rows.shape[0] // DH)], axis=0
    )


def attend_kernel(
    tok_hbm, flags_ref, embed_ref, cos_ref, sin_ref, wq_hbm, wk_hbm, wv_hbm, wo_hbm,
    o_ref, total_ref, q_out, kv_out, wg_out,
    tok_v, w_v, pacc, stq, stkv, qb, kvb, acc,
    load_sem, q_send, q_recv, a_send, kv_recv, f_send, dump_sem,
    wx_send, wx_recv, wz_send, wz_recv, ws_send, ws_recv,
):
    y_lo, x, z, y_hi, core = place()
    seq, head = seq_of(y_lo, x, z), y_hi * 2 + core
    sib = y_hi * 2 + (1 - core)
    straight = core == y_lo
    x_up, x_down = seq_of(y_lo, (x + 1) % 4, z), seq_of(y_lo, (x + 3) % 4, z)
    z_up, z_down = seq_of(y_lo, x, (z + 1) % 4), seq_of(y_lo, x, (z + 3) % 4)
    cross_seq, cross_head = seq_of(1 - y_lo, x, z), (1 - y_hi) * 2 + core

    pltpu.make_async_copy(tok_hbm, tok_v, load_sem.at[6]).start()
    far = 1 - z // 2
    near = z // 2
    order = [(wq_hbm, far), (wq_hbm, near), (wk_hbm, far), (wv_hbm, far), (wk_hbm, near), (wv_hbm, near)]

    def w_load(n):
        w, pair = order[n]
        cols = pl.ds(pl.multiple_of(pair * 256, 256), 256)
        return pltpu.make_async_copy(w.at[:, cols], w_v.at[n], load_sem.at[n])

    for n in range(6):
        w_load(n).start()

    barrier = pltpu.get_barrier_semaphore()

    def greet(s, h):
        pl.semaphore_signal(barrier, inc=1, device_id=(s, h), device_id_type=MESH)

    for i in range(4):
        @pl.when(jnp.logical_not(jnp.logical_and(straight, z == i)))
        def _():
            greet(seq_of(core, x, i), y_hi * 2 + y_lo)
    for s, h in ((x_up, head), (x_down, head), (z_up, head), (z_down, head), (seq, sib), (cross_seq, cross_head)):
        greet(s, h)

    @pl.when(straight)
    def _():
        pl.semaphore_wait(barrier, 9)

    @pl.when(jnp.logical_not(straight))
    def _():
        pl.semaphore_wait(barrier, 10)

    mine, theirs = (z % 2) * 256, (1 - z % 2) * 256

    def w_rows(base, k):
        return pl.ds(pl.multiple_of(base + 64 * k, 64), 64)

    def w_cross(k):
        return remote(wo_hbm.at[w_rows(mine, k)], wg_out.at[1, w_rows(mine, k)],
                      wx_send.at[k], wx_recv.at[k], cross_seq, cross_head)

    def w_side(k):
        to = z_up if k < 2 else z_down
        return remote(wg_out.at[1, w_rows(mine, k)], wg_out.at[1, w_rows(mine, k)],
                      wz_send.at[k], wz_recv.at[k], to, head)

    def w_side_in(k):
        return remote(wg_out.at[1, w_rows(theirs, k)], wg_out.at[1, w_rows(theirs, k)],
                      wz_send.at[k], wz_recv.at[k], z_up, head)

    def w_sib(n):
        if n == 8:
            return remote(wo_hbm, wg_out.at[0], ws_send.at[8], ws_recv.at[8], seq, sib)
        rows = w_rows(mine if n < 4 else theirs, n % 4)
        return remote(wg_out.at[1, rows], wg_out.at[2, rows], ws_send.at[n], ws_recv.at[n], seq, sib)

    def w_cross_in(k):
        w_cross(k).wait_recv()
        w_side(k).start()
        w_sib(k).start()

    for k in range(4):
        w_cross(k).start()

    pltpu.make_async_copy(tok_hbm, tok_v, load_sem.at[6]).wait()
    flag_cols = jnp.broadcast_to(flags_ref[...].astype(F32), (DH, flags_ref.shape[1])).T

    def add_embed(n, _):
        cols = pl.ds(pl.multiple_of(n * DH, DH), DH)
        added = embed_ref[:, cols].astype(F32)
        tok_v[:, cols] = (tok_v[:, cols].astype(F32) + flag_cols * added).astype(BF16)
        return 0

    lax.fori_loop(0, tok_v.shape[1] // DH, add_embed, 0)

    def rope(rows):
        return rows * cos_ref[...] + pltpu.roll(rows, DH // 2, 1) * sin_ref[...]

    def piece(n, e):
        return order_pair(n) * 2 + e

    def order_pair(n):
        return order[n][1]

    def a2a_q(m, pair, e):
        i = pair * 2 + e
        args = (stq.at[m], qb.at[z], q_send.at[m], q_recv.at[z])
        return remote(*args, seq_of(core, x, i), y_hi * 2 + y_lo), pltpu.make_async_copy(
            stq.at[m], qb.at[z], q_recv.at[z]), jnp.logical_and(straight, z == i)

    def a2a_kv(m, pair, e):
        i = pair * 2 + e
        d = (z - i + 4) % 4
        slot = d + (d + 3) // 4
        return remote(stkv.at[m], kvb.at[slot], a_send.at[m], kv_recv.at[slot],
                      seq_of(core, x, i), y_hi * 2 + y_lo), pltpu.make_async_copy(
            stkv.at[m], kvb.at[slot], kv_recv.at[slot]), jnp.logical_and(straight, z == i)

    def launch(copies):
        far_copy, own_copy, own = copies

        @pl.when(own)
        def _():
            own_copy.start()

        @pl.when(jnp.logical_not(own))
        def _():
            far_copy.start()

    def drain(copies):
        far_copy, _, own = copies

        @pl.when(jnp.logical_not(own))
        def _():
            far_copy.wait_send()

    score_scale = DH ** -0.5 * math.log2(math.e)
    for n in range(6):
        w_load(n).wait()
        pacc[...] = jnp.zeros_like(pacc)

        def multiply(k, _, n=n):
            depth = pl.ds(pl.multiple_of(k * 512, 512), 512)
            pacc[...] += jnp.dot(tok_v[:, depth], w_v[n, depth, :], preferred_element_type=F32)
            return 0

        lax.fori_loop(0, tok_v.shape[1] // 512, multiply, 0)
        pair = order[n][1]
        for e in range(2):
            rows = pacc[:, e * DH:(e + 1) * DH]
            if n < 2:
                m = n * 2 + e
                stq[m] = turned_blocks((rope(rows) * score_scale).astype(BF16))
                launch(a2a_q(m, pair, e))
            else:
                m = (n - 2) // 2 * 2 + e
                if n % 2 == 0:
                    stkv[m, 0] = rope(rows).astype(BF16)
                else:
                    stkv[m, 1] = turned_blocks(rows.astype(BF16))
                    launch(a2a_kv(m, pair, e))

    acc[...] = jnp.zeros_like(acc)
    total_ref[...] = jnp.zeros_like(total_ref)
    for j in range(4):
        remote(qb.at[j], qb.at[j], q_send.at[0], q_recv.at[j], seq, sib).wait_recv()
    q_dump = pltpu.make_async_copy(qb, q_out, dump_sem.at[16])
    q_dump.start()

    sends = []

    def forward(slot, to_slot, s, h):
        def copy():
            return remote(kvb.at[slot], kvb.at[to_slot], f_send.at[n_send], kv_recv.at[to_slot], s, h)
        n_send = len(sends)
        sends.append(copy)
        copy().start()

    def arrived(slot):
        remote(kvb.at[slot], kvb.at[slot], f_send.at[0], kv_recv.at[slot], seq, sib).wait_recv()
        if slot not in OWN_OF:
            return
        dx, d = OWN_OF[slot]
        if dx == 0:
            forward(slot, OWN[1, d], x_up, head)
            forward(slot, OWN[3, d], x_down, head)
        if dx == 1 and d % 2 == 0:
            forward(slot, OWN[2, d], x_up, head)
        if dx == 3 and d % 2 == 1:
            forward(slot, OWN[2, d], x_down, head)
        forward(slot, SIB[dx, d], seq, sib)

    extra = {
        2: lambda: w_cross_in(0),
        4: lambda: w_sib(8).start(),
        5: lambda: (w_side_in(0).wait_recv(), w_sib(4).start()),
        7: lambda: w_cross_in(1),
        10: lambda: (w_side_in(1).wait_recv(), w_sib(5).start()),
        12: lambda: w_cross_in(2),
        15: lambda: (w_side_in(2).wait_recv(), w_sib(6).start()),
    }
    blocks = qb.shape[0]

    def step(t, _):
        for k in range(16):
            @pl.when(t == k)
            def _(k=k):
                arrived(2 * k)
                arrived(2 * k + 1)
                if k in extra:
                    extra[k]()

        pltpu.make_async_copy(kvb.at[pl.ds(2 * t, 2)], kv_out.at[pl.ds(2 * t, 2)], dump_sem.at[t]).start()
        keys = kvb[pl.ds(2 * t, 2), 0].reshape(1024, DH)
        values = lanes(kvb[pl.ds(2 * t, 2), 1].reshape(8, DH, DH))

        def scores(i):
            return jnp.dot(keys, lanes(qb[i].reshape(4, DH, DH)), preferred_element_type=F32)

        now = scores(0)
        for i in range(blocks):
            later = scores(i + 1) if i + 1 < blocks else None
            cols = slice(i * 512, (i + 1) * 512)
            weights = jnp.exp2(now)
            total_ref[:, cols] += jnp.sum(weights.reshape(128, 8, 512), axis=0)
            acc[:, cols] += jnp.dot(values, weights.astype(BF16), preferred_element_type=F32)
            now = later
        return 0

    lax.fori_loop(0, 16, step, 0)

    w_cross_in(3)
    for i in range(blocks):
        cols = slice(i * 512, (i + 1) * 512)
        total = jnp.sum(total_ref[:, cols], axis=0, keepdims=True)
        done = (acc[:, cols] / total).astype(BF16)
        for n in range(4):
            o_ref[i * 512 + n * DH:i * 512 + (n + 1) * DH, :] = done[:, n * DH:(n + 1) * DH].T
    w_side_in(3).wait_recv()
    w_sib(7).start()

    for n in range(9):
        w_sib(n).wait_recv()
        w_sib(n).wait_send()
    for k in range(4):
        w_cross(k).wait_send()
        w_side(k).wait_send()
    for n in range(2):
        for e in range(2):
            drain(a2a_q(n * 2 + e, order[n][1], e))
            drain(a2a_kv(n * 2 + e, order[2 + 2 * n][1], e))
    for copy in sends:
        copy().wait_send()
    q_dump.wait()

    def dumped(t, _):
        pltpu.make_async_copy(kvb.at[pl.ds(2 * t, 2)], kv_out.at[pl.ds(2 * t, 2)], dump_sem.at[t]).wait()
        return 0

    lax.fori_loop(0, 16, dumped, 0)


def repair_kernel(total_ref, q_hbm, kv_hbm, o_in, o_hbm, qb, kv, acc, peak, total, o_v, sem):
    sums = jnp.sum(total_ref[...], axis=0, keepdims=True)
    good = jnp.logical_and(sums > TOTAL_LOW, sums < TOTAL_HIGH)
    bad = jnp.max(jnp.where(good, 0.0, 1.0))

    @pl.when(bad > 0.5)
    def _():
        load = pltpu.make_async_copy(q_hbm, qb, sem)
        load.start()
        load.wait()
        acc[...] = jnp.zeros_like(acc)
        total[...] = jnp.zeros_like(total)
        peak[...] = jnp.full_like(peak, -3e38)

        def chunk(n, _):
            load = pltpu.make_async_copy(kv_hbm.at[n], kv, sem)
            load.start()
            load.wait()

            def block(i, _):
                cols = pl.ds(pl.multiple_of(i * 512, 512), 512)
                scores = jnp.dot(kv[0], lanes(qb[i].reshape(4, DH, DH)), preferred_element_type=F32)
                old = peak[0:1, cols]
                new = jnp.maximum(old, jnp.max(scores, axis=0, keepdims=True))
                factor = jnp.exp2(old - new)
                weights = jnp.exp2(scores - new)
                peak[0:1, cols] = new
                total[0:1, cols] = total[0:1, cols] * factor + jnp.sum(weights, axis=0, keepdims=True)
                acc[:, cols] = acc[:, cols] * factor + jnp.dot(
                    lanes(kv[1].reshape(4, DH, DH)), weights.astype(BF16), preferred_element_type=F32
                )
                return 0

            lax.fori_loop(0, 4, block, 0)
            return 0

        lax.fori_loop(0, kv_hbm.shape[0], chunk, 0)
        for n in range(16):
            cols = slice(n * DH, (n + 1) * DH)
            o_v[cols, :] = (acc[:, cols] / total[0:1, cols]).astype(BF16).T
        store = pltpu.make_async_copy(o_v, o_hbm, sem)
        store.start()
        store.wait()


def out_kernel(o_ref, wo_hbm, wg_hbm, out_ref, full, w_v, load_sem, send_sem, recv_sem):
    y_lo, x, z, y_hi, core = place()
    straight = core == y_lo
    groups = [(wo_hbm, y_hi * 2 + core), (wg_hbm.at[0], y_hi * 2 + 1 - core),
              (wg_hbm.at[1], (1 - y_hi) * 2 + core), (wg_hbm.at[2], (1 - y_hi) * 2 + 1 - core)]
    loads = [pltpu.make_async_copy(src, w_v.at[g], load_sem.at[n]) for n, (src, g) in enumerate(groups)]
    for load in loads:
        load.start()

    barrier = pltpu.get_barrier_semaphore()
    for hi in range(2):
        for lo in range(2):
            for zz in range(4):
                same = (straight, y_hi == hi, y_lo == lo, z == zz)

                @pl.when(jnp.logical_not(functools.reduce(jnp.logical_and, same)))
                def _(hi=hi, lo=lo, zz=zz):
                    pl.semaphore_signal(barrier, inc=1, device_id=(seq_of(lo, x, zz), hi * 2 + y_lo), device_id_type=MESH)

    @pl.when(straight)
    def _():
        pl.semaphore_wait(barrier, 15)

    @pl.when(jnp.logical_not(straight))
    def _():
        pl.semaphore_wait(barrier, 16)

    mine = y_hi * 8 + y_lo * 4 + z
    copies = []
    for dz in range(4):
        for hi in range(2):
            for c in range(2):
                zz = (z + dz) % 4
                n = (dz * 2 + hi) * 2 + c
                own = functools.reduce(jnp.logical_and, (straight, y_hi == hi, core == c, dz == 0)) if dz == 0 else None
                rows = pl.ds(pl.multiple_of(zz * 512 + hi * 256 + c * 128, 128), 128)
                far = remote(o_ref.at[rows], full.at[mine], send_sem.at[n], recv_sem.at[mine],
                             seq_of(core, x, zz), hi * 2 + c)
                near = pltpu.make_async_copy(o_ref.at[rows], full.at[mine], recv_sem.at[mine])
                copies.append((far, near, own))
    for far, near, own in copies:
        if own is None:
            far.start()
        else:
            pl.when(own)(near.start)
            pl.when(jnp.logical_not(own))(far.start)
    for load in loads:
        load.wait()
    for n in range(16):
        remote(full.at[n], full.at[n], send_sem.at[0], recv_sem.at[n], seq_of(y_lo, x, z), y_hi * 2 + 1 - core).wait_recv()
    attention = [lanes(full[4 * g:4 * g + 4]) for g in range(4)]

    def columns(n, _):
        cols = pl.ds(pl.multiple_of(n * 512, 512), 512)
        total = jnp.dot(attention[0], w_v[0, :, cols], preferred_element_type=F32)
        for g in range(1, 4):
            total += jnp.dot(attention[g], w_v[g, :, cols], preferred_element_type=F32)
        out_ref[:, cols] = total.astype(BF16)
        return 0

    lax.fori_loop(0, out_ref.shape[1] // 512, columns, 0)
    for far, near, own in copies:
        if own is None:
            far.wait_send()
        else:
            pl.when(jnp.logical_not(own))(far.wait_send)


def rope_tables(rows):
    halfway = DH // 2
    frequency = jnp.exp(jnp.arange(halfway).astype(F32) * (-2.0 * math.log(500000.0) / DH))
    positions = (lax.axis_index("seq") * rows + jnp.arange(rows)).astype(F32)
    angles = positions[:, None] * frequency[None, :]
    cosine, sine = jnp.cos(angles), jnp.sin(angles)
    return jnp.concatenate([cosine, cosine], axis=1), jnp.concatenate([-sine, sine], axis=1)


def shards(tokens, mask_flags, mask_embed, w_query, w_key, w_value, w_out):
    rows, width = tokens.shape
    cosine, sine = rope_tables(rows)
    vmem, hbm = pl.BlockSpec(memory_space=pltpu.VMEM), pl.BlockSpec(memory_space=pl.ANY)
    dma = pltpu.SemaphoreType.DMA
    struct = jax.ShapeDtypeStruct
    attention, total, q_all, kv_all, w_all = pl.pallas_call(
        attend_kernel,
        out_shape=(
            struct((4 * rows, DH), BF16), struct((8, 4 * rows), F32), struct((4, rows, DH), BF16),
            struct((32, 2, rows, DH), BF16), struct((3,) + w_out.shape, BF16),
        ),
        in_specs=[hbm, vmem, vmem, vmem, vmem, hbm, hbm, hbm, hbm],
        out_specs=(vmem, vmem, hbm, hbm, hbm),
        scratch_shapes=[
            pltpu.VMEM((rows, width), BF16),
            pltpu.VMEM((6, width, 256), BF16),
            pltpu.VMEM((rows, 256), F32),
            pltpu.VMEM((4, rows, DH), BF16),
            pltpu.VMEM((4, 2, rows, DH), BF16),
            pltpu.VMEM((4, rows, DH), BF16),
            pltpu.VMEM((32, 2, rows, DH), BF16),
            pltpu.VMEM((DH, 4 * rows), F32),
            dma((7,)), dma((4,)), dma((4,)), dma((4,)), dma((32,)), dma((28,)), dma((17,)),
            dma((4,)), dma((4,)), dma((4,)), dma((4,)), dma((9,)), dma((9,)),
        ],
        compiler_params=pltpu.CompilerParams(
            collective_id=0, has_side_effects=True, vmem_limit_bytes=VMEM_BYTES
        ),
        name="attend",
    )(tokens, mask_flags.reshape(1, rows), mask_embed.reshape(1, width), cosine, sine, w_query, w_key, w_value, w_out)
    attention = pl.pallas_call(
        repair_kernel,
        out_shape=struct((4 * rows, DH), BF16),
        in_specs=[vmem, hbm, hbm, hbm],
        out_specs=hbm,
        scratch_shapes=[
            pltpu.VMEM((4, rows, DH), BF16),
            pltpu.VMEM((2, rows, DH), BF16),
            pltpu.VMEM((DH, 4 * rows), F32),
            pltpu.VMEM((8, 4 * rows), F32),
            pltpu.VMEM((8, 4 * rows), F32),
            pltpu.VMEM((4 * rows, DH), BF16),
            dma,
        ],
        input_output_aliases={3: 0},
        compiler_params=pltpu.CompilerParams(vmem_limit_bytes=VMEM_BYTES),
        name="repair",
    )(total, q_all, kv_all, attention)
    return pl.pallas_call(
        out_kernel,
        out_shape=struct((rows // 4, width), BF16),
        in_specs=[vmem, hbm, hbm],
        out_specs=vmem,
        scratch_shapes=[
            pltpu.VMEM((16, DH, DH), BF16),
            pltpu.VMEM((4,) + w_out.shape, BF16),
            dma((4,)), dma((16,)), dma((16,)),
        ],
        compiler_params=pltpu.CompilerParams(
            collective_id=1, has_side_effects=True, vmem_limit_bytes=VMEM_BYTES
        ),
        name="project_out",
    )(attention, w_out, w_all)


def solution(mesh):
    placed = (
        P("seq", None),
        P("seq"),
        P(),
        P(None, "head"),
        P(None, "head"),
        P(None, "head"),
        P("head", None),
    )
    return jax.shard_map(
        shards, mesh=mesh, in_specs=placed, out_specs=P(("seq", "head"), None), check_vma=False
    )
```

time: 554 us -> 247 us (0.45)
  waiting for transfers between devices: 339 us -> 0 us
  Pallas kernels: 0 us -> 240 us
  matrix products: 126 us -> 0 us
  other arithmetic: 47 us -> 2 us
  local copies, waits for them, and re-layouts: 27.8 us -> 3.6 us
  between operations: 13.2 us -> 0.03 us
    all_gather x2 -> x0, waiting for transfers between devices: 283 us -> none  [the longest x1 184 us: shards(): lax.all_gather(key_rows, 'seq', axis=0, tiled=True)]
    pallas_call x0 -> x3, Pallas kernels: none -> 240 us  [the longest x1 113 us: shards(): pl.pallas_call(repair_kernel, out_shape=struct((4 * rows, DH), BF16), in_...]
    dot_general x6 -> x0, matrix products: 126 us -> none  [the longest x1 52.5 us: shards(): jnp.einsum('qhd,khd->hqk', queries, key_part, preferred_element_type=jnp....]
    reduce_scatter x1 -> x0, waiting for transfers between devices: 55.6 us -> none  [shards(): lax.psum_scatter(partials.astype(jnp.bfloat16), 'head', scatter_dimension...]
    reduce_sum x1 -> x0, other arithmetic: 41.6 us -> none  [shards(): new_total = jnp.sum(weights, axis=-1)]
    reshape x1, local copies, waits for them, and re-layouts: 21.3 us -> 1.31 us  [shards(): mask_embed.reshape(1, width)]
  transfers between devices with their start and end apart: 3 -> 0, of which waited for: 3 -> 0; matrix products, arithmetic and copies ran while one was open for 18% -> 0% of each run, Pallas kernels for 0% -> 0%
where the time goes in v1:
time: 247 us; the launch traced here: 246 us
  Pallas kernels  240 us (97%)
  local copies, waits for them, and re-layouts  3.6 us (1%)
    pallas_call x1, Pallas kernels, shards(): pl.pallas_call(repair_kernel, out_shape=struct((4 * rows, DH), BF16), in_...  113 us
    pallas_call x1, Pallas kernels, shards(): pl.pallas_call(attend_kernel, out_shape=(struct((4 * rows, DH), BF16), st...  106 us
    pallas_call x1, Pallas kernels, shards(): pl.pallas_call(out_kernel, out_shape=struct((rows // 4, width), BF16), in...  21.1 us

profile of v1, /device:TPU:1, one launch (start us, length us, event | category | flops | bytes accessed | tf_op | source)
XLA Modules:
  0.0 245.9 jit_solution(4652535666363211649)
XLA Ops:
  0.0 1.3 reshape.18.embed_ref
  1.3 1.0 fusion
  2.3 1.0 pad_maximum_fusion
  3.3 105.8 %attend.1 = (bf16[2048,128]{1,0:T(8,128)(2,1)}, f32[8,2048]{1,0:T(8,128)}, bf16[4,512,128]{2,1,0:T(8,128)(2,1)}, bf16[32,2,512,128]{3,2,1,0:T(8,128)(2,1)}, bf16[3,512,4096]{2,1,0:T(8,128)(2,1)}) custom-call(bf16[512,4096]{1,0:T(8,128)(2,1)} %tok_hbm.1, s32[1,512]{1,0:T(1,128)} %bitcast.1, bf16[1,4096]{1,0:T(2,128)(2,1)} %reshape.18.embed_ref, ...), custom_call_target="tpu_custom_call" | custom-call | tf_op jit(solution)/shard_map/attend/pallas_call | solution.py:442
  109.1 113.3 %repair.1.o_ref = bf16[2048,128]{1,0:T(8,128)(2,1)} custom-call(f32[8,2048]{1,0:T(8,128)} %get-tuple-element.10.total_ref, bf16[4,512,128]{2,1,0:T(8,128)(2,1)} %get-tuple-element.11.q_hbm, bf16[32,2,512,128]{3,2,1,0:T(8,128)(2,1)} %get-tuple-element.12.kv_hbm, bf16[2048,128]{1,0:T(8,128)(2,1)} %get-tuple-element.13.o_in), custom_call_target="tpu_custom_call", output_to_operand_aliasing={{}: (3, {})} | custom-call | tf_op jit(solution)/shard_map/repair/pallas_call | solution.py:467
  222.5 21.1 %project_out.1 = bf16[128,4096]{1,0:T(8,128)(2,1)} custom-call(bf16[2048,128]{1,0:T(8,128)(2,1)} %repair.1.o_ref, bf16[512,4096]{1,0:T(8,128)(2,1)} %wo_hbm.3, bf16[3,512,4096]{2,1,0:T(8,128)(2,1)} %get-tuple-element.14.wg_hbm), custom_call_target="tpu_custom_call" | custom-call | tf_op jit(solution)/shard_map/project_out/pallas_call | solution.py:485
  243.6 2.3 copy.11
  (2 shorter events, 0.0 us)

commit v2 on v1

--- a/solution.py
+++ b/solution.py
@@ -16,13 +16,25 @@
 TOTAL_LOW = 2.0**-60
 TOTAL_HIGH = 2.0**100
 
-OWN = {(0, d): d + (d + 3) // 4 for d in range(4)}
-SIB = {(0, 0): 1, (0, 1): 5, (0, 2): 6, (0, 3): 7}
-for _d in range(4):
-    OWN[1, _d], OWN[3, _d], SIB[1, _d], SIB[3, _d] = (8 + 4 * _d + n for n in range(4))
-    OWN[2, _d] = 24 + 4 * (_d // 2) + _d % 2
-    SIB[2, _d] = OWN[2, _d] + 2
+USE = (
+    ("own", 0, 0), ("sib", 0, 0), ("own", 1, 0), ("own", 3, 0), ("sib", 1, 0), ("sib", 3, 0),
+    ("own", 0, 1), ("sib", 0, 1), ("own", 0, 3), ("own", 0, 2), ("sib", 0, 3), ("sib", 0, 2),
+    ("own", 1, 1), ("own", 3, 1), ("sib", 1, 1), ("sib", 3, 1), ("own", 1, 3), ("own", 3, 3), ("sib", 1, 3), ("sib", 3, 3),
+    ("own", 2, 0), ("own", 2, 1), ("sib", 2, 0), ("sib", 2, 1), ("own", 1, 2), ("own", 3, 2), ("sib", 1, 2), ("sib", 3, 2),
+    ("own", 2, 3), ("own", 2, 2), ("sib", 2, 3), ("sib", 2, 2),
+)
+OWN = {(dx, e): n for n, (by, dx, e) in enumerate(USE) if by == "own"}
+SIB = {(dx, e): n for n, (by, dx, e) in enumerate(USE) if by == "sib"}
+EARLY = {1: ((0, 1),), 3: ((0, 3),)}
 OWN_OF = {slot: key for key, slot in OWN.items()}
+
+ORDER = (("kv", 0), ("q", 0), ("q", 1), ("kv", 1), ("kv", 3), ("kv", 2))
+CROSS = (0, 1, 2, 3, 6, 7)
+EXTRA = {
+    0: (("own", 0),), 4: (("in", 0), ("in", 1)), 5: (("in", 2),), 6: (("in", 3),), 8: (("in", 4),), 9: (("in", 6),),
+    10: (("in", 5), ("side", 0), ("side", 1)), 11: (("side", 2),), 12: (("in", 7), ("side", 3)), 13: (("side", 4),),
+    14: (("side", 5),), 15: (("side", 6),), 16: (("side", 7),),
+}
 
 
 def place():
@@ -54,32 +66,35 @@
 
 
 def attend_kernel(
-    tok_hbm, flags_ref, embed_ref, cos_ref, sin_ref, wq_hbm, wk_hbm, wv_hbm, wo_hbm,
+    tok_hbm, flags_ref, embed_ref, wq_hbm, wk_hbm, wv_hbm, wo_hbm,
     o_ref, total_ref, q_out, kv_out, wg_out,
-    tok_v, w_v, pacc, stq, stkv, qb, kvb, acc,
+    tok_v, w_v, pacc, cos_v, sin_v, stq, stkv, qb, kvb, acc,
     load_sem, q_send, q_recv, a_send, kv_recv, f_send, dump_sem,
-    wx_send, wx_recv, wz_send, wz_recv, ws_send, ws_recv,
+    wx_send, wy_send, wx_recv, wz_send, wz_recv, ws_send, ws_recv,
 ):
     y_lo, x, z, y_hi, core = place()
     seq, head = seq_of(y_lo, x, z), y_hi * 2 + core
     sib = y_hi * 2 + (1 - core)
     straight = core == y_lo
+    rows_here = tok_hbm.shape[0]
     x_up, x_down = seq_of(y_lo, (x + 1) % 4, z), seq_of(y_lo, (x + 3) % 4, z)
     z_up, z_down = seq_of(y_lo, x, (z + 1) % 4), seq_of(y_lo, x, (z + 3) % 4)
-    cross_seq, cross_head = seq_of(1 - y_lo, x, z), (1 - y_hi) * 2 + core
-
-    pltpu.make_async_copy(tok_hbm, tok_v, load_sem.at[6]).start()
-    far = 1 - z // 2
-    near = z // 2
-    order = [(wq_hbm, far), (wq_hbm, near), (wk_hbm, far), (wv_hbm, far), (wk_hbm, near), (wv_hbm, near)]
-
-    def w_load(n):
-        w, pair = order[n]
-        cols = pl.ds(pl.multiple_of(pair * 256, 256), 256)
-        return pltpu.make_async_copy(w.at[:, cols], w_v.at[n], load_sem.at[n])
-
-    for n in range(6):
-        w_load(n).start()
+    y_seq = seq_of(1 - y_lo, x, z)
+    cross_head = (1 - y_hi) * 2 + core
+
+    def swapped(e):
+        return 2 * ((z // 2 + e // 2) % 2) + (z % 2 + e % 2) % 2
+
+    tok_load = pltpu.make_async_copy(tok_hbm, tok_v.at[pl.ds(0, rows_here)], load_sem.at[6])
+    tok_load.start()
+    for n, (kind, which) in enumerate(ORDER):
+        if kind == "q":
+            cols = pl.ds(pl.multiple_of(swapped(2 * which) // 2 * 256, 256), 256)
+            pltpu.make_async_copy(wq_hbm.at[:, cols], w_v.at[n], load_sem.at[n]).start()
+        else:
+            cols = pl.ds(pl.multiple_of(swapped(which) * DH, DH), DH)
+            pltpu.make_async_copy(wk_hbm.at[:, cols], w_v.at[n, :, pl.ds(0, DH)], load_sem.at[n]).start()
+            pltpu.make_async_copy(wv_hbm.at[:, cols], w_v.at[n, :, pl.ds(DH, DH)], load_sem.at[n]).start()
 
     barrier = pltpu.get_barrier_semaphore()
 
@@ -90,134 +105,138 @@
         @pl.when(jnp.logical_not(jnp.logical_and(straight, z == i)))
         def _():
             greet(seq_of(core, x, i), y_hi * 2 + y_lo)
-    for s, h in ((x_up, head), (x_down, head), (z_up, head), (z_down, head), (seq, sib), (cross_seq, cross_head)):
+    for s, h in ((x_up, head), (x_down, head), (z_up, head), (z_down, head),
+                 (seq, sib), (y_seq, head), (y_seq, cross_head)):
         greet(s, h)
+
+    lane = lax.broadcasted_iota(jnp.int32, (1, DH), 1)
+    frequency = jnp.exp((lane % (DH // 2)).astype(F32) * (-2.0 * math.log(500000.0) / DH))
+    sign = jnp.where(lane < DH // 2, -1.0, 1.0)
+
+    def angle_rows(n, _):
+        rows = pl.ds(pl.multiple_of(n * 64, 64), 64)
+        position = (lax.broadcasted_iota(jnp.int32, (64, DH), 0) + (seq * rows_here + n * 64)).astype(F32)
+        angle = position * frequency
+        cos_v[rows, :] = jnp.cos(angle)
+        sin_v[rows, :] = jnp.sin(angle) * sign
+        return 0
+
+    lax.fori_loop(0, rows_here // 64, angle_rows, 0)
 
     @pl.when(straight)
     def _():
-        pl.semaphore_wait(barrier, 9)
+        pl.semaphore_wait(barrier, 10)
 
     @pl.when(jnp.logical_not(straight))
     def _():
-        pl.semaphore_wait(barrier, 10)
-
-    mine, theirs = (z % 2) * 256, (1 - z % 2) * 256
-
-    def w_rows(base, k):
-        return pl.ds(pl.multiple_of(base + 64 * k, 64), 64)
-
-    def w_cross(k):
-        return remote(wo_hbm.at[w_rows(mine, k)], wg_out.at[1, w_rows(mine, k)],
-                      wx_send.at[k], wx_recv.at[k], cross_seq, cross_head)
-
-    def w_side(k):
-        to = z_up if k < 2 else z_down
-        return remote(wg_out.at[1, w_rows(mine, k)], wg_out.at[1, w_rows(mine, k)],
-                      wz_send.at[k], wz_recv.at[k], to, head)
-
-    def w_side_in(k):
-        return remote(wg_out.at[1, w_rows(theirs, k)], wg_out.at[1, w_rows(theirs, k)],
-                      wz_send.at[k], wz_recv.at[k], z_up, head)
+        pl.semaphore_wait(barrier, 11)
+
+    def w_chunk(colour_y, colour_z, q):
+        base = (colour_y * 2 + colour_z) * 128 + 32 * (q % 4)
+        return pl.ds(pl.multiple_of(base, 32), 32)
+
+    def w_rows(q, y=None, z_par=None):
+        y = y_lo if y is None else y
+        z_par = z % 2 if z_par is None else z_par
+        return w_chunk(y if q < 4 else 1 - y, z_par, q)
+
+    def w_cross(n):
+        rows = w_rows(CROSS[n], y=1 - y_lo)
+        return remote(wo_hbm.at[rows], wg_out.at[1, rows], wx_send.at[n], wx_recv.at[CROSS[n]], y_seq, cross_head)
+
+    def w_y(q):
+        rows = w_rows(q)
+        return remote(wg_out.at[1, rows], wg_out.at[1, rows], wy_send.at[q], wx_recv.at[q + 4], y_seq, head)
+
+    def w_z(q, rows=None):
+        rows = w_rows(q) if rows is None else rows
+        return remote(wg_out.at[1, rows], wg_out.at[1, rows], wz_send.at[q], wz_recv.at[q],
+                      z_up if q % 2 == 0 else z_down, head)
 
     def w_sib(n):
-        if n == 8:
-            return remote(wo_hbm, wg_out.at[0], ws_send.at[8], ws_recv.at[8], seq, sib)
-        rows = w_rows(mine if n < 4 else theirs, n % 4)
+        if n == 16:
+            return remote(wo_hbm, wg_out.at[0], ws_send.at[16], ws_recv.at[16], seq, sib)
+        rows = w_rows(n) if n < 8 else w_rows(n - 8, z_par=1 - z % 2)
         return remote(wg_out.at[1, rows], wg_out.at[2, rows], ws_send.at[n], ws_recv.at[n], seq, sib)
 
-    def w_cross_in(k):
-        w_cross(k).wait_recv()
-        w_side(k).start()
-        w_sib(k).start()
-
-    for k in range(4):
-        w_cross(k).start()
-
-    pltpu.make_async_copy(tok_hbm, tok_v, load_sem.at[6]).wait()
-    flag_cols = jnp.broadcast_to(flags_ref[...].astype(F32), (DH, flags_ref.shape[1])).T
-
-    def add_embed(n, _):
-        cols = pl.ds(pl.multiple_of(n * DH, DH), DH)
-        added = embed_ref[:, cols].astype(F32)
-        tok_v[:, cols] = (tok_v[:, cols].astype(F32) + flag_cols * added).astype(BF16)
+    def w_arrived(q):
+        rows = w_rows(q)
+        remote(wg_out.at[1, rows], wg_out.at[1, rows], wx_send.at[0], wx_recv.at[q], y_seq, head).wait_recv()
+        if q < 2:
+            w_y(q).start()
+        w_z(q).start()
+        w_sib(q).start()
+
+    def w_side(q):
+        w_z(q, w_rows(q, z_par=1 - z % 2)).wait_recv()
+        w_sib(8 + q).start()
+
+    for n in range(len(CROSS)):
+        w_cross(n).start()
+
+    flag_cols = jnp.broadcast_to(flags_ref[...].astype(F32), (DH, rows_here)).T
+    width = tok_v.shape[1]
+    tok_v[rows_here:, :] = jnp.broadcast_to(embed_ref[...].reshape(1, width), (16, width))
+    tok_load.wait()
+
+    def rope(rows):
+        return rows * cos_v[...] + pltpu.roll(rows, DH // 2, 1) * sin_v[...]
+
+    def q_piece(m, i):
+        return (remote(stq.at[m], qb.at[z], q_send.at[m], q_recv.at[z], seq_of(core, x, i), y_hi * 2 + y_lo),
+                pltpu.make_async_copy(stq.at[m], qb.at[z], q_recv.at[z]))
+
+    def kv_piece(high, low, i):
+        slot = low * (1 - high) * OWN[0, 1] + high * (OWN[0, 2] + low * (OWN[0, 3] - OWN[0, 2]))
+        m = 2 * high + low
+        return (remote(stkv.at[m], kvb.at[slot], a_send.at[m], kv_recv.at[slot],
+                       seq_of(core, x, i), y_hi * 2 + y_lo),
+                pltpu.make_async_copy(stkv.at[m], kvb.at[slot], kv_recv.at[slot]))
+
+    def launch(there, here, i):
+        own = jnp.logical_and(straight, z == i)
+        pl.when(own)(here.start)
+        pl.when(jnp.logical_not(own))(there.start)
+
+    def among(n, picks):
+        return functools.reduce(jnp.logical_or, [n == p for p in picks])
+
+    score_scale = DH ** -0.5 * math.log2(math.e)
+    q_steps = [n for n, (kind, _) in enumerate(ORDER) if kind == "q"]
+    kv_steps = {e: n for n, (kind, e) in enumerate(ORDER) if kind == "kv"}
+
+    def project(n, _):
+        pltpu.make_async_copy(wq_hbm.at[:, pl.ds(0, 256)], w_v.at[n], load_sem.at[n]).wait()
+        pacc[...] = jnp.dot(tok_v[...], w_v[n], preferred_element_type=F32)
+
+        def rows(e):
+            cols = slice(e * DH, (e + 1) * DH)
+            return pacc[0:rows_here, cols] + flag_cols * pacc[rows_here:rows_here + 1, cols]
+
+        @pl.when(among(n, q_steps))
+        def _():
+            apart = n - q_steps[0]
+            for e in range(2):
+                i = (z // 2 + apart) % 2 * 2 + e
+                m = apart * 2 + e
+                stq[m] = turned_blocks((rope(rows(e)) * score_scale).astype(BF16))
+                launch(*q_piece(m, i), i)
+
+        @pl.when(jnp.logical_not(among(n, q_steps)))
+        def _():
+            high = among(n, (kv_steps[2], kv_steps[3])).astype(jnp.int32)
+            low = among(n, (kv_steps[1], kv_steps[3])).astype(jnp.int32)
+            i = (z // 2 + high) % 2 * 2 + (z + low) % 2
+            m = 2 * high + low
+            stkv[m, 0] = rope(rows(0)).astype(BF16)
+            stkv[m, 1] = turned_blocks(rows(1).astype(BF16))
+            launch(*kv_piece(high, low, i), i)
         return 0
 
-    lax.fori_loop(0, tok_v.shape[1] // DH, add_embed, 0)
-
-    def rope(rows):
-        return rows * cos_ref[...] + pltpu.roll(rows, DH // 2, 1) * sin_ref[...]
-
-    def piece(n, e):
-        return order_pair(n) * 2 + e
-
-    def order_pair(n):
-        return order[n][1]
-
-    def a2a_q(m, pair, e):
-        i = pair * 2 + e
-        args = (stq.at[m], qb.at[z], q_send.at[m], q_recv.at[z])
-        return remote(*args, seq_of(core, x, i), y_hi * 2 + y_lo), pltpu.make_async_copy(
-            stq.at[m], qb.at[z], q_recv.at[z]), jnp.logical_and(straight, z == i)
-
-    def a2a_kv(m, pair, e):
-        i = pair * 2 + e
-        d = (z - i + 4) % 4
-        slot = d + (d + 3) // 4
-        return remote(stkv.at[m], kvb.at[slot], a_send.at[m], kv_recv.at[slot],
-                      seq_of(core, x, i), y_hi * 2 + y_lo), pltpu.make_async_copy(
-            stkv.at[m], kvb.at[slot], kv_recv.at[slot]), jnp.logical_and(straight, z == i)
-
-    def launch(copies):
-        far_copy, own_copy, own = copies
-
-        @pl.when(own)
-        def _():
-            own_copy.start()
-
-        @pl.when(jnp.logical_not(own))
-        def _():
-            far_copy.start()
-
-    def drain(copies):
-        far_copy, _, own = copies
-
-        @pl.when(jnp.logical_not(own))
-        def _():
-            far_copy.wait_send()
-
-    score_scale = DH ** -0.5 * math.log2(math.e)
-    for n in range(6):
-        w_load(n).wait()
-        pacc[...] = jnp.zeros_like(pacc)
-
-        def multiply(k, _, n=n):
-            depth = pl.ds(pl.multiple_of(k * 512, 512), 512)
-            pacc[...] += jnp.dot(tok_v[:, depth], w_v[n, depth, :], preferred_element_type=F32)
-            return 0
-
-        lax.fori_loop(0, tok_v.shape[1] // 512, multiply, 0)
-        pair = order[n][1]
-        for e in range(2):
-            rows = pacc[:, e * DH:(e + 1) * DH]
-            if n < 2:
-                m = n * 2 + e
-                stq[m] = turned_blocks((rope(rows) * score_scale).astype(BF16))
-                launch(a2a_q(m, pair, e))
-            else:
-                m = (n - 2) // 2 * 2 + e
-                if n % 2 == 0:
-                    stkv[m, 0] = rope(rows).astype(BF16)
-                else:
-                    stkv[m, 1] = turned_blocks(rows.astype(BF16))
-                    launch(a2a_kv(m, pair, e))
+    lax.fori_loop(0, 6, project, 0)
 
     acc[...] = jnp.zeros_like(acc)
     total_ref[...] = jnp.zeros_like(total_ref)
-    for j in range(4):
-        remote(qb.at[j], qb.at[j], q_send.at[0], q_recv.at[j], seq, sib).wait_recv()
-    q_dump = pltpu.make_async_copy(qb, q_out, dump_sem.at[16])
-    q_dump.start()
-
     sends = []
 
     def forward(slot, to_slot, s, h):
@@ -227,7 +246,12 @@
         sends.append(copy)
         copy().start()
 
+    taken = set()
+
     def arrived(slot):
+        if slot in taken:
+            return
+        taken.add(slot)
         remote(kvb.at[slot], kvb.at[slot], f_send.at[0], kv_recv.at[slot], seq, sib).wait_recv()
         if slot not in OWN_OF:
             return
@@ -235,31 +259,35 @@
         if dx == 0:
             forward(slot, OWN[1, d], x_up, head)
             forward(slot, OWN[3, d], x_down, head)
-        if dx == 1 and d % 2 == 0:
+        if dx == 1 and d in (0, 3):
             forward(slot, OWN[2, d], x_up, head)
-        if dx == 3 and d % 2 == 1:
+        if dx == 3 and d in (1, 2):
             forward(slot, OWN[2, d], x_down, head)
         forward(slot, SIB[dx, d], seq, sib)
 
-    extra = {
-        2: lambda: w_cross_in(0),
-        4: lambda: w_sib(8).start(),
-        5: lambda: (w_side_in(0).wait_recv(), w_sib(4).start()),
-        7: lambda: w_cross_in(1),
-        10: lambda: (w_side_in(1).wait_recv(), w_sib(5).start()),
-        12: lambda: w_cross_in(2),
-        15: lambda: (w_side_in(2).wait_recv(), w_sib(6).start()),
-    }
+    for key in ((0, 0), (1, 0), (3, 0)):
+        arrived(OWN[key])
+    for j in range(4):
+        remote(qb.at[j], qb.at[j], q_send.at[0], q_recv.at[j], seq, sib).wait_recv()
+    q_dump = pltpu.make_async_copy(qb, q_out, dump_sem.at[16])
+    q_dump.start()
     blocks = qb.shape[0]
 
     def step(t, _):
         for k in range(16):
             @pl.when(t == k)
             def _(k=k):
+                for key in EARLY.get(k, ()):
+                    arrived(OWN[key])
                 arrived(2 * k)
                 arrived(2 * k + 1)
-                if k in extra:
-                    extra[k]()
+                for action, n in EXTRA.get(k, ()):
+                    if action == "own":
+                        w_sib(16).start()
+                    elif action == "in":
+                        w_arrived(n)
+                    else:
+                        w_side(n)
 
         pltpu.make_async_copy(kvb.at[pl.ds(2 * t, 2)], kv_out.at[pl.ds(2 * t, 2)], dump_sem.at[t]).start()
         keys = kvb[pl.ds(2 * t, 2), 0].reshape(1024, DH)
@@ -280,26 +308,33 @@
 
     lax.fori_loop(0, 16, step, 0)
 
-    w_cross_in(3)
-    for i in range(blocks):
-        cols = slice(i * 512, (i + 1) * 512)
+    for action, n in EXTRA[16]:
+        w_arrived(n) if action == "in" else w_side(n)
+
+    def finish(i, _):
+        cols = pl.ds(pl.multiple_of(i * DH, DH), DH)
         total = jnp.sum(total_ref[:, cols], axis=0, keepdims=True)
-        done = (acc[:, cols] / total).astype(BF16)
-        for n in range(4):
-            o_ref[i * 512 + n * DH:i * 512 + (n + 1) * DH, :] = done[:, n * DH:(n + 1) * DH].T
-    w_side_in(3).wait_recv()
-    w_sib(7).start()
-
-    for n in range(9):
+        o_ref[cols, :] = (acc[:, cols] / total).astype(BF16).T
+        return 0
+
+    lax.fori_loop(0, blocks * 4, finish, 0)
+
+    for n in range(17):
         w_sib(n).wait_recv()
         w_sib(n).wait_send()
-    for k in range(4):
-        w_cross(k).wait_send()
-        w_side(k).wait_send()
-    for n in range(2):
-        for e in range(2):
-            drain(a2a_q(n * 2 + e, order[n][1], e))
-            drain(a2a_kv(n * 2 + e, order[2 + 2 * n][1], e))
+    for n in range(len(CROSS)):
+        w_cross(n).wait_send()
+    for q in range(2):
+        w_y(q).wait_send()
+    for q in range(8):
+        w_z(q).wait_send()
+    for m in range(4):
+        own = jnp.logical_and(straight, z % 2 == m) if m < 2 else None
+        for there, alone in ((q_piece(m, 0)[0], own), (kv_piece(m // 2, m % 2, 0)[0], straight if m == 0 else None)):
+            if alone is None:
+                there.wait_send()
+            else:
+                pl.when(jnp.logical_not(alone))(there.wait_send)
     for copy in sends:
         copy().wait_send()
     q_dump.wait()
@@ -424,18 +459,8 @@
             pl.when(jnp.logical_not(own))(far.wait_send)
 
 
-def rope_tables(rows):
-    halfway = DH // 2
-    frequency = jnp.exp(jnp.arange(halfway).astype(F32) * (-2.0 * math.log(500000.0) / DH))
-    positions = (lax.axis_index("seq") * rows + jnp.arange(rows)).astype(F32)
-    angles = positions[:, None] * frequency[None, :]
-    cosine, sine = jnp.cos(angles), jnp.sin(angles)
-    return jnp.concatenate([cosine, cosine], axis=1), jnp.concatenate([-sine, sine], axis=1)
-
-
 def shards(tokens, mask_flags, mask_embed, w_query, w_key, w_value, w_out):
     rows, width = tokens.shape
-    cosine, sine = rope_tables(rows)
     vmem, hbm = pl.BlockSpec(memory_space=pltpu.VMEM), pl.BlockSpec(memory_space=pl.ANY)
     dma = pltpu.SemaphoreType.DMA
     struct = jax.ShapeDtypeStruct
@@ -445,25 +470,27 @@
             struct((4 * rows, DH), BF16), struct((8, 4 * rows), F32), struct((4, rows, DH), BF16),
             struct((32, 2, rows, DH), BF16), struct((3,) + w_out.shape, BF16),
         ),
-        in_specs=[hbm, vmem, vmem, vmem, vmem, hbm, hbm, hbm, hbm],
+        in_specs=[hbm, vmem, vmem, hbm, hbm, hbm, hbm],
         out_specs=(vmem, vmem, hbm, hbm, hbm),
         scratch_shapes=[
-            pltpu.VMEM((rows, width), BF16),
+            pltpu.VMEM((rows + 16, width), BF16),
             pltpu.VMEM((6, width, 256), BF16),
-            pltpu.VMEM((rows, 256), F32),
+            pltpu.VMEM((rows + 16, 256), F32),
+            pltpu.VMEM((rows, DH), F32),
+            pltpu.VMEM((rows, DH), F32),
             pltpu.VMEM((4, rows, DH), BF16),
             pltpu.VMEM((4, 2, rows, DH), BF16),
             pltpu.VMEM((4, rows, DH), BF16),
             pltpu.VMEM((32, 2, rows, DH), BF16),
             pltpu.VMEM((DH, 4 * rows), F32),
             dma((7,)), dma((4,)), dma((4,)), dma((4,)), dma((32,)), dma((28,)), dma((17,)),
-            dma((4,)), dma((4,)), dma((4,)), dma((4,)), dma((9,)), dma((9,)),
+            dma((6,)), dma((2,)), dma((8,)), dma((8,)), dma((8,)), dma((17,)), dma((17,)),
         ],
         compiler_params=pltpu.CompilerParams(
             collective_id=0, has_side_effects=True, vmem_limit_bytes=VMEM_BYTES
         ),
         name="attend",
-    )(tokens, mask_flags.reshape(1, rows), mask_embed.reshape(1, width), cosine, sine, w_query, w_key, w_value, w_out)
+    )(tokens, mask_flags.reshape(1, rows), mask_embed, w_query, w_key, w_value, w_out)
     attention = pl.pallas_call(
         repair_kernel,
         out_shape=struct((4 * rows, DH), BF16),

time: 247 us -> 207 us (0.84)
  Pallas kernels: 240 us -> 203 us
    pallas_call x1, Pallas kernels: 106 us -> 71.3 us  [shards(): pl.pallas_call(attend_kernel, out_shape=(struct((4 * rows, DH), BF16), st...]
    pallas_call x1, Pallas kernels: 21.1 us -> 18.6 us  [shards(): pl.pallas_call(out_kernel, out_shape=struct((rows // 4, width), BF16), in...]
where the time goes in v2:
time: 207 us; the launch traced here: 206 us
  Pallas kernels  203 us (98%)
  local copies, waits for them, and re-layouts  2.29 us (1%)
    pallas_call x1, Pallas kernels, shards(): pl.pallas_call(repair_kernel, out_shape=struct((4 * rows, DH), BF16), in_...  113 us
    pallas_call x1, Pallas kernels, shards(): pl.pallas_call(attend_kernel, out_shape=(struct((4 * rows, DH), BF16), st...  71.3 us
    pallas_call x1, Pallas kernels, shards(): pl.pallas_call(out_kernel, out_shape=struct((rows // 4, width), BF16), in...  18.6 us

profile of v2, /device:TPU:1, one launch (start us, length us, event | category | flops | bytes accessed | tf_op | source)
XLA Modules:
  0.0 205.5 jit_solution(9764354911536165443)
XLA Ops:
  0.0 71.3 %attend.1 = (bf16[2048,128]{1,0:T(8,128)(2,1)}, f32[8,2048]{1,0:T(8,128)}, bf16[4,512,128]{2,1,0:T(8,128)(2,1)}, bf16[32,2,512,128]{3,2,1,0:T(8,128)(2,1)}, bf16[3,512,4096]{2,1,0:T(8,128)(2,1)}) custom-call(bf16[512,4096]{1,0:T(8,128)(2,1)} %tok_hbm.1, s32[1,512]{1,0:T(1,128)} %bitcast.1, bf16[4096]{0:T(1024)(128)(2,1)} %embed_ref.1, ...), custom_call_target="tpu_custom_call" | custom-call | tf_op jit(solution)/shard_map/attend/pallas_call | solution.py:467
  71.3 113.3 %repair.1.o_ref = bf16[2048,128]{1,0:T(8,128)(2,1)} custom-call(f32[8,2048]{1,0:T(8,128)} %get-tuple-element.10.total_ref, bf16[4,512,128]{2,1,0:T(8,128)(2,1)} %get-tuple-element.11.q_hbm, bf16[32,2,512,128]{3,2,1,0:T(8,128)(2,1)} %get-tuple-element.12.kv_hbm, bf16[2048,128]{1,0:T(8,128)(2,1)} %get-tuple-element.13.o_in), custom_call_target="tpu_custom_call", output_to_operand_aliasing={{}: (3, {})} | custom-call | tf_op jit(solution)/shard_map/repair/pallas_call | solution.py:494
  184.6 18.6 %project_out.1 = bf16[128,4096]{1,0:T(8,128)(2,1)} custom-call(bf16[2048,128]{1,0:T(8,128)(2,1)} %repair.1.o_ref, bf16[512,4096]{1,0:T(8,128)(2,1)} %wo_hbm.3, bf16[3,512,4096]{2,1,0:T(8,128)(2,1)} %get-tuple-element.14.wg_hbm), custom_call_target="tpu_custom_call" | custom-call | tf_op jit(solution)/shard_map/project_out/pallas_call | solution.py:512
  203.2 2.3 %copy.11 = bf16[128,4096]{1,0:T(8,128)(2,1)} copy(bf16[128,4096]{1,0:T(8,128)(2,1)} %project_out.1) | data formatting | bytes 2097152

commit v3 on v0

v3 whole, which is shorter than its diff:
```python
import functools
import math

import jax
import jax.numpy as jnp
from jax import lax
from jax.experimental import pallas as pl
from jax.experimental.pallas import tpu as pltpu
from jax.sharding import PartitionSpec as P

DH = 128
MESH = pl.DeviceIdType.MESH
F32 = jnp.float32
BF16 = jnp.bfloat16
VMEM_BYTES = 60 * 2**20
TOTAL_LOW = 2.0**-60
TOTAL_HIGH = 2.0**100

USE = (
    ("own", 0, 0), ("sib", 0, 0), ("own", 1, 0), ("own", 3, 0), ("sib", 1, 0), ("sib", 3, 0), ("own", 2, 0), ("sib", 2, 0),
    ("own", 0, 1), ("sib", 0, 1), ("own", 1, 1), ("own", 3, 1), ("sib", 1, 1), ("sib", 3, 1), ("own", 0, 3), ("sib", 0, 3),
    ("own", 0, 2), ("sib", 0, 2), ("own", 1, 3), ("own", 3, 3), ("sib", 1, 3), ("sib", 3, 3), ("own", 2, 1), ("sib", 2, 1),
    ("own", 1, 2), ("own", 3, 2), ("sib", 1, 2), ("sib", 3, 2), ("own", 2, 3), ("sib", 2, 3), ("own", 2, 2), ("sib", 2, 2),
)
OWN = {(dx, e): n for n, (by, dx, e) in enumerate(USE) if by == "own"}
SIB = {(dx, e): n for n, (by, dx, e) in enumerate(USE) if by == "sib"}
EARLY = {2: ((2, 0), (0, 1)), 4: ((0, 3),), 7: ((0, 2),), 9: ((2, 1),), 13: ((2, 3),)}
OWN_OF = {slot: key for key, slot in OWN.items()}

ORDER = (("kv", 0), ("q", 0), ("q", 1), ("kv", 1), ("kv", 3), ("kv", 2))
LAST = 15
CROSS = (0, 1, 2, 3, 6, 7, 15)
EXTRA = {
    0: (("own", 0),), 4: (("in", 0),), 5: (("in", 1),), 6: (("in", 2), ("in", 3)), 8: (("in", 6),), 11: (("in", 7), ("side", 0)),
    12: (("in", 4), ("side", 1)), 13: (("in", 5), ("side", 2), ("side", 3)), 14: (("side", 6),),
    16: (("side", 7), ("side", 4), ("side", 5)),
}


def place():
    seq, head = lax.axis_index("seq"), lax.axis_index("head")
    y_lo, x, z = seq // 16, (seq // 4) % 4, seq % 4
    y_hi, core = head // 2, head % 2
    return y_lo, x, z, y_hi, core


def seq_of(y_lo, x, z):
    return y_lo * 16 + x * 4 + z


def remote(src, dst, send_sem, recv_sem, seq, head):
    return pltpu.make_async_remote_copy(
        src_ref=src, dst_ref=dst, send_sem=send_sem, recv_sem=recv_sem,
        device_id=(seq, head), device_id_type=MESH,
    )


def lanes(blocks):
    return jnp.concatenate([blocks[n] for n in range(blocks.shape[0])], axis=1)


def turned_blocks(rows):
    return jnp.concatenate(
        [rows[n * DH:(n + 1) * DH].T for n in range(rows.shape[0] // DH)], axis=0
    )


def attend_kernel(
    tok_hbm, flags_ref, embed_ref, wq_hbm, wk_hbm, wv_hbm, wo_hbm,
    out_ref, bad_ref,
    tok_v, w_v, pacc, cos_v, sin_v, stq, stkv, qb, kvb, acc, total_v, o_v, full, w_full, flag_v, out_acc,
    load_sem, q_send, q_recv, a_send, kv_recv, f_send,
    wx_send, wy_send, wx_recv, wz_send, wz_recv, ws_send, ws_recv, o_send, o_recv, flag_send, flag_recv,
):
    y_lo, x, z, y_hi, core = place()
    seq, head = seq_of(y_lo, x, z), y_hi * 2 + core
    sib = y_hi * 2 + (1 - core)
    straight = core == y_lo
    rows_here = tok_hbm.shape[0]
    x_up, x_down = seq_of(y_lo, (x + 1) % 4, z), seq_of(y_lo, (x + 3) % 4, z)
    z_up, z_down = seq_of(y_lo, x, (z + 1) % 4), seq_of(y_lo, x, (z + 3) % 4)
    y_seq = seq_of(1 - y_lo, x, z)
    cross_head = (1 - y_hi) * 2 + core

    def swapped(e):
        return 2 * ((z // 2 + e // 2) % 2) + (z % 2 + e % 2) % 2

    tok_load = pltpu.make_async_copy(tok_hbm, tok_v.at[pl.ds(0, rows_here)], load_sem.at[6])
    tok_load.start()
    for n, (kind, which) in enumerate(ORDER):
        if kind == "q":
            cols = pl.ds(pl.multiple_of(swapped(2 * which) // 2 * 256, 256), 256)
            pltpu.make_async_copy(wq_hbm.at[:, cols], w_v.at[n], load_sem.at[n]).start()
        else:
            cols = pl.ds(pl.multiple_of(swapped(which) * DH, DH), DH)
            pltpu.make_async_copy(wk_hbm.at[:, cols], w_v.at[n, :, pl.ds(0, DH)], load_sem.at[n]).start()
            pltpu.make_async_copy(wv_hbm.at[:, cols], w_v.at[n, :, pl.ds(DH, DH)], load_sem.at[n]).start()

    barrier = pltpu.get_barrier_semaphore()

    def greet(s, h):
        pl.semaphore_signal(barrier, inc=1, device_id=(s, h), device_id_type=MESH)

    for i in range(4):
        @pl.when(jnp.logical_not(jnp.logical_and(straight, z == i)))
        def _():
            greet(seq_of(core, x, i), y_hi * 2 + y_lo)
    for s, h in ((x_up, head), (x_down, head), (z_up, head), (z_down, head),
                 (seq, sib), (y_seq, head), (y_seq, cross_head)):
        greet(s, h)

    for hi in range(2):
        for lo in range(2):
            for zz in range(4):
                same = functools.reduce(jnp.logical_and, (straight, y_hi == hi, y_lo == lo, z == zz))

                @pl.when(jnp.logical_not(same))
                def _(hi=hi, lo=lo, zz=zz):
                    greet(seq_of(lo, x, zz), hi * 2 + y_lo)
    flag_peers = [(seq_of((y_lo + n // 4) % 2, x, (z + n) % 4), head) for n in range(1, 8)] + [
        (seq_of(y_lo, (x + n) % 4, z), head) for n in range(1, 4)
    ] + [(seq, (head + n) % 4) for n in range(1, 4)]
    for s, h in flag_peers:
        greet(s, h)

    lane = lax.broadcasted_iota(jnp.int32, (1, DH), 1)
    frequency = jnp.exp((lane % (DH // 2)).astype(F32) * (-2.0 * math.log(500000.0) / DH))
    sign = jnp.where(lane < DH // 2, -1.0, 1.0)

    def angle_rows(n, _):
        rows = pl.ds(pl.multiple_of(n * 64, 64), 64)
        position = (lax.broadcasted_iota(jnp.int32, (64, DH), 0) + (seq * rows_here + n * 64)).astype(F32)
        angle = position * frequency
        cos_v[rows, :] = jnp.cos(angle)
        sin_v[rows, :] = jnp.sin(angle) * sign
        return 0

    lax.fori_loop(0, rows_here // 64, angle_rows, 0)

    @pl.when(straight)
    def _():
        pl.semaphore_wait(barrier, 38)

    @pl.when(jnp.logical_not(straight))
    def _():
        pl.semaphore_wait(barrier, 40)

    def w_chunk(colour_y, colour_z, q):
        base = (colour_y * 2 + colour_z) * 128 + 32 * (q % 4)
        return pl.ds(pl.multiple_of(base, 32), 32)

    def w_rows(q, y=None, z_par=None):
        y = y_lo if y is None else y
        z_par = z % 2 if z_par is None else z_par
        return w_chunk(y if q < 4 else 1 - y, z_par, q)

    group = (1 - y_hi) * 2 + core

    def w_cross(n):
        q = CROSS[n]
        rows = w_rows(q, y=1 - y_lo) if q < 8 else w_rows(q - 8, y=1 - y_lo, z_par=1 - z % 2)
        return remote(wo_hbm.at[rows], w_full.at[head, rows], wx_send.at[n], wx_recv.at[CROSS[n]], y_seq, cross_head)

    def w_y(q):
        rows = w_rows(q)
        return remote(w_full.at[group, rows], w_full.at[group, rows], wy_send.at[q], wx_recv.at[q + 4], y_seq, head)

    def w_z(q, rows=None):
        rows = w_rows(q) if rows is None else rows
        return remote(w_full.at[group, rows], w_full.at[group, rows], wz_send.at[q], wz_recv.at[q],
                      z_up if q % 2 == 0 else z_down, head)

    def w_sib(n):
        if n == 16:
            return remote(wo_hbm, w_full.at[head], ws_send.at[16], ws_recv.at[16], seq, sib)
        rows = w_rows(n) if n < 8 else w_rows(n - 8, z_par=1 - z % 2)
        return remote(w_full.at[group, rows], w_full.at[group, rows], ws_send.at[n], ws_recv.at[n], seq, sib)

    def w_arrived(q):
        rows = w_rows(q)
        remote(w_full.at[group, rows], w_full.at[group, rows], wx_send.at[0], wx_recv.at[q], y_seq, head).wait_recv()
        if q < 2:
            w_y(q).start()
        if q + 8 not in CROSS:
            w_z(q).start()
        w_sib(q).start()

    def w_side(q):
        if q + 8 in CROSS:
            rows = w_rows(q, z_par=1 - z % 2)
            remote(w_full.at[group, rows], w_full.at[group, rows], wx_send.at[0], wx_recv.at[q + 8], y_seq, head).wait_recv()
            w_sib(8 + q).start()
            return
        w_z(q, w_rows(q, z_par=1 - z % 2)).wait_recv()
        w_sib(8 + q).start()

    for n in range(len(CROSS)):
        w_cross(n).start()
    own_w = pltpu.make_async_copy(wo_hbm, w_full.at[head], load_sem.at[7])

    flag_cols = jnp.broadcast_to(flags_ref[...].astype(F32), (DH, rows_here)).T
    width = tok_v.shape[1]
    tok_v[rows_here:, :] = jnp.broadcast_to(embed_ref[...].reshape(1, width), (16, width))
    tok_load.wait()

    def rope(rows):
        return rows * cos_v[...] + pltpu.roll(rows, DH // 2, 1) * sin_v[...]

    def q_piece(m, i):
        return (remote(stq.at[m], qb.at[z], q_send.at[m], q_recv.at[z], seq_of(core, x, i), y_hi * 2 + y_lo),
                pltpu.make_async_copy(stq.at[m], qb.at[z], q_recv.at[z]))

    def kv_piece(high, low, i):
        slot = (1 - high) * low * OWN[0, 1] + high * (OWN[0, 2] + low * (OWN[0, 3] - OWN[0, 2]))
        m = 2 * high + low
        return (remote(stkv.at[m], kvb.at[slot], a_send.at[m], kv_recv.at[slot],
                       seq_of(core, x, i), y_hi * 2 + y_lo),
                pltpu.make_async_copy(stkv.at[m], kvb.at[slot], kv_recv.at[slot]))

    def launch(there, here, i):
        own = jnp.logical_and(straight, z == i)
        pl.when(own)(here.start)
        pl.when(jnp.logical_not(own))(there.start)

    def among(n, picks):
        return functools.reduce(jnp.logical_or, [n == p for p in picks])

    sends = []

    def forward(slot, to_slot, s, h, only=None):
        def copy():
            return remote(kvb.at[slot], kvb.at[to_slot], f_send.at[n_send], kv_recv.at[to_slot], s, h)
        n_send = len(sends)
        sends.append((copy, only))
        if only is None:
            copy().start()
        else:
            pl.when(only)(copy().start)

    crooked = jnp.logical_not(straight)
    taken = set()

    def arrived(slot):
        if slot in taken:
            return
        taken.add(slot)
        remote(kvb.at[slot], kvb.at[slot], f_send.at[0], kv_recv.at[slot], seq, sib).wait_recv()
        if slot not in OWN_OF:
            return
        dx, d = OWN_OF[slot]
        if dx == 0:
            forward(slot, OWN[1, d], x_up, head)
            forward(slot, OWN[3, d], x_down, head)
        if dx == 1:
            forward(slot, OWN[2, d], x_up, head, straight if d in (0, 3) else crooked)
        if dx == 3:
            forward(slot, OWN[2, d], x_down, head, crooked if d in (0, 3) else straight)
        forward(slot, SIB[dx, d], seq, sib)

    score_scale = DH ** -0.5 * math.log2(math.e)
    q_steps = [n for n, (kind, _) in enumerate(ORDER) if kind == "q"]
    kv_steps = {e: n for n, (kind, e) in enumerate(ORDER) if kind == "kv"}

    def project(n, _):
        pltpu.make_async_copy(wq_hbm.at[:, pl.ds(0, 256)], w_v.at[n], load_sem.at[n]).wait()
        pacc[...] = jnp.dot(tok_v[...], w_v[n], preferred_element_type=F32)

        @pl.when(jnp.logical_or(jnp.logical_and(straight, n == 1), jnp.logical_and(crooked, n == 3)))
        def _():
            arrived(OWN[0, 0])

        def rows(e):
            cols = slice(e * DH, (e + 1) * DH)
            return pacc[0:rows_here, cols] + flag_cols * pacc[rows_here:rows_here + 1, cols]

        @pl.when(among(n, q_steps))
        def _():
            apart = n - q_steps[0]
            for e in range(2):
                i = (z // 2 + apart) % 2 * 2 + e
                m = apart * 2 + e
                stq[m] = turned_blocks((rope(rows(e)) * score_scale).astype(BF16))
                launch(*q_piece(m, i), i)

        @pl.when(jnp.logical_not(among(n, q_steps)))
        def _():
            high = among(n, (kv_steps[2], kv_steps[3])).astype(jnp.int32)
            low = among(n, (kv_steps[1], kv_steps[3])).astype(jnp.int32)
            i = (z // 2 + high) % 2 * 2 + (z + low) % 2
            m = 2 * high + low
            stkv[m, 0] = rope(rows(0)).astype(BF16)
            stkv[m, 1] = turned_blocks(rows(1).astype(BF16))

            @pl.when(high == 0)
            def _():
                launch(*kv_piece(high, low, i), i)
        return 0

    lax.fori_loop(0, 6, project, 0)

    acc[...] = jnp.zeros_like(acc)
    total_v[...] = jnp.zeros_like(total_v)
    for key in ((1, 0), (3, 0)):
        arrived(OWN[key])
    for j in range(4):
        remote(qb.at[j], qb.at[j], q_send.at[0], q_recv.at[j], seq, sib).wait_recv()
    own_w.start()
    kv_piece(1, 1, swapped(3))[0].start()
    blocks = qb.shape[0]

    def take(k):
        if k == 1:
            kv_piece(1, 0, swapped(2))[0].start()
        for key in EARLY.get(k, ()):
            arrived(OWN[key])
        arrived(2 * k)
        arrived(2 * k + 1)
        for action, n in EXTRA.get(k, ()):
            if action == "own":
                w_sib(16).start()
            elif action == "in":
                w_arrived(n)
            else:
                w_side(n)

    def chunk_pair(t):
        keys = kvb[pl.ds(2 * t, 2), 0].reshape(1024, DH)
        return keys, lanes(kvb[pl.ds(2 * t, 2), 1].reshape(8, DH, DH))

    def scores(keys, i):
        return jnp.dot(keys, lanes(qb[i].reshape(4, DH, DH)), preferred_element_type=F32)

    def add_weighted(now, values, cols):
        weights = jnp.exp2(now)
        total_v[:, cols] += jnp.sum(weights.reshape(128, 8, 512), axis=0)
        acc[:, cols] += jnp.dot(values, weights.astype(BF16), preferred_element_type=F32)

    def step(t, _):
        for k in range(LAST):
            pl.when(t == k)(functools.partial(take, k))
        keys, values = chunk_pair(t)
        now = scores(keys, 0)
        for i in range(blocks):
            later = scores(keys, i + 1) if i + 1 < blocks else None
            add_weighted(now, values, slice(i * 512, (i + 1) * 512))
            now = later
        return 0

    lax.fori_loop(0, LAST, step, 0)
    for k in range(LAST, 16):
        take(k)

    mine = y_hi * 8 + y_lo * 4 + z

    def o_piece(zz, hi, c):
        rows = pl.ds(pl.multiple_of(zz * 512 + hi * 256 + c * 128, 128), 128)
        return (remote(o_v.at[rows], full.at[mine], o_send.at[zz * 4 + hi * 2 + c], o_recv.at[mine],
                       seq_of(core, x, zz), hi * 2 + c),
                pltpu.make_async_copy(o_v.at[rows], full.at[mine], o_recv.at[mine]))

    def o_stays(zz, hi, c):
        return functools.reduce(jnp.logical_and, (straight, zz == z, y_hi == hi, core == c))

    def last(n, _):
        zz = (z + 1 + n) % 4
        cols = pl.ds(pl.multiple_of(zz * 512, 512), 512)
        pairs = [chunk_pair(t) for t in range(LAST, 16)]
        now = scores(pairs[0][0], zz)
        for k, (_, values) in enumerate(pairs):
            later = scores(pairs[k + 1][0], zz) if k + 1 < len(pairs) else None
            add_weighted(now, values, cols)
            now = later
        total = jnp.sum(total_v[:, cols], axis=0, keepdims=True)
        done = (acc[:, cols] / total).astype(BF16)
        for m in range(4):
            o_v[pl.ds(pl.multiple_of(zz * 512 + m * DH, DH), DH), :] = done[:, m * DH:(m + 1) * DH].T
        for hi in range(2):
            for c in range(2):
                there, here = o_piece(zz, hi, c)
                stays = o_stays(zz, hi, c)
                pl.when(stays)(here.start)
                pl.when(jnp.logical_not(stays))(there.start)
        return 0

    lax.fori_loop(0, blocks, last, 0)

    rounds = (range(0, 7), range(7, 10), range(10, 13))

    def flag(n):
        k = [n in r for r in rounds].index(True)
        return remote(flag_v.at[13 + k], flag_v.at[n], flag_send.at[n], flag_recv.at[n], *flag_peers[n])

    def tell(k):
        for n in rounds[k]:
            flag(n).start()

    def hear(k):
        for n in rounds[k]:
            flag(n).wait_recv()
        told = flag_v[13 + k]
        for n in rounds[k]:
            told = jnp.maximum(told, flag_v[n])
        return told

    sums = jnp.sum(total_v[...], axis=0, keepdims=True)
    good = jnp.logical_and(sums > TOTAL_LOW, sums < TOTAL_HIGH)
    flag_v[13] = jnp.broadcast_to(jnp.max(jnp.where(good, 0.0, 1.0), axis=1, keepdims=True), (8, DH))
    tell(0)
    for action, n in EXTRA[16]:
        w_arrived(n) if action == "in" else w_side(n)
    own_w.wait()
    for n in range(17):
        w_sib(n).wait_recv()

    def project_out(n, _):
        zz = (z + 3 - n) % 4
        for hi in range(4):
            remote(full.at[hi * 4 + zz], full.at[hi * 4 + zz], o_send.at[0], o_recv.at[hi * 4 + zz], seq, sib).wait_recv()
        attention = jnp.concatenate([full[hi * 4 + zz] for hi in range(4)], axis=1)
        depth = pl.ds(pl.multiple_of(zz * DH, DH), DH)

        def columns(m, _):
            cols = pl.ds(pl.multiple_of(m * 512, 512), 512)
            weights = jnp.concatenate([w_full[hi, depth, cols] for hi in range(4)], axis=0)
            out_acc[:, cols] += jnp.dot(attention, weights, preferred_element_type=F32)
            return 0

        lax.fori_loop(0, out_ref.shape[1] // 512, columns, 0)
        for k in range(2):
            @pl.when(n == k)
            def _(k=k):
                flag_v[14 + k] = hear(k)
                tell(k + 1)
        return 0

    out_acc[...] = jnp.zeros_like(out_acc)
    lax.fori_loop(0, 4, project_out, 0)
    out_ref[...] = out_acc[...].astype(BF16)
    bad_ref[0, 0] = jnp.max(hear(2))

    for n in range(13):
        flag(n).wait_send()
    for zz in range(4):
        for hi in range(2):
            for c in range(2):
                pl.when(jnp.logical_not(o_stays(zz, hi, c)))(o_piece(zz, hi, c)[0].wait_send)
    for n in range(17):
        w_sib(n).wait_send()
    for n in range(len(CROSS)):
        w_cross(n).wait_send()
    for q in range(2):
        w_y(q).wait_send()
    for q in range(8):
        if q + 8 not in CROSS:
            w_z(q).wait_send()
    for m in range(4):
        own = jnp.logical_and(straight, z % 2 == m) if m < 2 else None
        for there, alone in ((q_piece(m, 0)[0], own), (kv_piece(m // 2, m % 2, 0)[0], straight if m == 0 else None)):
            if alone is None:
                there.wait_send()
            else:
                pl.when(jnp.logical_not(alone))(there.wait_send)
    for copy, only in sends:
        if only is None:
            copy().wait_send()
        else:
            pl.when(only)(copy().wait_send)


def rotate(values, positions, head_size):
    halfway = head_size // 2
    indices = jnp.arange(halfway).astype(jnp.float32)
    frequency = jnp.exp(indices * (-2.0 * math.log(500000.0) / head_size))
    angles = positions[:, None] * frequency[None, :]
    cosine = jnp.cos(angles)[:, None, :]
    sine_table = jnp.sin(angles)[:, None, :]
    shaped = values.reshape(values.shape[0], -1, head_size)
    leading = shaped[..., :halfway]
    trailing = shaped[..., halfway:]
    turned = jnp.concatenate(
        [leading * cosine - trailing * sine_table, trailing * cosine + leading * sine_table],
        axis=-1,
    )
    return turned.reshape(values.shape)


def plain_shards(tokens, mask_flags, mask_embed, w_query, w_key, w_value, w_out):
    tok_rows = tokens.shape[0]
    head_size = DH
    heads_here = w_query.shape[1] // head_size
    mask_rows = mask_flags.astype(jnp.float32)[:, None]
    hidden = (
        tokens.astype(jnp.float32) + mask_rows * mask_embed.astype(jnp.float32)[None, :]
    ).astype(jnp.bfloat16)
    positions = (lax.axis_index("seq") * tok_rows + jnp.arange(tok_rows)).astype(jnp.float32)
    query_rows = rotate(
        jnp.dot(hidden, w_query, preferred_element_type=jnp.float32), positions, head_size
    ).astype(jnp.bfloat16)
    key_rows = rotate(
        jnp.dot(hidden, w_key, preferred_element_type=jnp.float32), positions, head_size
    ).astype(jnp.bfloat16)
    value_rows = jnp.dot(hidden, w_value, preferred_element_type=jnp.float32).astype(jnp.bfloat16)
    queries = query_rows.reshape(tok_rows, heads_here, head_size)
    score_scale = head_size ** (-0.5)
    row_peak = jnp.full((heads_here, tok_rows), -1e30, jnp.float32)
    weighted = jnp.zeros((tok_rows, heads_here, head_size), jnp.float32)
    peers = lax.axis_size("seq")
    ring = [(n, (n + 1) % peers) for n in range(peers)]

    def add_part(_, carried):
        keys, values, row_peak, total, weighted = carried
        scores = (
            jnp.einsum("qhd,khd->hqk", queries, keys.reshape(queries.shape), preferred_element_type=jnp.float32)
            * score_scale
        )
        new_peak = jnp.maximum(row_peak, jnp.max(scores, axis=-1))
        factor = jnp.exp(row_peak - new_peak)
        weights = jnp.exp(scores - new_peak[..., None])
        total = total * factor + jnp.sum(weights, axis=-1)
        update = jnp.einsum(
            "hqk,khd->qhd", weights.astype(jnp.bfloat16), values.reshape(queries.shape), preferred_element_type=jnp.float32
        )
        weighted = weighted * factor.T[:, :, None] + update
        return lax.ppermute(keys, "seq", ring), lax.ppermute(values, "seq", ring), new_peak, total, weighted

    _, _, _, total, weighted = lax.fori_loop(
        0, peers, add_part, (key_rows, value_rows, row_peak, jnp.zeros_like(row_peak), weighted)
    )
    attention = (weighted / total.T[:, :, None]).reshape(tok_rows, heads_here * head_size).astype(jnp.bfloat16)
    partials = jnp.dot(attention, w_out, preferred_element_type=jnp.float32)
    heads = lax.axis_size("head")
    here, part = lax.axis_index("head"), tok_rows // heads
    mixed_rows = lax.dynamic_slice_in_dim(partials, here * part, part, 0)
    for n in range(1, heads):
        leaving = lax.dynamic_slice_in_dim(partials, (here + n) % heads * part, part, 0)
        mixed_rows += lax.ppermute(leaving, "head", [(m, (m + n) % heads) for m in range(heads)])
    return mixed_rows.astype(jnp.bfloat16)


def shards(tokens, mask_flags, mask_embed, w_query, w_key, w_value, w_out):
    rows, width = tokens.shape
    vmem, hbm = pl.BlockSpec(memory_space=pltpu.VMEM), pl.BlockSpec(memory_space=pl.ANY)
    dma = pltpu.SemaphoreType.DMA
    struct = jax.ShapeDtypeStruct
    mixed_rows, bad = pl.pallas_call(
        attend_kernel,
        out_shape=(struct((rows // 4, width), BF16), struct((1, 1), F32)),
        in_specs=[hbm, vmem, vmem, hbm, hbm, hbm, hbm],
        out_specs=(vmem, pl.BlockSpec(memory_space=pltpu.SMEM)),
        scratch_shapes=[
            pltpu.VMEM((rows + 16, width), BF16),
            pltpu.VMEM((6, width, 256), BF16),
            pltpu.VMEM((rows + 16, 256), F32),
            pltpu.VMEM((rows, DH), F32),
            pltpu.VMEM((rows, DH), F32),
            pltpu.VMEM((4, rows, DH), BF16),
            pltpu.VMEM((4, 2, rows, DH), BF16),
            pltpu.VMEM((4, rows, DH), BF16),
            pltpu.VMEM((32, 2, rows, DH), BF16),
            pltpu.VMEM((DH, 4 * rows), F32),
            pltpu.VMEM((8, 4 * rows), F32),
            pltpu.VMEM((4 * rows, DH), BF16),
            pltpu.VMEM((16, DH, DH), BF16),
            pltpu.VMEM((4,) + w_out.shape, BF16),
            pltpu.VMEM((16, 8, DH), F32),
            pltpu.VMEM((rows // 4, width), F32),
            dma((8,)), dma((4,)), dma((4,)), dma((4,)), dma((32,)), dma((32,)),
            dma((7,)), dma((2,)), dma((16,)), dma((8,)), dma((8,)), dma((17,)), dma((17,)),
            dma((16,)), dma((16,)), dma((13,)), dma((13,)),
        ],
        compiler_params=pltpu.CompilerParams(
            collective_id=0, has_side_effects=True, vmem_limit_bytes=VMEM_BYTES
        ),
        name="attend",
    )(tokens, mask_flags.reshape(1, rows), mask_embed, w_query, w_key, w_value, w_out)
    return lax.cond(
        bad[0, 0] > 0.5,
        lambda: plain_shards(tokens, mask_flags, mask_embed, w_query, w_key, w_value, w_out),
        lambda: mixed_rows,
    )


def solution(mesh):
    placed = (
        P("seq", None),
        P("seq"),
        P(),
        P(None, "head"),
        P(None, "head"),
        P(None, "head"),
        P("head", None),
    )
    return jax.shard_map(
        shards, mesh=mesh, in_specs=placed, out_specs=P(("seq", "head"), None), check_vma=False
    )
```

time: 554 us -> 1020 us (1.84)
  waiting for transfers between devices: 339 us -> 739 us
  Pallas kernels: 0 us -> 81.2 us
  matrix products: 126 us -> 84.2 us
  starting transfers between devices: 0.27 us -> 38.8 us
  other arithmetic: 47 us -> 28.7 us
  local copies, waits for them, and re-layouts: 27.8 us -> 40.8 us
  between operations: 13.2 us -> 0.66 us
    ppermute x0 -> x67, waiting for transfers between devices: none -> 739 us  [the longest x32 357 us: add_part(): lax.ppermute(keys, 'seq', ring)]
    all_gather x2 -> x0, waiting for transfers between devices: 283 us -> none  [the longest x1 184 us: shards(): lax.all_gather(key_rows, 'seq', axis=0, tiled=True)]
    pallas_call x0 -> x1, Pallas kernels: none -> 81.2 us  [shards(): pl.pallas_call(attend_kernel, out_shape=(struct((rows // 4, width), BF16)...]
    reduce_scatter x1 -> x0, waiting for transfers between devices: 55.6 us -> none  [shards(): lax.psum_scatter(partials.astype(jnp.bfloat16), 'head', scatter_dimension...]
    dot_general x6 -> x68, matrix products: 126 us -> 84.2 us  [the longest x32 44.6 us: add_part(): jnp.einsum('hqk,khd->qhd', weights.astype(jnp.bfloat16), values.reshape(q...]
    ppermute x0 -> x67, starting transfers between devices: none -> 38.8 us  [the longest x3 35.5 us: plain_shards(): lax.ppermute(leaving, 'head', [(m, (m + n) % heads) for m in range(heads)])]
    while x0 -> x97, local copies, waits for them, and re-layouts: none -> 34.9 us
    reshape x1 -> x0, local copies, waits for them, and re-layouts: 21.3 us -> none  [shards(): lax.all_gather(value_rows, 'seq', axis=0, tiled=True)]
  transfers between devices with their start and end apart: 3 -> 67, of which waited for: 3 -> 67; matrix products, arithmetic and copies ran while one was open for 18% -> 12% of each run, Pallas kernels for 0% -> 0%
where the time goes in v3:
time: 1020 us
  waiting for transfers between devices  739 us (72%)
  matrix products  84.2 us (8%)
  Pallas kernels  81.2 us (8%)
  local copies, waits for them, and re-layouts  40.8 us (4%)
  starting transfers between devices  38.8 us (4%)
  other arithmetic  28.7 us (3%)
    ppermute x32, waiting for transfers between devices, add_part(): lax.ppermute(keys, 'seq', ring)  357 us
    ppermute x32, waiting for transfers between devices, add_part(): lax.ppermute(values, 'seq', ring)  293 us
    ppermute x3, waiting for transfers between devices, plain_shards(): lax.ppermute(leaving, 'head', [(m, (m + n) % heads) for m in range(heads)])  88.8 us
    pallas_call x1, Pallas kernels, shards(): pl.pallas_call(attend_kernel, out_shape=(struct((rows // 4, width), BF16)...  81.2 us
    dot_general x32, matrix products, add_part(): jnp.einsum('hqk,khd->qhd', weights.astype(jnp.bfloat16), values.reshape(q...  44.6 us
    ppermute x3, starting transfers between devices, plain_shards(): lax.ppermute(leaving, 'head', [(m, (m + n) % heads) for m in range(heads)])  35.5 us
    while x96, local copies, waits for them, and re-layouts  34.6 us
    dot_general x32, matrix products, add_part(): jnp.einsum('qhd,khd->hqk', queries, keys.reshape(queries.shape), preferre...  23 us
  transfers between devices with their start and end apart: 67, of which 67 were waited for; matrix products, arithmetic and copies ran while one was open for 12% of the time, Pallas kernels for 0%

profile of v3, /device:TPU:1, one launch (start us, length us, event | category | flops | bytes accessed | tf_op | source)
XLA Modules:
  0.0 1015.8 jit_solution(11924247163662380840)
XLA Ops:
  0.0 81.2 %attend.1 = (bf16[128,4096]{1,0:T(8,128)(2,1)S(1)}, f32[1,1]{1,0:T(1,128)}) custom-call(bf16[512,4096]{1,0:T(8,128)(2,1)} %tok_hbm.1, s32[1,512]{1,0:T(1,128)} %bitcast.54, bf16[4096]{0:T(1024)(128)(2,1)} %embed_ref.1, bf16[4096,512]{1,0:T(8,128)(2,1)} %wq_hbm.1, bf16[4096,512]{1,0:T(8,128)(2,1)} %wk_hbm.1, bf16[4096,512]{1,0:T(8,128)(2,1)} %wv_hbm.1, ...), custom_call_target="tpu_custom_call" | custom-call | tf_op jit(solution)/shard_map/attend/pallas_call | solution.py:545
  81.9 933.0 %conditional.1 = (bf16[128,4096]{1,0:T(8,128)(2,1)S(1)}) conditional(s32[]{:T(128)} %bitcast.6, bf16[128,4096]{1,0:T(8,128)(2,1)S(1)} %get-tuple-element.71, (bf16[512,4096]{1,0:T(8,128)(2,1)}, s32[512]{0:T(512)S(1)}, bf16[4096]{0:T(1024)(128)(2,1)S(1)}, bf16[4096,512]{1,0:T(8,128)(2,1)}, bf16[4096,512]{1,0:T(8,128)(2,1)}, ...), branch_computations={%region_0.0_spmd, %region_1.6_spmd} | conditional | flops 9168275456 | bytes 206274176 | solution.py:576
  95.7 781.0 %while.18 = (s32[]{:T(128)}, bf16[512,512]{1,0:T(8,128)(2,1)S(1)}, bf16[512,512]{1,0:T(8,128)(2,1)}, f32[4,512]{1,0:T(4,128)S(1)}, f32[4,512]{1,0:T(4,128)S(1)},...) while((s32[]{:T(128)}, bf16[512,512]{1,0:T(8,128)(2,1)S(1)}, ...), condition=%wide.region_5.0_spmd.clone, body=%wide.region_2.0_spmd.clone.sunk | while | flops 546058240 | bytes 22675640 | solution.py:526
  100.8 12.1 %collective-permute-done = bf16[512,512]{1,0:T(8,128)(2,1)S(1)} collective-permute-done((bf16[512,512]{1,0:T(8,128)(2,1)S(1)}, bf16[512,512]{1,0:T(8,128)(2,1)S(1)}, u32[]{:S(2)}, u32[]{:S(2)}) %collective-permute-start) | collective-permute-done | bytes 524320 | tf_op jit(solution)/shard_map/cond/branch_1_fun/while/body/eval_jaxpr/ppermute | solution.py:524
  113.0 11.3 %collective-permute-done.1 = bf16[512,512]{1,0:T(8,128)(2,1)} collective-permute-done((bf16[512,512]{1,0:T(8,128)(2,1)S(1)}, bf16[512,512]{1,0:T(8,128)(2,1)}, u32[]{:S(2)}, u32[]{:S(2)}) %collective-permute-start.1) | collective-permute-done | bytes 524320 | tf_op jit(solution)/shard_map/cond/branch_1_fun/while/body/eval_jaxpr/ppermute | solution.py:524
  128.4 12.0 %collective-permute-done = bf16[512,512]{1,0:T(8,128)(2,1)S(1)} collective-permute-done((bf16[512,512]{1,0:T(8,128)(2,1)S(1)}, bf16[512,512]{1,0:T(8,128)(2,1)S(1)}, u32[]{:S(2)}, u32[]{:S(2)}) %collective-permute-start) | collective-permute-done | bytes 524320 | tf_op jit(solution)/shard_map/cond/branch_1_fun/while/body/eval_jaxpr/ppermute | solution.py:524
  140.4 11.3 %collective-permute-done.1 = bf16[512,512]{1,0:T(8,128)(2,1)} collective-permute-done((bf16[512,512]{1,0:T(8,128)(2,1)S(1)}, bf16[512,512]{1,0:T(8,128)(2,1)}, u32[]{:S(2)}, u32[]{:S(2)}) %collective-permute-start.1) | collective-permute-done | bytes 524320 | tf_op jit(solution)/shard_map/cond/branch_1_fun/while/body/eval_jaxpr/ppermute | solution.py:524
  166.9 11.3 %collective-permute-done.1 = bf16[512,512]{1,0:T(8,128)(2,1)} collective-permute-done((bf16[512,512]{1,0:T(8,128)(2,1)S(1)}, bf16[512,512]{1,0:T(8,128)(2,1)}, u32[]{:S(2)}, u32[]{:S(2)}) %collective-permute-start.1) | collective-permute-done | bytes 524320 | tf_op jit(solution)/shard_map/cond/branch_1_fun/while/body/eval_jaxpr/ppermute | solution.py:524
  192.4 11.3 %collective-permute-done.1 = bf16[512,512]{1,0:T(8,128)(2,1)} collective-permute-done((bf16[512,512]{1,0:T(8,128)(2,1)S(1)}, bf16[512,512]{1,0:T(8,128)(2,1)}, u32[]{:S(2)}, u32[]{:S(2)}) %collective-permute-start.1) | collective-permute-done | bytes 524320 | tf_op jit(solution)/shard_map/cond/branch_1_fun/while/body/eval_jaxpr/ppermute | solution.py:524
  217.1 11.3 %collective-permute-done.1 = bf16[512,512]{1,0:T(8,128)(2,1)} collective-permute-done((bf16[512,512]{1,0:T(8,128)(2,1)S(1)}, bf16[512,512]{1,0:T(8,128)(2,1)}, u32[]{:S(2)}, u32[]{:S(2)}) %collective-permute-start.1) | collective-permute-done | bytes 524320 | tf_op jit(solution)/shard_map/cond/branch_1_fun/while/body/eval_jaxpr/ppermute | solution.py:524
  364.7 12.1 %collective-permute-done = bf16[512,512]{1,0:T(8,128)(2,1)S(1)} collective-permute-done((bf16[512,512]{1,0:T(8,128)(2,1)S(1)}, bf16[512,512]{1,0:T(8,128)(2,1)S(1)}, u32[]{:S(2)}, u32[]{:S(2)}) %collective-permute-start) | collective-permute-done | bytes 524320 | tf_op jit(solution)/shard_map/cond/branch_1_fun/while/body/eval_jaxpr/ppermute | solution.py:524
  386.6 13.2 %collective-permute-done = bf16[512,512]{1,0:T(8,128)(2,1)S(1)} collective-permute-done((bf16[512,512]{1,0:T(8,128)(2,1)S(1)}, bf16[512,512]{1,0:T(8,128)(2,1)S(1)}, u32[]{:S(2)}, u32[]{:S(2)}) %collective-permute-start) | collective-permute-done | bytes 524320 | tf_op jit(solution)/shard_map/cond/branch_1_fun/while/body/eval_jaxpr/ppermute | solution.py:524
  409.6 14.4 %collective-permute-done = bf16[512,512]{1,0:T(8,128)(2,1)S(1)} collective-permute-done((bf16[512,512]{1,0:T(8,128)(2,1)S(1)}, bf16[512,512]{1,0:T(8,128)(2,1)S(1)}, u32[]{:S(2)}, u32[]{:S(2)}) %collective-permute-start) | collective-permute-done | bytes 524320 | tf_op jit(solution)/shard_map/cond/branch_1_fun/while/body/eval_jaxpr/ppermute | solution.py:524
  433.6 14.4 %collective-permute-done = bf16[512,512]{1,0:T(8,128)(2,1)S(1)} collective-permute-done((bf16[512,512]{1,0:T(8,128)(2,1)S(1)}, bf16[512,512]{1,0:T(8,128)(2,1)S(1)}, u32[]{:S(2)}, u32[]{:S(2)}) %collective-permute-start) | collective-permute-done | bytes 524320 | tf_op jit(solution)/shard_map/cond/branch_1_fun/while/body/eval_jaxpr/ppermute | solution.py:524
  458.7 14.4 %collective-permute-done = bf16[512,512]{1,0:T(8,128)(2,1)S(1)} collective-permute-done((bf16[512,512]{1,0:T(8,128)(2,1)S(1)}, bf16[512,512]{1,0:T(8,128)(2,1)S(1)}, u32[]{:S(2)}, u32[]{:S(2)}) %collective-permute-start) | collective-permute-done | bytes 524320 | tf_op jit(solution)/shard_map/cond/branch_1_fun/while/body/eval_jaxpr/ppermute | solution.py:524
  484.9 14.4 %collective-permute-done = bf16[512,512]{1,0:T(8,128)(2,1)S(1)} collective-permute-done((bf16[512,512]{1,0:T(8,128)(2,1)S(1)}, bf16[512,512]{1,0:T(8,128)(2,1)S(1)}, u32[]{:S(2)}, u32[]{:S(2)}) %collective-permute-start) | collective-permute-done | bytes 524320 | tf_op jit(solution)/shard_map/cond/branch_1_fun/while/body/eval_jaxpr/ppermute | solution.py:524
  512.2 14.3 %collective-permute-done = bf16[512,512]{1,0:T(8,128)(2,1)S(1)} collective-permute-done((bf16[512,512]{1,0:T(8,128)(2,1)S(1)}, bf16[512,512]{1,0:T(8,128)(2,1)S(1)}, u32[]{:S(2)}, u32[]{:S(2)}) %collective-permute-start) | collective-permute-done | bytes 524320 | tf_op jit(solution)/shard_map/cond/branch_1_fun/while/body/eval_jaxpr/ppermute | solution.py:524
  540.6 14.0 %collective-permute-done = bf16[512,512]{1,0:T(8,128)(2,1)S(1)} collective-permute-done((bf16[512,512]{1,0:T(8,128)(2,1)S(1)}, bf16[512,512]{1,0:T(8,128)(2,1)S(1)}, u32[]{:S(2)}, u32[]{:S(2)}) %collective-permute-start) | collective-permute-done | bytes 524320 | tf_op jit(solution)/shard_map/cond/branch_1_fun/while/body/eval_jaxpr/ppermute | solution.py:524
  554.6 11.3 %collective-permute-done.1 = bf16[512,512]{1,0:T(8,128)(2,1)} collective-permute-done((bf16[512,512]{1,0:T(8,128)(2,1)S(1)}, bf16[512,512]{1,0:T(8,128)(2,1)}, u32[]{:S(2)}, u32[]{:S(2)}) %collective-permute-start.1) | collective-permute-done | bytes 524320 | tf_op jit(solution)/shard_map/cond/branch_1_fun/while/body/eval_jaxpr/ppermute | solution.py:524
  570.0 13.2 %collective-permute-done = bf16[512,512]{1,0:T(8,128)(2,1)S(1)} collective-permute-done((bf16[512,512]{1,0:T(8,128)(2,1)S(1)}, bf16[512,512]{1,0:T(8,128)(2,1)S(1)}, u32[]{:S(2)}, u32[]{:S(2)}) %collective-permute-start) | collective-permute-done | bytes 524320 | tf_op jit(solution)/shard_map/cond/branch_1_fun/while/body/eval_jaxpr/ppermute | solution.py:524
  583.1 11.3 %collective-permute-done.1 = bf16[512,512]{1,0:T(8,128)(2,1)} collective-permute-done((bf16[512,512]{1,0:T(8,128)(2,1)S(1)}, bf16[512,512]{1,0:T(8,128)(2,1)}, u32[]{:S(2)}, u32[]{:S(2)}) %collective-permute-start.1) | collective-permute-done | bytes 524320 | tf_op jit(solution)/shard_map/cond/branch_1_fun/while/body/eval_jaxpr/ppermute | solution.py:524
  598.5 12.2 %collective-permute-done = bf16[512,512]{1,0:T(8,128)(2,1)S(1)} collective-permute-done((bf16[512,512]{1,0:T(8,128)(2,1)S(1)}, bf16[512,512]{1,0:T(8,128)(2,1)S(1)}, u32[]{:S(2)}, u32[]{:S(2)}) %collective-permute-start) | collective-permute-done | bytes 524320 | tf_op jit(solution)/shard_map/cond/branch_1_fun/while/body/eval_jaxpr/ppermute | solution.py:524
  610.8 11.3 %collective-permute-done.1 = bf16[512,512]{1,0:T(8,128)(2,1)} collective-permute-done((bf16[512,512]{1,0:T(8,128)(2,1)S(1)}, bf16[512,512]{1,0:T(8,128)(2,1)}, u32[]{:S(2)}, u32[]{:S(2)}) %collective-permute-start.1) | collective-permute-done | bytes 524320 | tf_op jit(solution)/shard_map/cond/branch_1_fun/while/body/eval_jaxpr/ppermute | solution.py:524
  637.5 11.3 %collective-permute-done.1 = bf16[512,512]{1,0:T(8,128)(2,1)} collective-permute-done((bf16[512,512]{1,0:T(8,128)(2,1)S(1)}, bf16[512,512]{1,0:T(8,128)(2,1)}, u32[]{:S(2)}, u32[]{:S(2)}) %collective-permute-start.1) | collective-permute-done | bytes 524320 | tf_op jit(solution)/shard_map/cond/branch_1_fun/while/body/eval_jaxpr/ppermute | solution.py:524
  663.2 11.3 %collective-permute-done.1 = bf16[512,512]{1,0:T(8,128)(2,1)} collective-permute-done((bf16[512,512]{1,0:T(8,128)(2,1)S(1)}, bf16[512,512]{1,0:T(8,128)(2,1)}, u32[]{:S(2)}, u32[]{:S(2)}) %collective-permute-start.1) | collective-permute-done | bytes 524320 | tf_op jit(solution)/shard_map/cond/branch_1_fun/while/body/eval_jaxpr/ppermute | solution.py:524
  688.1 11.3 %collective-permute-done.1 = bf16[512,512]{1,0:T(8,128)(2,1)} collective-permute-done((bf16[512,512]{1,0:T(8,128)(2,1)S(1)}, bf16[512,512]{1,0:T(8,128)(2,1)}, u32[]{:S(2)}, u32[]{:S(2)}) %collective-permute-start.1) | collective-permute-done | bytes 524320 | tf_op jit(solution)/shard_map/cond/branch_1_fun/while/body/eval_jaxpr/ppermute | solution.py:524
  711.8 11.5 %collective-permute-done.1 = bf16[512,512]{1,0:T(8,128)(2,1)} collective-permute-done((bf16[512,512]{1,0:T(8,128)(2,1)S(1)}, bf16[512,512]{1,0:T(8,128)(2,1)}, u32[]{:S(2)}, u32[]{:S(2)}) %collective-permute-start.1) | collective-permute-done | bytes 524320 | tf_op jit(solution)/shard_map/cond/branch_1_fun/while/body/eval_jaxpr/ppermute | solution.py:524
  836.4 11.9 %collective-permute-done = bf16[512,512]{1,0:T(8,128)(2,1)S(1)} collective-permute-done((bf16[512,512]{1,0:T(8,128)(2,1)S(1)}, bf16[512,512]{1,0:T(8,128)(2,1)S(1)}, u32[]{:S(2)}, u32[]{:S(2)}) %collective-permute-start) | collective-permute-done | bytes 524320 | tf_op jit(solution)/shard_map/cond/branch_1_fun/while/body/eval_jaxpr/ppermute | solution.py:524
  858.1 13.0 %collective-permute-done = bf16[512,512]{1,0:T(8,128)(2,1)S(1)} collective-permute-done((bf16[512,512]{1,0:T(8,128)(2,1)S(1)}, bf16[512,512]{1,0:T(8,128)(2,1)S(1)}, u32[]{:S(2)}, u32[]{:S(2)}) %collective-permute-start) | collective-permute-done | bytes 524320 | tf_op jit(solution)/shard_map/cond/branch_1_fun/while/body/eval_jaxpr/ppermute | solution.py:524
  886.4 34.5 %collective-permute-start.2 = (f32[128,4096]{1,0:T(8,128)}, f32[128,4096]{1,0:T(8,128)}, u32[]{:S(2)}, u32[]{:S(2)}) collective-permute-start(f32[128,4096]{1,0:T(8,128)} %get-tuple-element.122), channel_id=1, source_target_pairs={{0,1},{1,2},{2,3},{3,0},{4,5},{5,6},{6,7},{7,4},{8,9},{9,10},{10,1... | collective-permute-start | bytes 6291464 | tf_op jit(solution)/shard_map/cond/branch_1_fun/ppermute | solution.py:536
  921.9 43.2 %collective-permute-done.2 = f32[128,4096]{1,0:T(8,128)} collective-permute-done((f32[128,4096]{1,0:T(8,128)}, f32[128,4096]{1,0:T(8,128)}, u32[]{:S(2)}, u32[]{:S(2)}) %collective-permute-start.2) | collective-permute-done | bytes 2097184 | tf_op jit(solution)/shard_map/cond/branch_1_fun/ppermute | solution.py:536
  970.7 39.9 %collective-permute-done.3 = f32[128,4096]{1,0:T(8,128)} collective-permute-done((f32[128,4096]{1,0:T(8,128)S(1)}, f32[128,4096]{1,0:T(8,128)}, u32[]{:S(2)}, u32[]{:S(2)}) %collective-permute-start.3) | collective-permute-done | bytes 2097184 | tf_op jit(solution)/shard_map/cond/branch_1_fun/ppermute | solution.py:536
  (394 shorter events, 492.2 us)
Async XLA Ops:
  97.6 26.7 %collective-permute-start.1 = (bf16[512,512]{1,0:T(8,128)(2,1)S(1)}, bf16[512,512]{1,0:T(8,128)(2,1)}, u32[]{:S(2)}, u32[]{:S(2)}) collective-permute-start(bf16[512,512]{1,0:T(8,128)(2,1)S(1)} %copy.48), channel_id=1, source_target_pairs={{0,4},{4,8},{8,12},{12,16},{16,20},{20,24},{24,28},{28,32},{32,36}... | collective-permute-start | bytes 1572872 | tf_op jit(solution)/shard_map/cond/branch_1_fun/while/body/eval_jaxpr/ppermute | solution.py:524
  125.5 26.2 %collective-permute-start.1 = (bf16[512,512]{1,0:T(8,128)(2,1)S(1)}, bf16[512,512]{1,0:T(8,128)(2,1)}, u32[]{:S(2)}, u32[]{:S(2)}) collective-permute-start(bf16[512,512]{1,0:T(8,128)(2,1)S(1)} %copy.48), channel_id=1, source_target_pairs={{0,4},{4,8},{8,12},{12,16},{16,20},{20,24},{24,28},{28,32},{32,36}... | collective-permute-start | bytes 1572872 | tf_op jit(solution)/shard_map/cond/branch_1_fun/while/body/eval_jaxpr/ppermute | solution.py:524
  152.9 25.3 %collective-permute-start.1 = (bf16[512,512]{1,0:T(8,128)(2,1)S(1)}, bf16[512,512]{1,0:T(8,128)(2,1)}, u32[]{:S(2)}, u32[]{:S(2)}) collective-permute-start(bf16[512,512]{1,0:T(8,128)(2,1)S(1)} %copy.48), channel_id=1, source_target_pairs={{0,4},{4,8},{8,12},{12,16},{16,20},{20,24},{24,28},{28,32},{32,36}... | collective-permute-start | bytes 1572872 | tf_op jit(solution)/shard_map/cond/branch_1_fun/while/body/eval_jaxpr/ppermute | solution.py:524
  179.4 24.4 %collective-permute-start.1 = (bf16[512,512]{1,0:T(8,128)(2,1)S(1)}, bf16[512,512]{1,0:T(8,128)(2,1)}, u32[]{:S(2)}, u32[]{:S(2)}) collective-permute-start(bf16[512,512]{1,0:T(8,128)(2,1)S(1)} %copy.48), channel_id=1, source_target_pairs={{0,4},{4,8},{8,12},{12,16},{16,20},{20,24},{24,28},{28,32},{32,36}... | collective-permute-start | bytes 1572872 | tf_op jit(solution)/shard_map/cond/branch_1_fun/while/body/eval_jaxpr/ppermute | solution.py:524
  204.9 23.5 %collective-permute-start.1 = (bf16[512,512]{1,0:T(8,128)(2,1)S(1)}, bf16[512,512]{1,0:T(8,128)(2,1)}, u32[]{:S(2)}, u32[]{:S(2)}) collective-permute-start(bf16[512,512]{1,0:T(8,128)(2,1)S(1)} %copy.48), channel_id=1, source_target_pairs={{0,4},{4,8},{8,12},{12,16},{16,20},{20,24},{24,28},{28,32},{32,36}... | collective-permute-start | bytes 1572872 | tf_op jit(solution)/shard_map/cond/branch_1_fun/while/body/eval_jaxpr/ppermute | solution.py:524
  229.6 22.4 %collective-permute-start.1 = (bf16[512,512]{1,0:T(8,128)(2,1)S(1)}, bf16[512,512]{1,0:T(8,128)(2,1)}, u32[]{:S(2)}, u32[]{:S(2)}) collective-permute-start(bf16[512,512]{1,0:T(8,128)(2,1)S(1)} %copy.48), channel_id=1, source_target_pairs={{0,4},{4,8},{8,12},{12,16},{16,20},{20,24},{24,28},{28,32},{32,36}... | collective-permute-start | bytes 1572872 | tf_op jit(solution)/shard_map/cond/branch_1_fun/while/body/eval_jaxpr/ppermute | solution.py:524
  253.2 21.4 %collective-permute-start.1 = (bf16[512,512]{1,0:T(8,128)(2,1)S(1)}, bf16[512,512]{1,0:T(8,128)(2,1)}, u32[]{:S(2)}, u32[]{:S(2)}) collective-permute-start(bf16[512,512]{1,0:T(8,128)(2,1)S(1)} %copy.48), channel_id=1, source_target_pairs={{0,4},{4,8},{8,12},{12,16},{16,20},{20,24},{24,28},{28,32},{32,36}... | collective-permute-start | bytes 1572872 | tf_op jit(solution)/shard_map/cond/branch_1_fun/while/body/eval_jaxpr/ppermute | solution.py:524
  275.8 20.4 %collective-permute-start.1 = (bf16[512,512]{1,0:T(8,128)(2,1)S(1)}, bf16[512,512]{1,0:T(8,128)(2,1)}, u32[]{:S(2)}, u32[]{:S(2)}) collective-permute-start(bf16[512,512]{1,0:T(8,128)(2,1)S(1)} %copy.48), channel_id=1, source_target_pairs={{0,4},{4,8},{8,12},{12,16},{16,20},{20,24},{24,28},{28,32},{32,36}... | collective-permute-start | bytes 1572872 | tf_op jit(solution)/shard_map/cond/branch_1_fun/while/body/eval_jaxpr/ppermute | solution.py:524
  297.3 20.3 %collective-permute-start.1 = (bf16[512,512]{1,0:T(8,128)(2,1)S(1)}, bf16[512,512]{1,0:T(8,128)(2,1)}, u32[]{:S(2)}, u32[]{:S(2)}) collective-permute-start(bf16[512,512]{1,0:T(8,128)(2,1)S(1)} %copy.48), channel_id=1, source_target_pairs={{0,4},{4,8},{8,12},{12,16},{16,20},{20,24},{24,28},{28,32},{32,36}... | collective-permute-start | bytes 1572872 | tf_op jit(solution)/shard_map/cond/branch_1_fun/while/body/eval_jaxpr/ppermute | solution.py:524
  340.3 20.3 %collective-permute-start.1 = (bf16[512,512]{1,0:T(8,128)(2,1)S(1)}, bf16[512,512]{1,0:T(8,128)(2,1)}, u32[]{:S(2)}, u32[]{:S(2)}) collective-permute-start(bf16[512,512]{1,0:T(8,128)(2,1)S(1)} %copy.48), channel_id=1, source_target_pairs={{0,4},{4,8},{8,12},{12,16},{16,20},{20,24},{24,28},{28,32},{32,36}... | collective-permute-start | bytes 1572872 | tf_op jit(solution)/shard_map/cond/branch_1_fun/while/body/eval_jaxpr/ppermute | solution.py:524
  361.9 20.7 %collective-permute-start.1 = (bf16[512,512]{1,0:T(8,128)(2,1)S(1)}, bf16[512,512]{1,0:T(8,128)(2,1)}, u32[]{:S(2)}, u32[]{:S(2)}) collective-permute-start(bf16[512,512]{1,0:T(8,128)(2,1)S(1)} %copy.48), channel_id=1, source_target_pairs={{0,4},{4,8},{8,12},{12,16},{16,20},{20,24},{24,28},{28,32},{32,36}... | collective-permute-start | bytes 1572872 | tf_op jit(solution)/shard_map/cond/branch_1_fun/while/body/eval_jaxpr/ppermute | solution.py:524
  383.7 21.8 %collective-permute-start.1 = (bf16[512,512]{1,0:T(8,128)(2,1)S(1)}, bf16[512,512]{1,0:T(8,128)(2,1)}, u32[]{:S(2)}, u32[]{:S(2)}) collective-permute-start(bf16[512,512]{1,0:T(8,128)(2,1)S(1)} %copy.48), channel_id=1, source_target_pairs={{0,4},{4,8},{8,12},{12,16},{16,20},{20,24},{24,28},{28,32},{32,36}... | collective-permute-start | bytes 1572872 | tf_op jit(solution)/shard_map/cond/branch_1_fun/while/body/eval_jaxpr/ppermute | solution.py:524
  406.7 22.9 %collective-permute-start.1 = (bf16[512,512]{1,0:T(8,128)(2,1)S(1)}, bf16[512,512]{1,0:T(8,128)(2,1)}, u32[]{:S(2)}, u32[]{:S(2)}) collective-permute-start(bf16[512,512]{1,0:T(8,128)(2,1)S(1)} %copy.48), channel_id=1, source_target_pairs={{0,4},{4,8},{8,12},{12,16},{16,20},{20,24},{24,28},{28,32},{32,36}... | collective-permute-start | bytes 1572872 | tf_op jit(solution)/shard_map/cond/branch_1_fun/while/body/eval_jaxpr/ppermute | solution.py:524
  430.7 24.0 %collective-permute-start.1 = (bf16[512,512]{1,0:T(8,128)(2,1)S(1)}, bf16[512,512]{1,0:T(8,128)(2,1)}, u32[]{:S(2)}, u32[]{:S(2)}) collective-permute-start(bf16[512,512]{1,0:T(8,128)(2,1)S(1)} %copy.48), channel_id=1, source_target_pairs={{0,4},{4,8},{8,12},{12,16},{16,20},{20,24},{24,28},{28,32},{32,36}... | collective-permute-start | bytes 1572872 | tf_op jit(solution)/shard_map/cond/branch_1_fun/while/body/eval_jaxpr/ppermute | solution.py:524
  455.8 25.0 %collective-permute-start.1 = (bf16[512,512]{1,0:T(8,128)(2,1)S(1)}, bf16[512,512]{1,0:T(8,128)(2,1)}, u32[]{:S(2)}, u32[]{:S(2)}) collective-permute-start(bf16[512,512]{1,0:T(8,128)(2,1)S(1)} %copy.48), channel_id=1, source_target_pairs={{0,4},{4,8},{8,12},{12,16},{16,20},{20,24},{24,28},{28,32},{32,36}... | collective-permute-start | bytes 1572872 | tf_op jit(solution)/shard_map/cond/branch_1_fun/while/body/eval_jaxpr/ppermute | solution.py:524
  482.0 26.1 %collective-permute-start.1 = (bf16[512,512]{1,0:T(8,128)(2,1)S(1)}, bf16[512,512]{1,0:T(8,128)(2,1)}, u32[]{:S(2)}, u32[]{:S(2)}) collective-permute-start(bf16[512,512]{1,0:T(8,128)(2,1)S(1)} %copy.48), channel_id=1, source_target_pairs={{0,4},{4,8},{8,12},{12,16},{16,20},{20,24},{24,28},{28,32},{32,36}... | collective-permute-start | bytes 1572872 | tf_op jit(solution)/shard_map/cond/branch_1_fun/while/body/eval_jaxpr/ppermute | solution.py:524
  509.3 27.2 %collective-permute-start.1 = (bf16[512,512]{1,0:T(8,128)(2,1)S(1)}, bf16[512,512]{1,0:T(8,128)(2,1)}, u32[]{:S(2)}, u32[]{:S(2)}) collective-permute-start(bf16[512,512]{1,0:T(8,128)(2,1)S(1)} %copy.48), channel_id=1, source_target_pairs={{0,4},{4,8},{8,12},{12,16},{16,20},{20,24},{24,28},{28,32},{32,36}... | collective-permute-start | bytes 1572872 | tf_op jit(solution)/shard_map/cond/branch_1_fun/while/body/eval_jaxpr/ppermute | solution.py:524
  537.7 28.2 %collective-permute-start.1 = (bf16[512,512]{1,0:T(8,128)(2,1)S(1)}, bf16[512,512]{1,0:T(8,128)(2,1)}, u32[]{:S(2)}, u32[]{:S(2)}) collective-permute-start(bf16[512,512]{1,0:T(8,128)(2,1)S(1)} %copy.48), channel_id=1, source_target_pairs={{0,4},{4,8},{8,12},{12,16},{16,20},{20,24},{24,28},{28,32},{32,36}... | collective-permute-start | bytes 1572872 | tf_op jit(solution)/shard_map/cond/branch_1_fun/while/body/eval_jaxpr/ppermute | solution.py:524
  567.1 27.4 %collective-permute-start.1 = (bf16[512,512]{1,0:T(8,128)(2,1)S(1)}, bf16[512,512]{1,0:T(8,128)(2,1)}, u32[]{:S(2)}, u32[]{:S(2)}) collective-permute-start(bf16[512,512]{1,0:T(8,128)(2,1)S(1)} %copy.48), channel_id=1, source_target_pairs={{0,4},{4,8},{8,12},{12,16},{16,20},{20,24},{24,28},{28,32},{32,36}... | collective-permute-start | bytes 1572872 | tf_op jit(solution)/shard_map/cond/branch_1_fun/while/body/eval_jaxpr/ppermute | solution.py:524
  595.6 26.5 %collective-permute-start.1 = (bf16[512,512]{1,0:T(8,128)(2,1)S(1)}, bf16[512,512]{1,0:T(8,128)(2,1)}, u32[]{:S(2)}, u32[]{:S(2)}) collective-permute-start(bf16[512,512]{1,0:T(8,128)(2,1)S(1)} %copy.48), channel_id=1, source_target_pairs={{0,4},{4,8},{8,12},{12,16},{16,20},{20,24},{24,28},{28,32},{32,36}... | collective-permute-start | bytes 1572872 | tf_op jit(solution)/shard_map/cond/branch_1_fun/while/body/eval_jaxpr/ppermute | solution.py:524
  623.3 25.5 %collective-permute-start.1 = (bf16[512,512]{1,0:T(8,128)(2,1)S(1)}, bf16[512,512]{1,0:T(8,128)(2,1)}, u32[]{:S(2)}, u32[]{:S(2)}) collective-permute-start(bf16[512,512]{1,0:T(8,128)(2,1)S(1)} %copy.48), channel_id=1, source_target_pairs={{0,4},{4,8},{8,12},{12,16},{16,20},{20,24},{24,28},{28,32},{32,36}... | collective-permute-start | bytes 1572872 | tf_op jit(solution)/shard_map/cond/branch_1_fun/while/body/eval_jaxpr/ppermute | solution.py:524
  650.0 24.6 %collective-permute-start.1 = (bf16[512,512]{1,0:T(8,128)(2,1)S(1)}, bf16[512,512]{1,0:T(8,128)(2,1)}, u32[]{:S(2)}, u32[]{:S(2)}) collective-permute-start(bf16[512,512]{1,0:T(8,128)(2,1)S(1)} %copy.48), channel_id=1, source_target_pairs={{0,4},{4,8},{8,12},{12,16},{16,20},{20,24},{24,28},{28,32},{32,36}... | collective-permute-start | bytes 1572872 | tf_op jit(solution)/shard_map/cond/branch_1_fun/while/body/eval_jaxpr/ppermute | solution.py:524
  675.7 23.7 %collective-permute-start.1 = (bf16[512,512]{1,0:T(8,128)(2,1)S(1)}, bf16[512,512]{1,0:T(8,128)(2,1)}, u32[]{:S(2)}, u32[]{:S(2)}) collective-permute-start(bf16[512,512]{1,0:T(8,128)(2,1)S(1)} %copy.48), channel_id=1, source_target_pairs={{0,4},{4,8},{8,12},{12,16},{16,20},{20,24},{24,28},{28,32},{32,36}... | collective-permute-start | bytes 1572872 | tf_op jit(solution)/shard_map/cond/branch_1_fun/while/body/eval_jaxpr/ppermute | solution.py:524
  700.6 22.7 %collective-permute-start.1 = (bf16[512,512]{1,0:T(8,128)(2,1)S(1)}, bf16[512,512]{1,0:T(8,128)(2,1)}, u32[]{:S(2)}, u32[]{:S(2)}) collective-permute-start(bf16[512,512]{1,0:T(8,128)(2,1)S(1)} %copy.48), channel_id=1, source_target_pairs={{0,4},{4,8},{8,12},{12,16},{16,20},{20,24},{24,28},{28,32},{32,36}... | collective-permute-start | bytes 1572872 | tf_op jit(solution)/shard_map/cond/branch_1_fun/while/body/eval_jaxpr/ppermute | solution.py:524
  724.4 21.6 %collective-permute-start.1 = (bf16[512,512]{1,0:T(8,128)(2,1)S(1)}, bf16[512,512]{1,0:T(8,128)(2,1)}, u32[]{:S(2)}, u32[]{:S(2)}) collective-permute-start(bf16[512,512]{1,0:T(8,128)(2,1)S(1)} %copy.48), channel_id=1, source_target_pairs={{0,4},{4,8},{8,12},{12,16},{16,20},{20,24},{24,28},{28,32},{32,36}... | collective-permute-start | bytes 1572872 | tf_op jit(solution)/shard_map/cond/branch_1_fun/while/body/eval_jaxpr/ppermute | solution.py:524
  747.2 20.6 %collective-permute-start.1 = (bf16[512,512]{1,0:T(8,128)(2,1)S(1)}, bf16[512,512]{1,0:T(8,128)(2,1)}, u32[]{:S(2)}, u32[]{:S(2)}) collective-permute-start(bf16[512,512]{1,0:T(8,128)(2,1)S(1)} %copy.48), channel_id=1, source_target_pairs={{0,4},{4,8},{8,12},{12,16},{16,20},{20,24},{24,28},{28,32},{32,36}... | collective-permute-start | bytes 1572872 | tf_op jit(solution)/shard_map/cond/branch_1_fun/while/body/eval_jaxpr/ppermute | solution.py:524
  769.0 20.3 %collective-permute-start.1 = (bf16[512,512]{1,0:T(8,128)(2,1)S(1)}, bf16[512,512]{1,0:T(8,128)(2,1)}, u32[]{:S(2)}, u32[]{:S(2)}) collective-permute-start(bf16[512,512]{1,0:T(8,128)(2,1)S(1)} %copy.48), channel_id=1, source_target_pairs={{0,4},{4,8},{8,12},{12,16},{16,20},{20,24},{24,28},{28,32},{32,36}... | collective-permute-start | bytes 1572872 | tf_op jit(solution)/shard_map/cond/branch_1_fun/while/body/eval_jaxpr/ppermute | solution.py:524
  833.6 20.5 %collective-permute-start.1 = (bf16[512,512]{1,0:T(8,128)(2,1)S(1)}, bf16[512,512]{1,0:T(8,128)(2,1)}, u32[]{:S(2)}, u32[]{:S(2)}) collective-permute-start(bf16[512,512]{1,0:T(8,128)(2,1)S(1)} %copy.48), channel_id=1, source_target_pairs={{0,4},{4,8},{8,12},{12,16},{16,20},{20,24},{24,28},{28,32},{32,36}... | collective-permute-start | bytes 1572872 | tf_op jit(solution)/shard_map/cond/branch_1_fun/while/body/eval_jaxpr/ppermute | solution.py:524
  855.2 21.6 %collective-permute-start.1 = (bf16[512,512]{1,0:T(8,128)(2,1)S(1)}, bf16[512,512]{1,0:T(8,128)(2,1)}, u32[]{:S(2)}, u32[]{:S(2)}) collective-permute-start(bf16[512,512]{1,0:T(8,128)(2,1)S(1)} %copy.48), channel_id=1, source_target_pairs={{0,4},{4,8},{8,12},{12,16},{16,20},{20,24},{24,28},{28,32},{32,36}... | collective-permute-start | bytes 1572872 | tf_op jit(solution)/shard_map/cond/branch_1_fun/while/body/eval_jaxpr/ppermute | solution.py:524
  886.4 78.7 %collective-permute-start.2 = (f32[128,4096]{1,0:T(8,128)}, f32[128,4096]{1,0:T(8,128)}, u32[]{:S(2)}, u32[]{:S(2)}) collective-permute-start(f32[128,4096]{1,0:T(8,128)} %get-tuple-element.122), channel_id=1, source_target_pairs={{0,1},{1,2},{2,3},{3,0},{4,5},{5,6},{6,7},{7,4},{8,9},{9,10},{10,1... | collective-permute-start | bytes 6291464 | tf_op jit(solution)/shard_map/cond/branch_1_fun/ppermute | solution.py:536
  920.9 49.8 %collective-permute-start.4 = (f32[128,4096]{1,0:T(8,128)}, f32[128,4096]{1,0:T(8,128)}, u32[]{:S(2)}, u32[]{:S(2)}) collective-permute-start(f32[128,4096]{1,0:T(8,128)} %get-tuple-element.123), channel_id=1, source_target_pairs={{0,3},{1,0},{2,1},{3,2},{4,7},{5,4},{6,5},{7,6},{8,11},{9,8},{10,9... | collective-permute-start | bytes 6291464 | tf_op jit(solution)/shard_map/cond/branch_1_fun/ppermute | solution.py:536
  920.9 89.7 %collective-permute-start.3 = (f32[128,4096]{1,0:T(8,128)S(1)}, f32[128,4096]{1,0:T(8,128)}, u32[]{:S(2)}, u32[]{:S(2)}) collective-permute-start(f32[128,4096]{1,0:T(8,128)S(1)} %get-tuple-element.124), channel_id=1, source_target_pairs={{0,2},{1,3},{2,0},{3,1},{4,6},{5,7},{6,4},{7,5},{8,10},{9,11},{10,... | collective-permute-start | bytes 6291464 | tf_op jit(solution)/shard_map/cond/branch_1_fun/ppermute | solution.py:536
  (41 other events, 732.2 us)

commit v4 on v3

--- a/solution.py
+++ b/solution.py
@@ -24,7 +24,9 @@
 )
 OWN = {(dx, e): n for n, (by, dx, e) in enumerate(USE) if by == "own"}
 SIB = {(dx, e): n for n, (by, dx, e) in enumerate(USE) if by == "sib"}
-EARLY = {2: ((2, 0), (0, 1)), 4: ((0, 3),), 7: ((0, 2),), 9: ((2, 1),), 13: ((2, 3),)}
+EARLY = {
+    2: ((2, 0, None), (0, 1, None)), 4: ((0, 3, None),), 7: ((0, 2, None),), 9: ((2, 1, None),), 13: ((2, 3, None),),
+}
 OWN_OF = {slot: key for key, slot in OWN.items()}
 
 ORDER = (("kv", 0), ("q", 0), ("q", 1), ("kv", 1), ("kv", 3), ("kv", 2))
@@ -46,6 +48,10 @@
 
 def seq_of(y_lo, x, z):
     return y_lo * 16 + x * 4 + z
+
+
+def block_order(n):
+    return (2 + 3 * n + 3 * (n // 2) + 2 * (n // 3)) % 4
 
 
 def remote(src, dst, send_sem, recv_sem, seq, head):
@@ -137,14 +143,6 @@
 
     lax.fori_loop(0, rows_here // 64, angle_rows, 0)
 
-    @pl.when(straight)
-    def _():
-        pl.semaphore_wait(barrier, 38)
-
-    @pl.when(jnp.logical_not(straight))
-    def _():
-        pl.semaphore_wait(barrier, 40)
-
     def w_chunk(colour_y, colour_z, q):
         base = (colour_y * 2 + colour_z) * 128 + 32 * (q % 4)
         return pl.ds(pl.multiple_of(base, 32), 32)
@@ -194,8 +192,6 @@
         w_z(q, w_rows(q, z_par=1 - z % 2)).wait_recv()
         w_sib(8 + q).start()
 
-    for n in range(len(CROSS)):
-        w_cross(n).start()
     own_w = pltpu.make_async_copy(wo_hbm, w_full.at[head], load_sem.at[7])
 
     flag_cols = jnp.broadcast_to(flags_ref[...].astype(F32), (DH, rows_here)).T
@@ -225,25 +221,18 @@
     def among(n, picks):
         return functools.reduce(jnp.logical_or, [n == p for p in picks])
 
-    sends = []
+    crooked = jnp.logical_not(straight)
+    sends = {}
 
     def forward(slot, to_slot, s, h, only=None):
-        def copy():
-            return remote(kvb.at[slot], kvb.at[to_slot], f_send.at[n_send], kv_recv.at[to_slot], s, h)
-        n_send = len(sends)
-        sends.append((copy, only))
+        n_send = sends.setdefault((slot, to_slot), (len(sends), s, h, only))[0]
+        copy = remote(kvb.at[slot], kvb.at[to_slot], f_send.at[n_send], kv_recv.at[to_slot], s, h)
         if only is None:
-            copy().start()
+            copy.start()
         else:
-            pl.when(only)(copy().start)
-
-    crooked = jnp.logical_not(straight)
-    taken = set()
-
-    def arrived(slot):
-        if slot in taken:
-            return
-        taken.add(slot)
+            pl.when(only)(copy.start)
+
+    def take_up(slot):
         remote(kvb.at[slot], kvb.at[slot], f_send.at[0], kv_recv.at[slot], seq, sib).wait_recv()
         if slot not in OWN_OF:
             return
@@ -257,6 +246,19 @@
             forward(slot, OWN[2, d], x_down, head, crooked if d in (0, 3) else straight)
         forward(slot, SIB[dx, d], seq, sib)
 
+    taken = set()
+
+    def arrived(slot, kind=None):
+        if slot in taken:
+            return
+        if kind is None:
+            taken.add(slot)
+            take_up(slot)
+        else:
+            if kind == "crooked":
+                taken.add(slot)
+            pl.when(straight if kind == "straight" else crooked)(functools.partial(take_up, slot))
+
     score_scale = DH ** -0.5 * math.log2(math.e)
     q_steps = [n for n, (kind, _) in enumerate(ORDER) if kind == "q"]
     kv_steps = {e: n for n, (kind, e) in enumerate(ORDER) if kind == "kv"}
@@ -265,9 +267,23 @@
         pltpu.make_async_copy(wq_hbm.at[:, pl.ds(0, 256)], w_v.at[n], load_sem.at[n]).wait()
         pacc[...] = jnp.dot(tok_v[...], w_v[n], preferred_element_type=F32)
 
+        @pl.when(n == 0)
+        def _():
+            @pl.when(straight)
+            def _():
+                pl.semaphore_wait(barrier, 38)
+
+            @pl.when(jnp.logical_not(straight))
+            def _():
+                pl.semaphore_wait(barrier, 40)
+
+            for k in range(len(CROSS)):
+                w_cross(k).start()
+
         @pl.when(jnp.logical_or(jnp.logical_and(straight, n == 1), jnp.logical_and(crooked, n == 3)))
         def _():
-            arrived(OWN[0, 0])
+            taken.add(OWN[0, 0])
+            take_up(OWN[0, 0])
 
         def rows(e):
             cols = slice(e * DH, (e + 1) * DH)
@@ -291,7 +307,7 @@
             stkv[m, 0] = rope(rows(0)).astype(BF16)
             stkv[m, 1] = turned_blocks(rows(1).astype(BF16))
 
-            @pl.when(high == 0)
+            @pl.when(jnp.logical_or(high == 0, straight))
             def _():
                 launch(*kv_piece(high, low, i), i)
         return 0
@@ -305,14 +321,14 @@
     for j in range(4):
         remote(qb.at[j], qb.at[j], q_send.at[0], q_recv.at[j], seq, sib).wait_recv()
     own_w.start()
-    kv_piece(1, 1, swapped(3))[0].start()
+    pl.when(crooked)(kv_piece(1, 1, swapped(3))[0].start)
     blocks = qb.shape[0]
 
     def take(k):
         if k == 1:
-            kv_piece(1, 0, swapped(2))[0].start()
-        for key in EARLY.get(k, ()):
-            arrived(OWN[key])
+            pl.when(crooked)(kv_piece(1, 0, swapped(2))[0].start)
+        for dx, e, kind in EARLY.get(k, ()):
+            arrived(OWN[dx, e], kind)
         arrived(2 * k)
         arrived(2 * k + 1)
         for action, n in EXTRA.get(k, ()):
@@ -362,7 +378,7 @@
         return functools.reduce(jnp.logical_and, (straight, zz == z, y_hi == hi, core == c))
 
     def last(n, _):
-        zz = (z + 1 + n) % 4
+        zz = (z + block_order(n)) % 4
         cols = pl.ds(pl.multiple_of(zz * 512, 512), 512)
         pairs = [chunk_pair(t) for t in range(LAST, 16)]
         now = scores(pairs[0][0], zz)
@@ -413,7 +429,7 @@
         w_sib(n).wait_recv()
 
     def project_out(n, _):
-        zz = (z + 3 - n) % 4
+        zz = (z + 4 - block_order(n)) % 4
         for hi in range(4):
             remote(full.at[hi * 4 + zz], full.at[hi * 4 + zz], o_send.at[0], o_recv.at[hi * 4 + zz], seq, sib).wait_recv()
         attention = jnp.concatenate([full[hi * 4 + zz] for hi in range(4)], axis=1)
@@ -460,11 +476,12 @@
                 there.wait_send()
             else:
                 pl.when(jnp.logical_not(alone))(there.wait_send)
-    for copy, only in sends:
+    for (slot, to_slot), (n, s, h, only) in sends.items():
+        copy = remote(kvb.at[slot], kvb.at[to_slot], f_send.at[n], kv_recv.at[to_slot], s, h)
         if only is None:
-            copy().wait_send()
+            copy.wait_send()
         else:
-            pl.when(only)(copy().wait_send)
+            pl.when(only)(copy.wait_send)
 
 
 def rotate(values, positions, head_size):

time: 1020 us -> 1020 us (level)
  no operation moved by 1% of the time
where the time goes in v4:
time: 1020 us; the launch traced here: 1010 us
  waiting for transfers between devices  739 us (72%)
  matrix products  84.2 us (8%)
  Pallas kernels  78.5 us (8%)
  local copies, waits for them, and re-layouts  40.8 us (4%)
  starting transfers between devices  39.5 us (4%)
  other arithmetic  28.7 us (3%)
    ppermute x32, waiting for transfers between devices, add_part(): lax.ppermute(keys, 'seq', ring)  356 us
    ppermute x32, waiting for transfers between devices, add_part(): lax.ppermute(values, 'seq', ring)  294 us
    ppermute x3, waiting for transfers between devices, plain_shards(): lax.ppermute(leaving, 'head', [(m, (m + n) % heads) for m in range(heads)])  88.6 us
    pallas_call x1, Pallas kernels, shards(): pl.pallas_call(attend_kernel, out_shape=(struct((rows // 4, width), BF16)...  78.5 us
    dot_general x32, matrix products, add_part(): jnp.einsum('hqk,khd->qhd', weights.astype(jnp.bfloat16), values.reshape(q...  44.6 us
    ppermute x3, starting transfers between devices, plain_shards(): lax.ppermute(leaving, 'head', [(m, (m + n) % heads) for m in range(heads)])  35.3 us
    while x96, local copies, waits for them, and re-layouts  34.6 us
    dot_general x32, matrix products, add_part(): jnp.einsum('qhd,khd->hqk', queries, keys.reshape(queries.shape), preferre...  23 us
  transfers between devices with their start and end apart: 67, of which 67 were waited for; matrix products, arithmetic and copies ran while one was open for 12% of the time, Pallas kernels for 0%

profile of v4, /device:TPU:1, one launch (start us, length us, event | category | flops | bytes accessed | tf_op | source)
XLA Modules:
  0.0 1013.6 jit_solution(3071158804707900239)
XLA Ops:
  0.0 78.5 %attend.1 = (bf16[128,4096]{1,0:T(8,128)(2,1)S(1)}, f32[1,1]{1,0:T(1,128)}) custom-call(bf16[512,4096]{1,0:T(8,128)(2,1)} %tok_hbm.1, s32[1,512]{1,0:T(1,128)} %bitcast.54, bf16[4096]{0:T(1024)(128)(2,1)} %embed_ref.1, bf16[4096,512]{1,0:T(8,128)(2,1)} %wq_hbm.1, bf16[4096,512]{1,0:T(8,128)(2,1)} %wk_hbm.1, bf16[4096,512]{1,0:T(8,128)(2,1)} %wv_hbm.1, ...), custom_call_target="tpu_custom_call" | custom-call | tf_op jit(solution)/shard_map/attend/pallas_call | solution.py:562
  79.1 933.5 %conditional.1 = (bf16[128,4096]{1,0:T(8,128)(2,1)S(1)}) conditional(s32[]{:T(128)} %bitcast.6, bf16[128,4096]{1,0:T(8,128)(2,1)S(1)} %get-tuple-element.71, (bf16[512,4096]{1,0:T(8,128)(2,1)}, s32[512]{0:T(512)S(1)}, bf16[4096]{0:T(1024)(128)(2,1)S(1)}, bf16[4096,512]{1,0:T(8,128)(2,1)}, bf16[4096,512]{1,0:T(8,128)(2,1)}, ...), branch_computations={%region_0.0_spmd, %region_1.6_spmd} | conditional | flops 9168275456 | bytes 206274176 | solution.py:593
  92.9 782.0 %while.18 = (s32[]{:T(128)}, bf16[512,512]{1,0:T(8,128)(2,1)S(1)}, bf16[512,512]{1,0:T(8,128)(2,1)}, f32[4,512]{1,0:T(4,128)S(1)}, f32[4,512]{1,0:T(4,128)S(1)},...) while((s32[]{:T(128)}, bf16[512,512]{1,0:T(8,128)(2,1)S(1)}, ...), condition=%wide.region_5.0_spmd.clone, body=%wide.region_2.0_spmd.clone.sunk | while | flops 546058240 | bytes 22675640 | solution.py:543
  110.3 11.3 %collective-permute-done.1 = bf16[512,512]{1,0:T(8,128)(2,1)} collective-permute-done((bf16[512,512]{1,0:T(8,128)(2,1)S(1)}, bf16[512,512]{1,0:T(8,128)(2,1)}, u32[]{:S(2)}, u32[]{:S(2)}) %collective-permute-start.1) | collective-permute-done | bytes 524320 | tf_op jit(solution)/shard_map/cond/branch_1_fun/while/body/eval_jaxpr/ppermute | solution.py:541
  125.7 12.1 %collective-permute-done = bf16[512,512]{1,0:T(8,128)(2,1)S(1)} collective-permute-done((bf16[512,512]{1,0:T(8,128)(2,1)S(1)}, bf16[512,512]{1,0:T(8,128)(2,1)S(1)}, u32[]{:S(2)}, u32[]{:S(2)}) %collective-permute-start) | collective-permute-done | bytes 524320 | tf_op jit(solution)/shard_map/cond/branch_1_fun/while/body/eval_jaxpr/ppermute | solution.py:541
  137.7 11.3 %collective-permute-done.1 = bf16[512,512]{1,0:T(8,128)(2,1)} collective-permute-done((bf16[512,512]{1,0:T(8,128)(2,1)S(1)}, bf16[512,512]{1,0:T(8,128)(2,1)}, u32[]{:S(2)}, u32[]{:S(2)}) %collective-permute-start.1) | collective-permute-done | bytes 524320 | tf_op jit(solution)/shard_map/cond/branch_1_fun/while/body/eval_jaxpr/ppermute | solution.py:541
  164.3 11.3 %collective-permute-done.1 = bf16[512,512]{1,0:T(8,128)(2,1)} collective-permute-done((bf16[512,512]{1,0:T(8,128)(2,1)S(1)}, bf16[512,512]{1,0:T(8,128)(2,1)}, u32[]{:S(2)}, u32[]{:S(2)}) %collective-permute-start.1) | collective-permute-done | bytes 524320 | tf_op jit(solution)/shard_map/cond/branch_1_fun/while/body/eval_jaxpr/ppermute | solution.py:541
  190.0 11.3 %collective-permute-done.1 = bf16[512,512]{1,0:T(8,128)(2,1)} collective-permute-done((bf16[512,512]{1,0:T(8,128)(2,1)S(1)}, bf16[512,512]{1,0:T(8,128)(2,1)}, u32[]{:S(2)}, u32[]{:S(2)}) %collective-permute-start.1) | collective-permute-done | bytes 524320 | tf_op jit(solution)/shard_map/cond/branch_1_fun/while/body/eval_jaxpr/ppermute | solution.py:541
  214.7 11.3 %collective-permute-done.1 = bf16[512,512]{1,0:T(8,128)(2,1)} collective-permute-done((bf16[512,512]{1,0:T(8,128)(2,1)S(1)}, bf16[512,512]{1,0:T(8,128)(2,1)}, u32[]{:S(2)}, u32[]{:S(2)}) %collective-permute-start.1) | collective-permute-done | bytes 524320 | tf_op jit(solution)/shard_map/cond/branch_1_fun/while/body/eval_jaxpr/ppermute | solution.py:541
  362.6 12.0 %collective-permute-done = bf16[512,512]{1,0:T(8,128)(2,1)S(1)} collective-permute-done((bf16[512,512]{1,0:T(8,128)(2,1)S(1)}, bf16[512,512]{1,0:T(8,128)(2,1)S(1)}, u32[]{:S(2)}, u32[]{:S(2)}) %collective-permute-start) | collective-permute-done | bytes 524320 | tf_op jit(solution)/shard_map/cond/branch_1_fun/while/body/eval_jaxpr/ppermute | solution.py:541
  384.4 13.1 %collective-permute-done = bf16[512,512]{1,0:T(8,128)(2,1)S(1)} collective-permute-done((bf16[512,512]{1,0:T(8,128)(2,1)S(1)}, bf16[512,512]{1,0:T(8,128)(2,1)S(1)}, u32[]{:S(2)}, u32[]{:S(2)}) %collective-permute-start) | collective-permute-done | bytes 524320 | tf_op jit(solution)/shard_map/cond/branch_1_fun/while/body/eval_jaxpr/ppermute | solution.py:541
  407.3 14.4 %collective-permute-done = bf16[512,512]{1,0:T(8,128)(2,1)S(1)} collective-permute-done((bf16[512,512]{1,0:T(8,128)(2,1)S(1)}, bf16[512,512]{1,0:T(8,128)(2,1)S(1)}, u32[]{:S(2)}, u32[]{:S(2)}) %collective-permute-start) | collective-permute-done | bytes 524320 | tf_op jit(solution)/shard_map/cond/branch_1_fun/while/body/eval_jaxpr/ppermute | solution.py:541
  431.2 14.4 %collective-permute-done = bf16[512,512]{1,0:T(8,128)(2,1)S(1)} collective-permute-done((bf16[512,512]{1,0:T(8,128)(2,1)S(1)}, bf16[512,512]{1,0:T(8,128)(2,1)S(1)}, u32[]{:S(2)}, u32[]{:S(2)}) %collective-permute-start) | collective-permute-done | bytes 524320 | tf_op jit(solution)/shard_map/cond/branch_1_fun/while/body/eval_jaxpr/ppermute | solution.py:541
  456.3 14.4 %collective-permute-done = bf16[512,512]{1,0:T(8,128)(2,1)S(1)} collective-permute-done((bf16[512,512]{1,0:T(8,128)(2,1)S(1)}, bf16[512,512]{1,0:T(8,128)(2,1)S(1)}, u32[]{:S(2)}, u32[]{:S(2)}) %collective-permute-start) | collective-permute-done | bytes 524320 | tf_op jit(solution)/shard_map/cond/branch_1_fun/while/body/eval_jaxpr/ppermute | solution.py:541
  482.4 14.4 %collective-permute-done = bf16[512,512]{1,0:T(8,128)(2,1)S(1)} collective-permute-done((bf16[512,512]{1,0:T(8,128)(2,1)S(1)}, bf16[512,512]{1,0:T(8,128)(2,1)S(1)}, u32[]{:S(2)}, u32[]{:S(2)}) %collective-permute-start) | collective-permute-done | bytes 524320 | tf_op jit(solution)/shard_map/cond/branch_1_fun/while/body/eval_jaxpr/ppermute | solution.py:541
  509.6 14.3 %collective-permute-done = bf16[512,512]{1,0:T(8,128)(2,1)S(1)} collective-permute-done((bf16[512,512]{1,0:T(8,128)(2,1)S(1)}, bf16[512,512]{1,0:T(8,128)(2,1)S(1)}, u32[]{:S(2)}, u32[]{:S(2)}) %collective-permute-start) | collective-permute-done | bytes 524320 | tf_op jit(solution)/shard_map/cond/branch_1_fun/while/body/eval_jaxpr/ppermute | solution.py:541
  537.9 14.1 %collective-permute-done = bf16[512,512]{1,0:T(8,128)(2,1)S(1)} collective-permute-done((bf16[512,512]{1,0:T(8,128)(2,1)S(1)}, bf16[512,512]{1,0:T(8,128)(2,1)S(1)}, u32[]{:S(2)}, u32[]{:S(2)}) %collective-permute-start) | collective-permute-done | bytes 524320 | tf_op jit(solution)/shard_map/cond/branch_1_fun/while/body/eval_jaxpr/ppermute | solution.py:541
  552.0 11.3 %collective-permute-done.1 = bf16[512,512]{1,0:T(8,128)(2,1)} collective-permute-done((bf16[512,512]{1,0:T(8,128)(2,1)S(1)}, bf16[512,512]{1,0:T(8,128)(2,1)}, u32[]{:S(2)}, u32[]{:S(2)}) %collective-permute-start.1) | collective-permute-done | bytes 524320 | tf_op jit(solution)/shard_map/cond/branch_1_fun/while/body/eval_jaxpr/ppermute | solution.py:541
  567.4 13.3 %collective-permute-done = bf16[512,512]{1,0:T(8,128)(2,1)S(1)} collective-permute-done((bf16[512,512]{1,0:T(8,128)(2,1)S(1)}, bf16[512,512]{1,0:T(8,128)(2,1)S(1)}, u32[]{:S(2)}, u32[]{:S(2)}) %collective-permute-start) | collective-permute-done | bytes 524320 | tf_op jit(solution)/shard_map/cond/branch_1_fun/while/body/eval_jaxpr/ppermute | solution.py:541
  580.6 11.3 %collective-permute-done.1 = bf16[512,512]{1,0:T(8,128)(2,1)} collective-permute-done((bf16[512,512]{1,0:T(8,128)(2,1)S(1)}, bf16[512,512]{1,0:T(8,128)(2,1)}, u32[]{:S(2)}, u32[]{:S(2)}) %collective-permute-start.1) | collective-permute-done | bytes 524320 | tf_op jit(solution)/shard_map/cond/branch_1_fun/while/body/eval_jaxpr/ppermute | solution.py:541
  596.0 12.3 %collective-permute-done = bf16[512,512]{1,0:T(8,128)(2,1)S(1)} collective-permute-done((bf16[512,512]{1,0:T(8,128)(2,1)S(1)}, bf16[512,512]{1,0:T(8,128)(2,1)S(1)}, u32[]{:S(2)}, u32[]{:S(2)}) %collective-permute-start) | collective-permute-done | bytes 524320 | tf_op jit(solution)/shard_map/cond/branch_1_fun/while/body/eval_jaxpr/ppermute | solution.py:541
  608.4 11.3 %collective-permute-done.1 = bf16[512,512]{1,0:T(8,128)(2,1)} collective-permute-done((bf16[512,512]{1,0:T(8,128)(2,1)S(1)}, bf16[512,512]{1,0:T(8,128)(2,1)}, u32[]{:S(2)}, u32[]{:S(2)}) %collective-permute-start.1) | collective-permute-done | bytes 524320 | tf_op jit(solution)/shard_map/cond/branch_1_fun/while/body/eval_jaxpr/ppermute | solution.py:541
  623.8 11.4 %collective-permute-done = bf16[512,512]{1,0:T(8,128)(2,1)S(1)} collective-permute-done((bf16[512,512]{1,0:T(8,128)(2,1)S(1)}, bf16[512,512]{1,0:T(8,128)(2,1)S(1)}, u32[]{:S(2)}, u32[]{:S(2)}) %collective-permute-start) | collective-permute-done | bytes 524320 | tf_op jit(solution)/shard_map/cond/branch_1_fun/while/body/eval_jaxpr/ppermute | solution.py:541
  635.2 11.3 %collective-permute-done.1 = bf16[512,512]{1,0:T(8,128)(2,1)} collective-permute-done((bf16[512,512]{1,0:T(8,128)(2,1)S(1)}, bf16[512,512]{1,0:T(8,128)(2,1)}, u32[]{:S(2)}, u32[]{:S(2)}) %collective-permute-start.1) | collective-permute-done | bytes 524320 | tf_op jit(solution)/shard_map/cond/branch_1_fun/while/body/eval_jaxpr/ppermute | solution.py:541
  661.1 11.3 %collective-permute-done.1 = bf16[512,512]{1,0:T(8,128)(2,1)} collective-permute-done((bf16[512,512]{1,0:T(8,128)(2,1)S(1)}, bf16[512,512]{1,0:T(8,128)(2,1)}, u32[]{:S(2)}, u32[]{:S(2)}) %collective-permute-start.1) | collective-permute-done | bytes 524320 | tf_op jit(solution)/shard_map/cond/branch_1_fun/while/body/eval_jaxpr/ppermute | solution.py:541
  686.1 11.3 %collective-permute-done.1 = bf16[512,512]{1,0:T(8,128)(2,1)} collective-permute-done((bf16[512,512]{1,0:T(8,128)(2,1)S(1)}, bf16[512,512]{1,0:T(8,128)(2,1)}, u32[]{:S(2)}, u32[]{:S(2)}) %collective-permute-start.1) | collective-permute-done | bytes 524320 | tf_op jit(solution)/shard_map/cond/branch_1_fun/while/body/eval_jaxpr/ppermute | solution.py:541
  710.1 11.3 %collective-permute-done.1 = bf16[512,512]{1,0:T(8,128)(2,1)} collective-permute-done((bf16[512,512]{1,0:T(8,128)(2,1)S(1)}, bf16[512,512]{1,0:T(8,128)(2,1)}, u32[]{:S(2)}, u32[]{:S(2)}) %collective-permute-start.1) | collective-permute-done | bytes 524320 | tf_op jit(solution)/shard_map/cond/branch_1_fun/while/body/eval_jaxpr/ppermute | solution.py:541
  835.0 11.7 %collective-permute-done = bf16[512,512]{1,0:T(8,128)(2,1)S(1)} collective-permute-done((bf16[512,512]{1,0:T(8,128)(2,1)S(1)}, bf16[512,512]{1,0:T(8,128)(2,1)S(1)}, u32[]{:S(2)}, u32[]{:S(2)}) %collective-permute-start) | collective-permute-done | bytes 524320 | tf_op jit(solution)/shard_map/cond/branch_1_fun/while/body/eval_jaxpr/ppermute | solution.py:541
  856.5 12.7 %collective-permute-done = bf16[512,512]{1,0:T(8,128)(2,1)S(1)} collective-permute-done((bf16[512,512]{1,0:T(8,128)(2,1)S(1)}, bf16[512,512]{1,0:T(8,128)(2,1)S(1)}, u32[]{:S(2)}, u32[]{:S(2)}) %collective-permute-start) | collective-permute-done | bytes 524320 | tf_op jit(solution)/shard_map/cond/branch_1_fun/while/body/eval_jaxpr/ppermute | solution.py:541
  884.6 34.5 %collective-permute-start.2 = (f32[128,4096]{1,0:T(8,128)}, f32[128,4096]{1,0:T(8,128)}, u32[]{:S(2)}, u32[]{:S(2)}) collective-permute-start(f32[128,4096]{1,0:T(8,128)} %get-tuple-element.122), channel_id=1, source_target_pairs={{0,1},{1,2},{2,3},{3,0},{4,5},{5,6},{6,7},{7,4},{8,9},{9,10},{10,1... | collective-permute-start | bytes 6291464 | tf_op jit(solution)/shard_map/cond/branch_1_fun/ppermute | solution.py:553
  919.8 43.6 %collective-permute-done.2 = f32[128,4096]{1,0:T(8,128)} collective-permute-done((f32[128,4096]{1,0:T(8,128)}, f32[128,4096]{1,0:T(8,128)}, u32[]{:S(2)}, u32[]{:S(2)}) %collective-permute-start.2) | collective-permute-done | bytes 2097184 | tf_op jit(solution)/shard_map/cond/branch_1_fun/ppermute | solution.py:553
  968.9 39.5 %collective-permute-done.3 = f32[128,4096]{1,0:T(8,128)} collective-permute-done((f32[128,4096]{1,0:T(8,128)S(1)}, f32[128,4096]{1,0:T(8,128)}, u32[]{:S(2)}, u32[]{:S(2)}) %collective-permute-start.3) | collective-permute-done | bytes 2097184 | tf_op jit(solution)/shard_map/cond/branch_1_fun/ppermute | solution.py:553
  (394 shorter events, 493.8 us)
Async XLA Ops:
  95.8 25.8 %collective-permute-start.1 = (bf16[512,512]{1,0:T(8,128)(2,1)S(1)}, bf16[512,512]{1,0:T(8,128)(2,1)}, u32[]{:S(2)}, u32[]{:S(2)}) collective-permute-start(bf16[512,512]{1,0:T(8,128)(2,1)S(1)} %copy.48), channel_id=1, source_target_pairs={{0,4},{4,8},{8,12},{12,16},{16,20},{20,24},{24,28},{28,32},{32,36}... | collective-permute-start | bytes 1572872 | tf_op jit(solution)/shard_map/cond/branch_1_fun/while/body/eval_jaxpr/ppermute | solution.py:541
  122.8 26.3 %collective-permute-start.1 = (bf16[512,512]{1,0:T(8,128)(2,1)S(1)}, bf16[512,512]{1,0:T(8,128)(2,1)}, u32[]{:S(2)}, u32[]{:S(2)}) collective-permute-start(bf16[512,512]{1,0:T(8,128)(2,1)S(1)} %copy.48), channel_id=1, source_target_pairs={{0,4},{4,8},{8,12},{12,16},{16,20},{20,24},{24,28},{28,32},{32,36}... | collective-permute-start | bytes 1572872 | tf_op jit(solution)/shard_map/cond/branch_1_fun/while/body/eval_jaxpr/ppermute | solution.py:541
  150.3 25.4 %collective-permute-start.1 = (bf16[512,512]{1,0:T(8,128)(2,1)S(1)}, bf16[512,512]{1,0:T(8,128)(2,1)}, u32[]{:S(2)}, u32[]{:S(2)}) collective-permute-start(bf16[512,512]{1,0:T(8,128)(2,1)S(1)} %copy.48), channel_id=1, source_target_pairs={{0,4},{4,8},{8,12},{12,16},{16,20},{20,24},{24,28},{28,32},{32,36}... | collective-permute-start | bytes 1572872 | tf_op jit(solution)/shard_map/cond/branch_1_fun/while/body/eval_jaxpr/ppermute | solution.py:541
  176.8 24.5 %collective-permute-start.1 = (bf16[512,512]{1,0:T(8,128)(2,1)S(1)}, bf16[512,512]{1,0:T(8,128)(2,1)}, u32[]{:S(2)}, u32[]{:S(2)}) collective-permute-start(bf16[512,512]{1,0:T(8,128)(2,1)S(1)} %copy.48), channel_id=1, source_target_pairs={{0,4},{4,8},{8,12},{12,16},{16,20},{20,24},{24,28},{28,32},{32,36}... | collective-permute-start | bytes 1572872 | tf_op jit(solution)/shard_map/cond/branch_1_fun/while/body/eval_jaxpr/ppermute | solution.py:541
  202.5 23.6 %collective-permute-start.1 = (bf16[512,512]{1,0:T(8,128)(2,1)S(1)}, bf16[512,512]{1,0:T(8,128)(2,1)}, u32[]{:S(2)}, u32[]{:S(2)}) collective-permute-start(bf16[512,512]{1,0:T(8,128)(2,1)S(1)} %copy.48), channel_id=1, source_target_pairs={{0,4},{4,8},{8,12},{12,16},{16,20},{20,24},{24,28},{28,32},{32,36}... | collective-permute-start | bytes 1572872 | tf_op jit(solution)/shard_map/cond/branch_1_fun/while/body/eval_jaxpr/ppermute | solution.py:541
  227.2 22.5 %collective-permute-start.1 = (bf16[512,512]{1,0:T(8,128)(2,1)S(1)}, bf16[512,512]{1,0:T(8,128)(2,1)}, u32[]{:S(2)}, u32[]{:S(2)}) collective-permute-start(bf16[512,512]{1,0:T(8,128)(2,1)S(1)} %copy.48), channel_id=1, source_target_pairs={{0,4},{4,8},{8,12},{12,16},{16,20},{20,24},{24,28},{28,32},{32,36}... | collective-permute-start | bytes 1572872 | tf_op jit(solution)/shard_map/cond/branch_1_fun/while/body/eval_jaxpr/ppermute | solution.py:541
  250.9 21.5 %collective-permute-start.1 = (bf16[512,512]{1,0:T(8,128)(2,1)S(1)}, bf16[512,512]{1,0:T(8,128)(2,1)}, u32[]{:S(2)}, u32[]{:S(2)}) collective-permute-start(bf16[512,512]{1,0:T(8,128)(2,1)S(1)} %copy.48), channel_id=1, source_target_pairs={{0,4},{4,8},{8,12},{12,16},{16,20},{20,24},{24,28},{28,32},{32,36}... | collective-permute-start | bytes 1572872 | tf_op jit(solution)/shard_map/cond/branch_1_fun/while/body/eval_jaxpr/ppermute | solution.py:541
  273.6 20.5 %collective-permute-start.1 = (bf16[512,512]{1,0:T(8,128)(2,1)S(1)}, bf16[512,512]{1,0:T(8,128)(2,1)}, u32[]{:S(2)}, u32[]{:S(2)}) collective-permute-start(bf16[512,512]{1,0:T(8,128)(2,1)S(1)} %copy.48), channel_id=1, source_target_pairs={{0,4},{4,8},{8,12},{12,16},{16,20},{20,24},{24,28},{28,32},{32,36}... | collective-permute-start | bytes 1572872 | tf_op jit(solution)/shard_map/cond/branch_1_fun/while/body/eval_jaxpr/ppermute | solution.py:541
  295.2 20.3 %collective-permute-start.1 = (bf16[512,512]{1,0:T(8,128)(2,1)S(1)}, bf16[512,512]{1,0:T(8,128)(2,1)}, u32[]{:S(2)}, u32[]{:S(2)}) collective-permute-start(bf16[512,512]{1,0:T(8,128)(2,1)S(1)} %copy.48), channel_id=1, source_target_pairs={{0,4},{4,8},{8,12},{12,16},{16,20},{20,24},{24,28},{28,32},{32,36}... | collective-permute-start | bytes 1572872 | tf_op jit(solution)/shard_map/cond/branch_1_fun/while/body/eval_jaxpr/ppermute | solution.py:541
  338.2 20.3 %collective-permute-start.1 = (bf16[512,512]{1,0:T(8,128)(2,1)S(1)}, bf16[512,512]{1,0:T(8,128)(2,1)}, u32[]{:S(2)}, u32[]{:S(2)}) collective-permute-start(bf16[512,512]{1,0:T(8,128)(2,1)S(1)} %copy.48), channel_id=1, source_target_pairs={{0,4},{4,8},{8,12},{12,16},{16,20},{20,24},{24,28},{28,32},{32,36}... | collective-permute-start | bytes 1572872 | tf_op jit(solution)/shard_map/cond/branch_1_fun/while/body/eval_jaxpr/ppermute | solution.py:541
  359.7 20.6 %collective-permute-start.1 = (bf16[512,512]{1,0:T(8,128)(2,1)S(1)}, bf16[512,512]{1,0:T(8,128)(2,1)}, u32[]{:S(2)}, u32[]{:S(2)}) collective-permute-start(bf16[512,512]{1,0:T(8,128)(2,1)S(1)} %copy.48), channel_id=1, source_target_pairs={{0,4},{4,8},{8,12},{12,16},{16,20},{20,24},{24,28},{28,32},{32,36}... | collective-permute-start | bytes 1572872 | tf_op jit(solution)/shard_map/cond/branch_1_fun/while/body/eval_jaxpr/ppermute | solution.py:541
  381.5 21.7 %collective-permute-start.1 = (bf16[512,512]{1,0:T(8,128)(2,1)S(1)}, bf16[512,512]{1,0:T(8,128)(2,1)}, u32[]{:S(2)}, u32[]{:S(2)}) collective-permute-start(bf16[512,512]{1,0:T(8,128)(2,1)S(1)} %copy.48), channel_id=1, source_target_pairs={{0,4},{4,8},{8,12},{12,16},{16,20},{20,24},{24,28},{28,32},{32,36}... | collective-permute-start | bytes 1572872 | tf_op jit(solution)/shard_map/cond/branch_1_fun/while/body/eval_jaxpr/ppermute | solution.py:541
  404.4 22.8 %collective-permute-start.1 = (bf16[512,512]{1,0:T(8,128)(2,1)S(1)}, bf16[512,512]{1,0:T(8,128)(2,1)}, u32[]{:S(2)}, u32[]{:S(2)}) collective-permute-start(bf16[512,512]{1,0:T(8,128)(2,1)S(1)} %copy.48), channel_id=1, source_target_pairs={{0,4},{4,8},{8,12},{12,16},{16,20},{20,24},{24,28},{28,32},{32,36}... | collective-permute-start | bytes 1572872 | tf_op jit(solution)/shard_map/cond/branch_1_fun/while/body/eval_jaxpr/ppermute | solution.py:541
  428.4 23.9 %collective-permute-start.1 = (bf16[512,512]{1,0:T(8,128)(2,1)S(1)}, bf16[512,512]{1,0:T(8,128)(2,1)}, u32[]{:S(2)}, u32[]{:S(2)}) collective-permute-start(bf16[512,512]{1,0:T(8,128)(2,1)S(1)} %copy.48), channel_id=1, source_target_pairs={{0,4},{4,8},{8,12},{12,16},{16,20},{20,24},{24,28},{28,32},{32,36}... | collective-permute-start | bytes 1572872 | tf_op jit(solution)/shard_map/cond/branch_1_fun/while/body/eval_jaxpr/ppermute | solution.py:541
  453.4 25.0 %collective-permute-start.1 = (bf16[512,512]{1,0:T(8,128)(2,1)S(1)}, bf16[512,512]{1,0:T(8,128)(2,1)}, u32[]{:S(2)}, u32[]{:S(2)}) collective-permute-start(bf16[512,512]{1,0:T(8,128)(2,1)S(1)} %copy.48), channel_id=1, source_target_pairs={{0,4},{4,8},{8,12},{12,16},{16,20},{20,24},{24,28},{28,32},{32,36}... | collective-permute-start | bytes 1572872 | tf_op jit(solution)/shard_map/cond/branch_1_fun/while/body/eval_jaxpr/ppermute | solution.py:541
  479.5 26.0 %collective-permute-start.1 = (bf16[512,512]{1,0:T(8,128)(2,1)S(1)}, bf16[512,512]{1,0:T(8,128)(2,1)}, u32[]{:S(2)}, u32[]{:S(2)}) collective-permute-start(bf16[512,512]{1,0:T(8,128)(2,1)S(1)} %copy.48), channel_id=1, source_target_pairs={{0,4},{4,8},{8,12},{12,16},{16,20},{20,24},{24,28},{28,32},{32,36}... | collective-permute-start | bytes 1572872 | tf_op jit(solution)/shard_map/cond/branch_1_fun/while/body/eval_jaxpr/ppermute | solution.py:541
  506.7 27.1 %collective-permute-start.1 = (bf16[512,512]{1,0:T(8,128)(2,1)S(1)}, bf16[512,512]{1,0:T(8,128)(2,1)}, u32[]{:S(2)}, u32[]{:S(2)}) collective-permute-start(bf16[512,512]{1,0:T(8,128)(2,1)S(1)} %copy.48), channel_id=1, source_target_pairs={{0,4},{4,8},{8,12},{12,16},{16,20},{20,24},{24,28},{28,32},{32,36}... | collective-permute-start | bytes 1572872 | tf_op jit(solution)/shard_map/cond/branch_1_fun/while/body/eval_jaxpr/ppermute | solution.py:541
  535.0 28.3 %collective-permute-start.1 = (bf16[512,512]{1,0:T(8,128)(2,1)S(1)}, bf16[512,512]{1,0:T(8,128)(2,1)}, u32[]{:S(2)}, u32[]{:S(2)}) collective-permute-start(bf16[512,512]{1,0:T(8,128)(2,1)S(1)} %copy.48), channel_id=1, source_target_pairs={{0,4},{4,8},{8,12},{12,16},{16,20},{20,24},{24,28},{28,32},{32,36}... | collective-permute-start | bytes 1572872 | tf_op jit(solution)/shard_map/cond/branch_1_fun/while/body/eval_jaxpr/ppermute | solution.py:541
  564.5 27.5 %collective-permute-start.1 = (bf16[512,512]{1,0:T(8,128)(2,1)S(1)}, bf16[512,512]{1,0:T(8,128)(2,1)}, u32[]{:S(2)}, u32[]{:S(2)}) collective-permute-start(bf16[512,512]{1,0:T(8,128)(2,1)S(1)} %copy.48), channel_id=1, source_target_pairs={{0,4},{4,8},{8,12},{12,16},{16,20},{20,24},{24,28},{28,32},{32,36}... | collective-permute-start | bytes 1572872 | tf_op jit(solution)/shard_map/cond/branch_1_fun/while/body/eval_jaxpr/ppermute | solution.py:541
  593.1 26.6 %collective-permute-start.1 = (bf16[512,512]{1,0:T(8,128)(2,1)S(1)}, bf16[512,512]{1,0:T(8,128)(2,1)}, u32[]{:S(2)}, u32[]{:S(2)}) collective-permute-start(bf16[512,512]{1,0:T(8,128)(2,1)S(1)} %copy.48), channel_id=1, source_target_pairs={{0,4},{4,8},{8,12},{12,16},{16,20},{20,24},{24,28},{28,32},{32,36}... | collective-permute-start | bytes 1572872 | tf_op jit(solution)/shard_map/cond/branch_1_fun/while/body/eval_jaxpr/ppermute | solution.py:541
  620.9 25.6 %collective-permute-start.1 = (bf16[512,512]{1,0:T(8,128)(2,1)S(1)}, bf16[512,512]{1,0:T(8,128)(2,1)}, u32[]{:S(2)}, u32[]{:S(2)}) collective-permute-start(bf16[512,512]{1,0:T(8,128)(2,1)S(1)} %copy.48), channel_id=1, source_target_pairs={{0,4},{4,8},{8,12},{12,16},{16,20},{20,24},{24,28},{28,32},{32,36}... | collective-permute-start | bytes 1572872 | tf_op jit(solution)/shard_map/cond/branch_1_fun/while/body/eval_jaxpr/ppermute | solution.py:541
  647.7 24.7 %collective-permute-start.1 = (bf16[512,512]{1,0:T(8,128)(2,1)S(1)}, bf16[512,512]{1,0:T(8,128)(2,1)}, u32[]{:S(2)}, u32[]{:S(2)}) collective-permute-start(bf16[512,512]{1,0:T(8,128)(2,1)S(1)} %copy.48), channel_id=1, source_target_pairs={{0,4},{4,8},{8,12},{12,16},{16,20},{20,24},{24,28},{28,32},{32,36}... | collective-permute-start | bytes 1572872 | tf_op jit(solution)/shard_map/cond/branch_1_fun/while/body/eval_jaxpr/ppermute | solution.py:541
  673.6 23.8 %collective-permute-start.1 = (bf16[512,512]{1,0:T(8,128)(2,1)S(1)}, bf16[512,512]{1,0:T(8,128)(2,1)}, u32[]{:S(2)}, u32[]{:S(2)}) collective-permute-start(bf16[512,512]{1,0:T(8,128)(2,1)S(1)} %copy.48), channel_id=1, source_target_pairs={{0,4},{4,8},{8,12},{12,16},{16,20},{20,24},{24,28},{28,32},{32,36}... | collective-permute-start | bytes 1572872 | tf_op jit(solution)/shard_map/cond/branch_1_fun/while/body/eval_jaxpr/ppermute | solution.py:541
  698.6 22.9 %collective-permute-start.1 = (bf16[512,512]{1,0:T(8,128)(2,1)S(1)}, bf16[512,512]{1,0:T(8,128)(2,1)}, u32[]{:S(2)}, u32[]{:S(2)}) collective-permute-start(bf16[512,512]{1,0:T(8,128)(2,1)S(1)} %copy.48), channel_id=1, source_target_pairs={{0,4},{4,8},{8,12},{12,16},{16,20},{20,24},{24,28},{28,32},{32,36}... | collective-permute-start | bytes 1572872 | tf_op jit(solution)/shard_map/cond/branch_1_fun/while/body/eval_jaxpr/ppermute | solution.py:541
  722.6 21.9 %collective-permute-start.1 = (bf16[512,512]{1,0:T(8,128)(2,1)S(1)}, bf16[512,512]{1,0:T(8,128)(2,1)}, u32[]{:S(2)}, u32[]{:S(2)}) collective-permute-start(bf16[512,512]{1,0:T(8,128)(2,1)S(1)} %copy.48), channel_id=1, source_target_pairs={{0,4},{4,8},{8,12},{12,16},{16,20},{20,24},{24,28},{28,32},{32,36}... | collective-permute-start | bytes 1572872 | tf_op jit(solution)/shard_map/cond/branch_1_fun/while/body/eval_jaxpr/ppermute | solution.py:541
  745.6 20.8 %collective-permute-start.1 = (bf16[512,512]{1,0:T(8,128)(2,1)S(1)}, bf16[512,512]{1,0:T(8,128)(2,1)}, u32[]{:S(2)}, u32[]{:S(2)}) collective-permute-start(bf16[512,512]{1,0:T(8,128)(2,1)S(1)} %copy.48), channel_id=1, source_target_pairs={{0,4},{4,8},{8,12},{12,16},{16,20},{20,24},{24,28},{28,32},{32,36}... | collective-permute-start | bytes 1572872 | tf_op jit(solution)/shard_map/cond/branch_1_fun/while/body/eval_jaxpr/ppermute | solution.py:541
  767.6 20.3 %collective-permute-start.1 = (bf16[512,512]{1,0:T(8,128)(2,1)S(1)}, bf16[512,512]{1,0:T(8,128)(2,1)}, u32[]{:S(2)}, u32[]{:S(2)}) collective-permute-start(bf16[512,512]{1,0:T(8,128)(2,1)S(1)} %copy.48), channel_id=1, source_target_pairs={{0,4},{4,8},{8,12},{12,16},{16,20},{20,24},{24,28},{28,32},{32,36}... | collective-permute-start | bytes 1572872 | tf_op jit(solution)/shard_map/cond/branch_1_fun/while/body/eval_jaxpr/ppermute | solution.py:541
  789.1 20.3 %collective-permute-start.1 = (bf16[512,512]{1,0:T(8,128)(2,1)S(1)}, bf16[512,512]{1,0:T(8,128)(2,1)}, u32[]{:S(2)}, u32[]{:S(2)}) collective-permute-start(bf16[512,512]{1,0:T(8,128)(2,1)S(1)} %copy.48), channel_id=1, source_target_pairs={{0,4},{4,8},{8,12},{12,16},{16,20},{20,24},{24,28},{28,32},{32,36}... | collective-permute-start | bytes 1572872 | tf_op jit(solution)/shard_map/cond/branch_1_fun/while/body/eval_jaxpr/ppermute | solution.py:541
  853.6 21.4 %collective-permute-start.1 = (bf16[512,512]{1,0:T(8,128)(2,1)S(1)}, bf16[512,512]{1,0:T(8,128)(2,1)}, u32[]{:S(2)}, u32[]{:S(2)}) collective-permute-start(bf16[512,512]{1,0:T(8,128)(2,1)S(1)} %copy.48), channel_id=1, source_target_pairs={{0,4},{4,8},{8,12},{12,16},{16,20},{20,24},{24,28},{28,32},{32,36}... | collective-permute-start | bytes 1572872 | tf_op jit(solution)/shard_map/cond/branch_1_fun/while/body/eval_jaxpr/ppermute | solution.py:541
  884.6 78.9 %collective-permute-start.2 = (f32[128,4096]{1,0:T(8,128)}, f32[128,4096]{1,0:T(8,128)}, u32[]{:S(2)}, u32[]{:S(2)}) collective-permute-start(f32[128,4096]{1,0:T(8,128)} %get-tuple-element.122), channel_id=1, source_target_pairs={{0,1},{1,2},{2,3},{3,0},{4,5},{5,6},{6,7},{7,4},{8,9},{9,10},{10,1... | collective-permute-start | bytes 6291464 | tf_op jit(solution)/shard_map/cond/branch_1_fun/ppermute | solution.py:553
  919.0 49.8 %collective-permute-start.4 = (f32[128,4096]{1,0:T(8,128)}, f32[128,4096]{1,0:T(8,128)}, u32[]{:S(2)}, u32[]{:S(2)}) collective-permute-start(f32[128,4096]{1,0:T(8,128)} %get-tuple-element.123), channel_id=1, source_target_pairs={{0,3},{1,0},{2,1},{3,2},{4,7},{5,4},{6,5},{7,6},{8,11},{9,8},{10,9... | collective-permute-start | bytes 6291464 | tf_op jit(solution)/shard_map/cond/branch_1_fun/ppermute | solution.py:553
  919.1 89.4 %collective-permute-start.3 = (f32[128,4096]{1,0:T(8,128)S(1)}, f32[128,4096]{1,0:T(8,128)}, u32[]{:S(2)}, u32[]{:S(2)}) collective-permute-start(f32[128,4096]{1,0:T(8,128)S(1)} %get-tuple-element.124), channel_id=1, source_target_pairs={{0,2},{1,3},{2,0},{3,1},{4,6},{5,7},{6,4},{7,5},{8,10},{9,11},{10,... | collective-permute-start | bytes 6291464 | tf_op jit(solution)/shard_map/cond/branch_1_fun/ppermute | solution.py:553
  (41 other events, 726.5 us)

commit v5 on v4

--- a/solution.py
+++ b/solution.py
@@ -33,8 +33,8 @@
 LAST = 15
 CROSS = (0, 1, 2, 3, 6, 7, 15)
 EXTRA = {
-    0: (("own", 0),), 4: (("in", 0),), 5: (("in", 1),), 6: (("in", 2), ("in", 3)), 8: (("in", 6),), 11: (("in", 7), ("side", 0)),
-    12: (("in", 4), ("side", 1)), 13: (("in", 5), ("side", 2), ("side", 3)), 14: (("side", 6),),
+    0: (("own", 0),), 2: (("in", 0),), 3: (("in", 1),), 5: (("in", 2),), 7: (("in", 3),), 9: (("in", 6),), 10: (("side", 0), ("side", 1)),
+    11: (("in", 7), ("in", 4)), 12: (("in", 5), ("side", 2)), 13: (("side", 3),), 14: (("side", 6),),
     16: (("side", 7), ("side", 4), ("side", 5)),
 }
 

time: 1020 us -> 1020 us (level)
  no operation moved by 1% of the time
where the time goes in v5:
time: 1020 us; the launch traced here: 1010 us
  waiting for transfers between devices  738 us (72%)
  matrix products  84.2 us (8%)
  Pallas kernels  78.4 us (8%)
  local copies, waits for them, and re-layouts  40.8 us (4%)
  starting transfers between devices  39.4 us (4%)
  other arithmetic  28.7 us (3%)
    ppermute x32, waiting for transfers between devices, add_part(): lax.ppermute(keys, 'seq', ring)  357 us
    ppermute x32, waiting for transfers between devices, add_part(): lax.ppermute(values, 'seq', ring)  293 us
    ppermute x3, waiting for transfers between devices, plain_shards(): lax.ppermute(leaving, 'head', [(m, (m + n) % heads) for m in range(heads)])  88.5 us
    pallas_call x1, Pallas kernels, shards(): pl.pallas_call(attend_kernel, out_shape=(struct((rows // 4, width), BF16)...  78.4 us
    dot_general x32, matrix products, add_part(): jnp.einsum('hqk,khd->qhd', weights.astype(jnp.bfloat16), values.reshape(q...  44.6 us
    ppermute x3, starting transfers between devices, plain_shards(): lax.ppermute(leaving, 'head', [(m, (m + n) % heads) for m in range(heads)])  35.5 us
    while x96, local copies, waits for them, and re-layouts  34.6 us
    dot_general x32, matrix products, add_part(): jnp.einsum('qhd,khd->hqk', queries, keys.reshape(queries.shape), preferre...  23 us
  transfers between devices with their start and end apart: 67, of which 67 were waited for; matrix products, arithmetic and copies ran while one was open for 12% of the time, Pallas kernels for 0%

profile of v5, /device:TPU:1, one launch (start us, length us, event | category | flops | bytes accessed | tf_op | source)
XLA Modules:
  0.0 1012.7 jit_solution(2781913509002869487)
XLA Ops:
  0.0 78.4 %attend.1 = (bf16[128,4096]{1,0:T(8,128)(2,1)S(1)}, f32[1,1]{1,0:T(1,128)}) custom-call(bf16[512,4096]{1,0:T(8,128)(2,1)} %tok_hbm.1, s32[1,512]{1,0:T(1,128)} %bitcast.54, bf16[4096]{0:T(1024)(128)(2,1)} %embed_ref.1, bf16[4096,512]{1,0:T(8,128)(2,1)} %wq_hbm.1, bf16[4096,512]{1,0:T(8,128)(2,1)} %wk_hbm.1, bf16[4096,512]{1,0:T(8,128)(2,1)} %wv_hbm.1, ...), custom_call_target="tpu_custom_call" | custom-call | tf_op jit(solution)/shard_map/attend/pallas_call | solution.py:562
  79.1 932.7 %conditional.1 = (bf16[128,4096]{1,0:T(8,128)(2,1)S(1)}) conditional(s32[]{:T(128)} %bitcast.6, bf16[128,4096]{1,0:T(8,128)(2,1)S(1)} %get-tuple-element.71, (bf16[512,4096]{1,0:T(8,128)(2,1)}, s32[512]{0:T(512)S(1)}, bf16[4096]{0:T(1024)(128)(2,1)S(1)}, bf16[4096,512]{1,0:T(8,128)(2,1)}, bf16[4096,512]{1,0:T(8,128)(2,1)}, ...), branch_computations={%region_0.0_spmd, %region_1.6_spmd} | conditional | flops 9168275456 | bytes 206274176 | solution.py:593
  92.9 781.0 %while.18 = (s32[]{:T(128)}, bf16[512,512]{1,0:T(8,128)(2,1)S(1)}, bf16[512,512]{1,0:T(8,128)(2,1)}, f32[4,512]{1,0:T(4,128)S(1)}, f32[4,512]{1,0:T(4,128)S(1)},...) while((s32[]{:T(128)}, bf16[512,512]{1,0:T(8,128)(2,1)S(1)}, ...), condition=%wide.region_5.0_spmd.clone, body=%wide.region_2.0_spmd.clone.sunk | while | flops 546058240 | bytes 22675640 | solution.py:543
  98.6 11.6 %collective-permute-done = bf16[512,512]{1,0:T(8,128)(2,1)S(1)} collective-permute-done((bf16[512,512]{1,0:T(8,128)(2,1)S(1)}, bf16[512,512]{1,0:T(8,128)(2,1)S(1)}, u32[]{:S(2)}, u32[]{:S(2)}) %collective-permute-start) | collective-permute-done | bytes 524320 | tf_op jit(solution)/shard_map/cond/branch_1_fun/while/body/eval_jaxpr/ppermute | solution.py:541
  110.1 11.3 %collective-permute-done.1 = bf16[512,512]{1,0:T(8,128)(2,1)} collective-permute-done((bf16[512,512]{1,0:T(8,128)(2,1)S(1)}, bf16[512,512]{1,0:T(8,128)(2,1)}, u32[]{:S(2)}, u32[]{:S(2)}) %collective-permute-start.1) | collective-permute-done | bytes 524320 | tf_op jit(solution)/shard_map/cond/branch_1_fun/while/body/eval_jaxpr/ppermute | solution.py:541
  125.5 12.0 %collective-permute-done = bf16[512,512]{1,0:T(8,128)(2,1)S(1)} collective-permute-done((bf16[512,512]{1,0:T(8,128)(2,1)S(1)}, bf16[512,512]{1,0:T(8,128)(2,1)S(1)}, u32[]{:S(2)}, u32[]{:S(2)}) %collective-permute-start) | collective-permute-done | bytes 524320 | tf_op jit(solution)/shard_map/cond/branch_1_fun/while/body/eval_jaxpr/ppermute | solution.py:541
  137.5 11.3 %collective-permute-done.1 = bf16[512,512]{1,0:T(8,128)(2,1)} collective-permute-done((bf16[512,512]{1,0:T(8,128)(2,1)S(1)}, bf16[512,512]{1,0:T(8,128)(2,1)}, u32[]{:S(2)}, u32[]{:S(2)}) %collective-permute-start.1) | collective-permute-done | bytes 524320 | tf_op jit(solution)/shard_map/cond/branch_1_fun/while/body/eval_jaxpr/ppermute | solution.py:541
  164.0 11.3 %collective-permute-done.1 = bf16[512,512]{1,0:T(8,128)(2,1)} collective-permute-done((bf16[512,512]{1,0:T(8,128)(2,1)S(1)}, bf16[512,512]{1,0:T(8,128)(2,1)}, u32[]{:S(2)}, u32[]{:S(2)}) %collective-permute-start.1) | collective-permute-done | bytes 524320 | tf_op jit(solution)/shard_map/cond/branch_1_fun/while/body/eval_jaxpr/ppermute | solution.py:541
  189.6 11.3 %collective-permute-done.1 = bf16[512,512]{1,0:T(8,128)(2,1)} collective-permute-done((bf16[512,512]{1,0:T(8,128)(2,1)S(1)}, bf16[512,512]{1,0:T(8,128)(2,1)}, u32[]{:S(2)}, u32[]{:S(2)}) %collective-permute-start.1) | collective-permute-done | bytes 524320 | tf_op jit(solution)/shard_map/cond/branch_1_fun/while/body/eval_jaxpr/ppermute | solution.py:541
  214.2 11.3 %collective-permute-done.1 = bf16[512,512]{1,0:T(8,128)(2,1)} collective-permute-done((bf16[512,512]{1,0:T(8,128)(2,1)S(1)}, bf16[512,512]{1,0:T(8,128)(2,1)}, u32[]{:S(2)}, u32[]{:S(2)}) %collective-permute-start.1) | collective-permute-done | bytes 524320 | tf_op jit(solution)/shard_map/cond/branch_1_fun/while/body/eval_jaxpr/ppermute | solution.py:541
  361.8 12.1 %collective-permute-done = bf16[512,512]{1,0:T(8,128)(2,1)S(1)} collective-permute-done((bf16[512,512]{1,0:T(8,128)(2,1)S(1)}, bf16[512,512]{1,0:T(8,128)(2,1)S(1)}, u32[]{:S(2)}, u32[]{:S(2)}) %collective-permute-start) | collective-permute-done | bytes 524320 | tf_op jit(solution)/shard_map/cond/branch_1_fun/while/body/eval_jaxpr/ppermute | solution.py:541
  383.7 13.2 %collective-permute-done = bf16[512,512]{1,0:T(8,128)(2,1)S(1)} collective-permute-done((bf16[512,512]{1,0:T(8,128)(2,1)S(1)}, bf16[512,512]{1,0:T(8,128)(2,1)S(1)}, u32[]{:S(2)}, u32[]{:S(2)}) %collective-permute-start) | collective-permute-done | bytes 524320 | tf_op jit(solution)/shard_map/cond/branch_1_fun/while/body/eval_jaxpr/ppermute | solution.py:541
  406.7 14.4 %collective-permute-done = bf16[512,512]{1,0:T(8,128)(2,1)S(1)} collective-permute-done((bf16[512,512]{1,0:T(8,128)(2,1)S(1)}, bf16[512,512]{1,0:T(8,128)(2,1)S(1)}, u32[]{:S(2)}, u32[]{:S(2)}) %collective-permute-start) | collective-permute-done | bytes 524320 | tf_op jit(solution)/shard_map/cond/branch_1_fun/while/body/eval_jaxpr/ppermute | solution.py:541
  430.8 14.4 %collective-permute-done = bf16[512,512]{1,0:T(8,128)(2,1)S(1)} collective-permute-done((bf16[512,512]{1,0:T(8,128)(2,1)S(1)}, bf16[512,512]{1,0:T(8,128)(2,1)S(1)}, u32[]{:S(2)}, u32[]{:S(2)}) %collective-permute-start) | collective-permute-done | bytes 524320 | tf_op jit(solution)/shard_map/cond/branch_1_fun/while/body/eval_jaxpr/ppermute | solution.py:541
  455.9 14.4 %collective-permute-done = bf16[512,512]{1,0:T(8,128)(2,1)S(1)} collective-permute-done((bf16[512,512]{1,0:T(8,128)(2,1)S(1)}, bf16[512,512]{1,0:T(8,128)(2,1)S(1)}, u32[]{:S(2)}, u32[]{:S(2)}) %collective-permute-start) | collective-permute-done | bytes 524320 | tf_op jit(solution)/shard_map/cond/branch_1_fun/while/body/eval_jaxpr/ppermute | solution.py:541
  482.1 14.4 %collective-permute-done = bf16[512,512]{1,0:T(8,128)(2,1)S(1)} collective-permute-done((bf16[512,512]{1,0:T(8,128)(2,1)S(1)}, bf16[512,512]{1,0:T(8,128)(2,1)S(1)}, u32[]{:S(2)}, u32[]{:S(2)}) %collective-permute-start) | collective-permute-done | bytes 524320 | tf_op jit(solution)/shard_map/cond/branch_1_fun/while/body/eval_jaxpr/ppermute | solution.py:541
  509.4 14.3 %collective-permute-done = bf16[512,512]{1,0:T(8,128)(2,1)S(1)} collective-permute-done((bf16[512,512]{1,0:T(8,128)(2,1)S(1)}, bf16[512,512]{1,0:T(8,128)(2,1)S(1)}, u32[]{:S(2)}, u32[]{:S(2)}) %collective-permute-start) | collective-permute-done | bytes 524320 | tf_op jit(solution)/shard_map/cond/branch_1_fun/while/body/eval_jaxpr/ppermute | solution.py:541
  537.8 14.0 %collective-permute-done = bf16[512,512]{1,0:T(8,128)(2,1)S(1)} collective-permute-done((bf16[512,512]{1,0:T(8,128)(2,1)S(1)}, bf16[512,512]{1,0:T(8,128)(2,1)S(1)}, u32[]{:S(2)}, u32[]{:S(2)}) %collective-permute-start) | collective-permute-done | bytes 524320 | tf_op jit(solution)/shard_map/cond/branch_1_fun/while/body/eval_jaxpr/ppermute | solution.py:541
  551.8 11.3 %collective-permute-done.1 = bf16[512,512]{1,0:T(8,128)(2,1)} collective-permute-done((bf16[512,512]{1,0:T(8,128)(2,1)S(1)}, bf16[512,512]{1,0:T(8,128)(2,1)}, u32[]{:S(2)}, u32[]{:S(2)}) %collective-permute-start.1) | collective-permute-done | bytes 524320 | tf_op jit(solution)/shard_map/cond/branch_1_fun/while/body/eval_jaxpr/ppermute | solution.py:541
  567.1 13.1 %collective-permute-done = bf16[512,512]{1,0:T(8,128)(2,1)S(1)} collective-permute-done((bf16[512,512]{1,0:T(8,128)(2,1)S(1)}, bf16[512,512]{1,0:T(8,128)(2,1)S(1)}, u32[]{:S(2)}, u32[]{:S(2)}) %collective-permute-start) | collective-permute-done | bytes 524320 | tf_op jit(solution)/shard_map/cond/branch_1_fun/while/body/eval_jaxpr/ppermute | solution.py:541
  580.3 11.3 %collective-permute-done.1 = bf16[512,512]{1,0:T(8,128)(2,1)} collective-permute-done((bf16[512,512]{1,0:T(8,128)(2,1)S(1)}, bf16[512,512]{1,0:T(8,128)(2,1)}, u32[]{:S(2)}, u32[]{:S(2)}) %collective-permute-start.1) | collective-permute-done | bytes 524320 | tf_op jit(solution)/shard_map/cond/branch_1_fun/while/body/eval_jaxpr/ppermute | solution.py:541
  595.7 12.2 %collective-permute-done = bf16[512,512]{1,0:T(8,128)(2,1)S(1)} collective-permute-done((bf16[512,512]{1,0:T(8,128)(2,1)S(1)}, bf16[512,512]{1,0:T(8,128)(2,1)S(1)}, u32[]{:S(2)}, u32[]{:S(2)}) %collective-permute-start) | collective-permute-done | bytes 524320 | tf_op jit(solution)/shard_map/cond/branch_1_fun/while/body/eval_jaxpr/ppermute | solution.py:541
  607.9 11.3 %collective-permute-done.1 = bf16[512,512]{1,0:T(8,128)(2,1)} collective-permute-done((bf16[512,512]{1,0:T(8,128)(2,1)S(1)}, bf16[512,512]{1,0:T(8,128)(2,1)}, u32[]{:S(2)}, u32[]{:S(2)}) %collective-permute-start.1) | collective-permute-done | bytes 524320 | tf_op jit(solution)/shard_map/cond/branch_1_fun/while/body/eval_jaxpr/ppermute | solution.py:541
  634.6 11.3 %collective-permute-done.1 = bf16[512,512]{1,0:T(8,128)(2,1)} collective-permute-done((bf16[512,512]{1,0:T(8,128)(2,1)S(1)}, bf16[512,512]{1,0:T(8,128)(2,1)}, u32[]{:S(2)}, u32[]{:S(2)}) %collective-permute-start.1) | collective-permute-done | bytes 524320 | tf_op jit(solution)/shard_map/cond/branch_1_fun/while/body/eval_jaxpr/ppermute | solution.py:541
  660.4 11.3 %collective-permute-done.1 = bf16[512,512]{1,0:T(8,128)(2,1)} collective-permute-done((bf16[512,512]{1,0:T(8,128)(2,1)S(1)}, bf16[512,512]{1,0:T(8,128)(2,1)}, u32[]{:S(2)}, u32[]{:S(2)}) %collective-permute-start.1) | collective-permute-done | bytes 524320 | tf_op jit(solution)/shard_map/cond/branch_1_fun/while/body/eval_jaxpr/ppermute | solution.py:541
  685.2 11.3 %collective-permute-done.1 = bf16[512,512]{1,0:T(8,128)(2,1)} collective-permute-done((bf16[512,512]{1,0:T(8,128)(2,1)S(1)}, bf16[512,512]{1,0:T(8,128)(2,1)}, u32[]{:S(2)}, u32[]{:S(2)}) %collective-permute-start.1) | collective-permute-done | bytes 524320 | tf_op jit(solution)/shard_map/cond/branch_1_fun/while/body/eval_jaxpr/ppermute | solution.py:541
  708.9 11.5 %collective-permute-done.1 = bf16[512,512]{1,0:T(8,128)(2,1)} collective-permute-done((bf16[512,512]{1,0:T(8,128)(2,1)S(1)}, bf16[512,512]{1,0:T(8,128)(2,1)}, u32[]{:S(2)}, u32[]{:S(2)}) %collective-permute-start.1) | collective-permute-done | bytes 524320 | tf_op jit(solution)/shard_map/cond/branch_1_fun/while/body/eval_jaxpr/ppermute | solution.py:541
  833.5 11.9 %collective-permute-done = bf16[512,512]{1,0:T(8,128)(2,1)S(1)} collective-permute-done((bf16[512,512]{1,0:T(8,128)(2,1)S(1)}, bf16[512,512]{1,0:T(8,128)(2,1)S(1)}, u32[]{:S(2)}, u32[]{:S(2)}) %collective-permute-start) | collective-permute-done | bytes 524320 | tf_op jit(solution)/shard_map/cond/branch_1_fun/while/body/eval_jaxpr/ppermute | solution.py:541
  855.2 13.0 %collective-permute-done = bf16[512,512]{1,0:T(8,128)(2,1)S(1)} collective-permute-done((bf16[512,512]{1,0:T(8,128)(2,1)S(1)}, bf16[512,512]{1,0:T(8,128)(2,1)S(1)}, u32[]{:S(2)}, u32[]{:S(2)}) %collective-permute-start) | collective-permute-done | bytes 524320 | tf_op jit(solution)/shard_map/cond/branch_1_fun/while/body/eval_jaxpr/ppermute | solution.py:541
  883.5 34.7 %collective-permute-start.2 = (f32[128,4096]{1,0:T(8,128)}, f32[128,4096]{1,0:T(8,128)}, u32[]{:S(2)}, u32[]{:S(2)}) collective-permute-start(f32[128,4096]{1,0:T(8,128)} %get-tuple-element.122), channel_id=1, source_target_pairs={{0,1},{1,2},{2,3},{3,0},{4,5},{5,6},{6,7},{7,4},{8,9},{9,10},{10,1... | collective-permute-start | bytes 6291464 | tf_op jit(solution)/shard_map/cond/branch_1_fun/ppermute | solution.py:553
  919.0 43.6 %collective-permute-done.2 = f32[128,4096]{1,0:T(8,128)} collective-permute-done((f32[128,4096]{1,0:T(8,128)}, f32[128,4096]{1,0:T(8,128)}, u32[]{:S(2)}, u32[]{:S(2)}) %collective-permute-start.2) | collective-permute-done | bytes 2097184 | tf_op jit(solution)/shard_map/cond/branch_1_fun/ppermute | solution.py:553
  968.1 39.5 %collective-permute-done.3 = f32[128,4096]{1,0:T(8,128)} collective-permute-done((f32[128,4096]{1,0:T(8,128)S(1)}, f32[128,4096]{1,0:T(8,128)}, u32[]{:S(2)}, u32[]{:S(2)}) %collective-permute-start.3) | collective-permute-done | bytes 2097184 | tf_op jit(solution)/shard_map/cond/branch_1_fun/ppermute | solution.py:553
  (394 shorter events, 492.2 us)
Async XLA Ops:
  95.1 26.4 %collective-permute-start.1 = (bf16[512,512]{1,0:T(8,128)(2,1)S(1)}, bf16[512,512]{1,0:T(8,128)(2,1)}, u32[]{:S(2)}, u32[]{:S(2)}) collective-permute-start(bf16[512,512]{1,0:T(8,128)(2,1)S(1)} %copy.48), channel_id=1, source_target_pairs={{0,4},{4,8},{8,12},{12,16},{16,20},{20,24},{24,28},{28,32},{32,36}... | collective-permute-start | bytes 1572872 | tf_op jit(solution)/shard_map/cond/branch_1_fun/while/body/eval_jaxpr/ppermute | solution.py:541
  122.7 26.2 %collective-permute-start.1 = (bf16[512,512]{1,0:T(8,128)(2,1)S(1)}, bf16[512,512]{1,0:T(8,128)(2,1)}, u32[]{:S(2)}, u32[]{:S(2)}) collective-permute-start(bf16[512,512]{1,0:T(8,128)(2,1)S(1)} %copy.48), channel_id=1, source_target_pairs={{0,4},{4,8},{8,12},{12,16},{16,20},{20,24},{24,28},{28,32},{32,36}... | collective-permute-start | bytes 1572872 | tf_op jit(solution)/shard_map/cond/branch_1_fun/while/body/eval_jaxpr/ppermute | solution.py:541
  150.0 25.3 %collective-permute-start.1 = (bf16[512,512]{1,0:T(8,128)(2,1)S(1)}, bf16[512,512]{1,0:T(8,128)(2,1)}, u32[]{:S(2)}, u32[]{:S(2)}) collective-permute-start(bf16[512,512]{1,0:T(8,128)(2,1)S(1)} %copy.48), channel_id=1, source_target_pairs={{0,4},{4,8},{8,12},{12,16},{16,20},{20,24},{24,28},{28,32},{32,36}... | collective-permute-start | bytes 1572872 | tf_op jit(solution)/shard_map/cond/branch_1_fun/while/body/eval_jaxpr/ppermute | solution.py:541
  176.5 24.4 %collective-permute-start.1 = (bf16[512,512]{1,0:T(8,128)(2,1)S(1)}, bf16[512,512]{1,0:T(8,128)(2,1)}, u32[]{:S(2)}, u32[]{:S(2)}) collective-permute-start(bf16[512,512]{1,0:T(8,128)(2,1)S(1)} %copy.48), channel_id=1, source_target_pairs={{0,4},{4,8},{8,12},{12,16},{16,20},{20,24},{24,28},{28,32},{32,36}... | collective-permute-start | bytes 1572872 | tf_op jit(solution)/shard_map/cond/branch_1_fun/while/body/eval_jaxpr/ppermute | solution.py:541
  202.1 23.5 %collective-permute-start.1 = (bf16[512,512]{1,0:T(8,128)(2,1)S(1)}, bf16[512,512]{1,0:T(8,128)(2,1)}, u32[]{:S(2)}, u32[]{:S(2)}) collective-permute-start(bf16[512,512]{1,0:T(8,128)(2,1)S(1)} %copy.48), channel_id=1, source_target_pairs={{0,4},{4,8},{8,12},{12,16},{16,20},{20,24},{24,28},{28,32},{32,36}... | collective-permute-start | bytes 1572872 | tf_op jit(solution)/shard_map/cond/branch_1_fun/while/body/eval_jaxpr/ppermute | solution.py:541
  226.7 22.4 %collective-permute-start.1 = (bf16[512,512]{1,0:T(8,128)(2,1)S(1)}, bf16[512,512]{1,0:T(8,128)(2,1)}, u32[]{:S(2)}, u32[]{:S(2)}) collective-permute-start(bf16[512,512]{1,0:T(8,128)(2,1)S(1)} %copy.48), channel_id=1, source_target_pairs={{0,4},{4,8},{8,12},{12,16},{16,20},{20,24},{24,28},{28,32},{32,36}... | collective-permute-start | bytes 1572872 | tf_op jit(solution)/shard_map/cond/branch_1_fun/while/body/eval_jaxpr/ppermute | solution.py:541
  250.3 21.4 %collective-permute-start.1 = (bf16[512,512]{1,0:T(8,128)(2,1)S(1)}, bf16[512,512]{1,0:T(8,128)(2,1)}, u32[]{:S(2)}, u32[]{:S(2)}) collective-permute-start(bf16[512,512]{1,0:T(8,128)(2,1)S(1)} %copy.48), channel_id=1, source_target_pairs={{0,4},{4,8},{8,12},{12,16},{16,20},{20,24},{24,28},{28,32},{32,36}... | collective-permute-start | bytes 1572872 | tf_op jit(solution)/shard_map/cond/branch_1_fun/while/body/eval_jaxpr/ppermute | solution.py:541
  272.9 20.4 %collective-permute-start.1 = (bf16[512,512]{1,0:T(8,128)(2,1)S(1)}, bf16[512,512]{1,0:T(8,128)(2,1)}, u32[]{:S(2)}, u32[]{:S(2)}) collective-permute-start(bf16[512,512]{1,0:T(8,128)(2,1)S(1)} %copy.48), channel_id=1, source_target_pairs={{0,4},{4,8},{8,12},{12,16},{16,20},{20,24},{24,28},{28,32},{32,36}... | collective-permute-start | bytes 1572872 | tf_op jit(solution)/shard_map/cond/branch_1_fun/while/body/eval_jaxpr/ppermute | solution.py:541
  337.4 20.3 %collective-permute-start.1 = (bf16[512,512]{1,0:T(8,128)(2,1)S(1)}, bf16[512,512]{1,0:T(8,128)(2,1)}, u32[]{:S(2)}, u32[]{:S(2)}) collective-permute-start(bf16[512,512]{1,0:T(8,128)(2,1)S(1)} %copy.48), channel_id=1, source_target_pairs={{0,4},{4,8},{8,12},{12,16},{16,20},{20,24},{24,28},{28,32},{32,36}... | collective-permute-start | bytes 1572872 | tf_op jit(solution)/shard_map/cond/branch_1_fun/while/body/eval_jaxpr/ppermute | solution.py:541
  359.0 20.7 %collective-permute-start.1 = (bf16[512,512]{1,0:T(8,128)(2,1)S(1)}, bf16[512,512]{1,0:T(8,128)(2,1)}, u32[]{:S(2)}, u32[]{:S(2)}) collective-permute-start(bf16[512,512]{1,0:T(8,128)(2,1)S(1)} %copy.48), channel_id=1, source_target_pairs={{0,4},{4,8},{8,12},{12,16},{16,20},{20,24},{24,28},{28,32},{32,36}... | collective-permute-start | bytes 1572872 | tf_op jit(solution)/shard_map/cond/branch_1_fun/while/body/eval_jaxpr/ppermute | solution.py:541
  380.8 21.8 %collective-permute-start.1 = (bf16[512,512]{1,0:T(8,128)(2,1)S(1)}, bf16[512,512]{1,0:T(8,128)(2,1)}, u32[]{:S(2)}, u32[]{:S(2)}) collective-permute-start(bf16[512,512]{1,0:T(8,128)(2,1)S(1)} %copy.48), channel_id=1, source_target_pairs={{0,4},{4,8},{8,12},{12,16},{16,20},{20,24},{24,28},{28,32},{32,36}... | collective-permute-start | bytes 1572872 | tf_op jit(solution)/shard_map/cond/branch_1_fun/while/body/eval_jaxpr/ppermute | solution.py:541
  403.8 22.9 %collective-permute-start.1 = (bf16[512,512]{1,0:T(8,128)(2,1)S(1)}, bf16[512,512]{1,0:T(8,128)(2,1)}, u32[]{:S(2)}, u32[]{:S(2)}) collective-permute-start(bf16[512,512]{1,0:T(8,128)(2,1)S(1)} %copy.48), channel_id=1, source_target_pairs={{0,4},{4,8},{8,12},{12,16},{16,20},{20,24},{24,28},{28,32},{32,36}... | collective-permute-start | bytes 1572872 | tf_op jit(solution)/shard_map/cond/branch_1_fun/while/body/eval_jaxpr/ppermute | solution.py:541
  427.9 24.0 %collective-permute-start.1 = (bf16[512,512]{1,0:T(8,128)(2,1)S(1)}, bf16[512,512]{1,0:T(8,128)(2,1)}, u32[]{:S(2)}, u32[]{:S(2)}) collective-permute-start(bf16[512,512]{1,0:T(8,128)(2,1)S(1)} %copy.48), channel_id=1, source_target_pairs={{0,4},{4,8},{8,12},{12,16},{16,20},{20,24},{24,28},{28,32},{32,36}... | collective-permute-start | bytes 1572872 | tf_op jit(solution)/shard_map/cond/branch_1_fun/while/body/eval_jaxpr/ppermute | solution.py:541
  453.0 25.0 %collective-permute-start.1 = (bf16[512,512]{1,0:T(8,128)(2,1)S(1)}, bf16[512,512]{1,0:T(8,128)(2,1)}, u32[]{:S(2)}, u32[]{:S(2)}) collective-permute-start(bf16[512,512]{1,0:T(8,128)(2,1)S(1)} %copy.48), channel_id=1, source_target_pairs={{0,4},{4,8},{8,12},{12,16},{16,20},{20,24},{24,28},{28,32},{32,36}... | collective-permute-start | bytes 1572872 | tf_op jit(solution)/shard_map/cond/branch_1_fun/while/body/eval_jaxpr/ppermute | solution.py:541
  479.2 26.1 %collective-permute-start.1 = (bf16[512,512]{1,0:T(8,128)(2,1)S(1)}, bf16[512,512]{1,0:T(8,128)(2,1)}, u32[]{:S(2)}, u32[]{:S(2)}) collective-permute-start(bf16[512,512]{1,0:T(8,128)(2,1)S(1)} %copy.48), channel_id=1, source_target_pairs={{0,4},{4,8},{8,12},{12,16},{16,20},{20,24},{24,28},{28,32},{32,36}... | collective-permute-start | bytes 1572872 | tf_op jit(solution)/shard_map/cond/branch_1_fun/while/body/eval_jaxpr/ppermute | solution.py:541
  506.5 27.2 %collective-permute-start.1 = (bf16[512,512]{1,0:T(8,128)(2,1)S(1)}, bf16[512,512]{1,0:T(8,128)(2,1)}, u32[]{:S(2)}, u32[]{:S(2)}) collective-permute-start(bf16[512,512]{1,0:T(8,128)(2,1)S(1)} %copy.48), channel_id=1, source_target_pairs={{0,4},{4,8},{8,12},{12,16},{16,20},{20,24},{24,28},{28,32},{32,36}... | collective-permute-start | bytes 1572872 | tf_op jit(solution)/shard_map/cond/branch_1_fun/while/body/eval_jaxpr/ppermute | solution.py:541
  534.9 28.2 %collective-permute-start.1 = (bf16[512,512]{1,0:T(8,128)(2,1)S(1)}, bf16[512,512]{1,0:T(8,128)(2,1)}, u32[]{:S(2)}, u32[]{:S(2)}) collective-permute-start(bf16[512,512]{1,0:T(8,128)(2,1)S(1)} %copy.48), channel_id=1, source_target_pairs={{0,4},{4,8},{8,12},{12,16},{16,20},{20,24},{24,28},{28,32},{32,36}... | collective-permute-start | bytes 1572872 | tf_op jit(solution)/shard_map/cond/branch_1_fun/while/body/eval_jaxpr/ppermute | solution.py:541
  564.3 27.4 %collective-permute-start.1 = (bf16[512,512]{1,0:T(8,128)(2,1)S(1)}, bf16[512,512]{1,0:T(8,128)(2,1)}, u32[]{:S(2)}, u32[]{:S(2)}) collective-permute-start(bf16[512,512]{1,0:T(8,128)(2,1)S(1)} %copy.48), channel_id=1, source_target_pairs={{0,4},{4,8},{8,12},{12,16},{16,20},{20,24},{24,28},{28,32},{32,36}... | collective-permute-start | bytes 1572872 | tf_op jit(solution)/shard_map/cond/branch_1_fun/while/body/eval_jaxpr/ppermute | solution.py:541
  592.8 26.4 %collective-permute-start.1 = (bf16[512,512]{1,0:T(8,128)(2,1)S(1)}, bf16[512,512]{1,0:T(8,128)(2,1)}, u32[]{:S(2)}, u32[]{:S(2)}) collective-permute-start(bf16[512,512]{1,0:T(8,128)(2,1)S(1)} %copy.48), channel_id=1, source_target_pairs={{0,4},{4,8},{8,12},{12,16},{16,20},{20,24},{24,28},{28,32},{32,36}... | collective-permute-start | bytes 1572872 | tf_op jit(solution)/shard_map/cond/branch_1_fun/while/body/eval_jaxpr/ppermute | solution.py:541
  620.4 25.5 %collective-permute-start.1 = (bf16[512,512]{1,0:T(8,128)(2,1)S(1)}, bf16[512,512]{1,0:T(8,128)(2,1)}, u32[]{:S(2)}, u32[]{:S(2)}) collective-permute-start(bf16[512,512]{1,0:T(8,128)(2,1)S(1)} %copy.48), channel_id=1, source_target_pairs={{0,4},{4,8},{8,12},{12,16},{16,20},{20,24},{24,28},{28,32},{32,36}... | collective-permute-start | bytes 1572872 | tf_op jit(solution)/shard_map/cond/branch_1_fun/while/body/eval_jaxpr/ppermute | solution.py:541
  647.1 24.6 %collective-permute-start.1 = (bf16[512,512]{1,0:T(8,128)(2,1)S(1)}, bf16[512,512]{1,0:T(8,128)(2,1)}, u32[]{:S(2)}, u32[]{:S(2)}) collective-permute-start(bf16[512,512]{1,0:T(8,128)(2,1)S(1)} %copy.48), channel_id=1, source_target_pairs={{0,4},{4,8},{8,12},{12,16},{16,20},{20,24},{24,28},{28,32},{32,36}... | collective-permute-start | bytes 1572872 | tf_op jit(solution)/shard_map/cond/branch_1_fun/while/body/eval_jaxpr/ppermute | solution.py:541
  672.9 23.7 %collective-permute-start.1 = (bf16[512,512]{1,0:T(8,128)(2,1)S(1)}, bf16[512,512]{1,0:T(8,128)(2,1)}, u32[]{:S(2)}, u32[]{:S(2)}) collective-permute-start(bf16[512,512]{1,0:T(8,128)(2,1)S(1)} %copy.48), channel_id=1, source_target_pairs={{0,4},{4,8},{8,12},{12,16},{16,20},{20,24},{24,28},{28,32},{32,36}... | collective-permute-start | bytes 1572872 | tf_op jit(solution)/shard_map/cond/branch_1_fun/while/body/eval_jaxpr/ppermute | solution.py:541
  697.7 22.7 %collective-permute-start.1 = (bf16[512,512]{1,0:T(8,128)(2,1)S(1)}, bf16[512,512]{1,0:T(8,128)(2,1)}, u32[]{:S(2)}, u32[]{:S(2)}) collective-permute-start(bf16[512,512]{1,0:T(8,128)(2,1)S(1)} %copy.48), channel_id=1, source_target_pairs={{0,4},{4,8},{8,12},{12,16},{16,20},{20,24},{24,28},{28,32},{32,36}... | collective-permute-start | bytes 1572872 | tf_op jit(solution)/shard_map/cond/branch_1_fun/while/body/eval_jaxpr/ppermute | solution.py:541
  721.6 21.6 %collective-permute-start.1 = (bf16[512,512]{1,0:T(8,128)(2,1)S(1)}, bf16[512,512]{1,0:T(8,128)(2,1)}, u32[]{:S(2)}, u32[]{:S(2)}) collective-permute-start(bf16[512,512]{1,0:T(8,128)(2,1)S(1)} %copy.48), channel_id=1, source_target_pairs={{0,4},{4,8},{8,12},{12,16},{16,20},{20,24},{24,28},{28,32},{32,36}... | collective-permute-start | bytes 1572872 | tf_op jit(solution)/shard_map/cond/branch_1_fun/while/body/eval_jaxpr/ppermute | solution.py:541
  744.3 20.6 %collective-permute-start.1 = (bf16[512,512]{1,0:T(8,128)(2,1)S(1)}, bf16[512,512]{1,0:T(8,128)(2,1)}, u32[]{:S(2)}, u32[]{:S(2)}) collective-permute-start(bf16[512,512]{1,0:T(8,128)(2,1)S(1)} %copy.48), channel_id=1, source_target_pairs={{0,4},{4,8},{8,12},{12,16},{16,20},{20,24},{24,28},{28,32},{32,36}... | collective-permute-start | bytes 1572872 | tf_op jit(solution)/shard_map/cond/branch_1_fun/while/body/eval_jaxpr/ppermute | solution.py:541
  766.1 20.3 %collective-permute-start.1 = (bf16[512,512]{1,0:T(8,128)(2,1)S(1)}, bf16[512,512]{1,0:T(8,128)(2,1)}, u32[]{:S(2)}, u32[]{:S(2)}) collective-permute-start(bf16[512,512]{1,0:T(8,128)(2,1)S(1)} %copy.48), channel_id=1, source_target_pairs={{0,4},{4,8},{8,12},{12,16},{16,20},{20,24},{24,28},{28,32},{32,36}... | collective-permute-start | bytes 1572872 | tf_op jit(solution)/shard_map/cond/branch_1_fun/while/body/eval_jaxpr/ppermute | solution.py:541
  809.1 20.3 %collective-permute-start.1 = (bf16[512,512]{1,0:T(8,128)(2,1)S(1)}, bf16[512,512]{1,0:T(8,128)(2,1)}, u32[]{:S(2)}, u32[]{:S(2)}) collective-permute-start(bf16[512,512]{1,0:T(8,128)(2,1)S(1)} %copy.48), channel_id=1, source_target_pairs={{0,4},{4,8},{8,12},{12,16},{16,20},{20,24},{24,28},{28,32},{32,36}... | collective-permute-start | bytes 1572872 | tf_op jit(solution)/shard_map/cond/branch_1_fun/while/body/eval_jaxpr/ppermute | solution.py:541
  830.6 20.5 %collective-permute-start.1 = (bf16[512,512]{1,0:T(8,128)(2,1)S(1)}, bf16[512,512]{1,0:T(8,128)(2,1)}, u32[]{:S(2)}, u32[]{:S(2)}) collective-permute-start(bf16[512,512]{1,0:T(8,128)(2,1)S(1)} %copy.48), channel_id=1, source_target_pairs={{0,4},{4,8},{8,12},{12,16},{16,20},{20,24},{24,28},{28,32},{32,36}... | collective-permute-start | bytes 1572872 | tf_op jit(solution)/shard_map/cond/branch_1_fun/while/body/eval_jaxpr/ppermute | solution.py:541
  852.3 21.6 %collective-permute-start.1 = (bf16[512,512]{1,0:T(8,128)(2,1)S(1)}, bf16[512,512]{1,0:T(8,128)(2,1)}, u32[]{:S(2)}, u32[]{:S(2)}) collective-permute-start(bf16[512,512]{1,0:T(8,128)(2,1)S(1)} %copy.48), channel_id=1, source_target_pairs={{0,4},{4,8},{8,12},{12,16},{16,20},{20,24},{24,28},{28,32},{32,36}... | collective-permute-start | bytes 1572872 | tf_op jit(solution)/shard_map/cond/branch_1_fun/while/body/eval_jaxpr/ppermute | solution.py:541
  883.5 79.1 %collective-permute-start.2 = (f32[128,4096]{1,0:T(8,128)}, f32[128,4096]{1,0:T(8,128)}, u32[]{:S(2)}, u32[]{:S(2)}) collective-permute-start(f32[128,4096]{1,0:T(8,128)} %get-tuple-element.122), channel_id=1, source_target_pairs={{0,1},{1,2},{2,3},{3,0},{4,5},{5,6},{6,7},{7,4},{8,9},{9,10},{10,1... | collective-permute-start | bytes 6291464 | tf_op jit(solution)/shard_map/cond/branch_1_fun/ppermute | solution.py:553
  918.2 49.8 %collective-permute-start.4 = (f32[128,4096]{1,0:T(8,128)}, f32[128,4096]{1,0:T(8,128)}, u32[]{:S(2)}, u32[]{:S(2)}) collective-permute-start(f32[128,4096]{1,0:T(8,128)} %get-tuple-element.123), channel_id=1, source_target_pairs={{0,3},{1,0},{2,1},{3,2},{4,7},{5,4},{6,5},{7,6},{8,11},{9,8},{10,9... | collective-permute-start | bytes 6291464 | tf_op jit(solution)/shard_map/cond/branch_1_fun/ppermute | solution.py:553
  918.2 89.3 %collective-permute-start.3 = (f32[128,4096]{1,0:T(8,128)S(1)}, f32[128,4096]{1,0:T(8,128)}, u32[]{:S(2)}, u32[]{:S(2)}) collective-permute-start(f32[128,4096]{1,0:T(8,128)S(1)} %get-tuple-element.124), channel_id=1, source_target_pairs={{0,2},{1,3},{2,0},{3,1},{4,6},{5,7},{6,4},{7,5},{8,10},{9,11},{10,... | collective-permute-start | bytes 6291464 | tf_op jit(solution)/shard_map/cond/branch_1_fun/ppermute | solution.py:553
  (41 other events, 726.6 us)
